TPU v7x, 32 devices: a whole 2x2x4 slice. The times are simulated.
32 devices in a mesh: seq: 8 (over z, y), row: 4 (over x, core).
Axes of the slice: x: 2, y: 2, z: 4, core: 2. Of those that a mesh axis runs over, the one named last changes fastest.
Arguments:
- tokens: bfloat16 [4, 1152, 1024], P('row', 'seq'), may hold values from -6 to 6
- attn_in: bfloat16 [2, 1024, 3072], P(None, ('seq', 'row')), may hold values from -0.1875 to 0.1875
- attn_out: bfloat16 [2, 1024, 1024], P(None, ('seq', 'row')), may hold values from -0.75 to 0.75
- ffn_up: bfloat16 [2, 1024, 4096], P(None, ('seq', 'row')), may hold values from -0.1875 to 0.1875
- ffn_down: bfloat16 [2, 4096, 1024], P(None, ('seq', 'row')), may hold values from -0.09375 to 0.09375
- norm_gains: bfloat16 [2, 2048], P(None, ('seq', 'row')), may hold values from 0.5 to 1.5
- biases: bfloat16 [2, 11264], P(None, ('seq', 'row')), may hold values from -1 to 1
- colbert: bfloat16 [1024, 128], P(('seq', 'row')), may hold values from -0.1875 to 0.1875
- log_scale: float32 [1], replicated, may hold values from 1.1 to 2.1
- cotangent: bfloat16 [4, 1152, 1024], P('row', 'seq'), may hold values from -6 to 6
- seg_lengths: int32 [4, 8], P('row'), may hold values from 1 to 1008, as said below
- seg_kinds: int32 [4, 8], P('row'), may hold values from 0 to 1, as said below
- pairing: int32 [4, 4], P('row'), may hold values from 0 to 3
Outputs:
- hidden_out: bfloat16 [4, 1152, 1024], P('row', 'seq')
- loss: float32 [1], replicated
- tokens_grad: float32 [4, 1152, 1024], P('row', 'seq')
- attn_in_grad: float32 [2, 1024, 3072], P(None, ('seq', 'row'))
- attn_out_grad: float32 [2, 1024, 1024], P(None, ('seq', 'row'))
- ffn_up_grad: float32 [2, 1024, 4096], P(None, ('seq', 'row'))
- ffn_down_grad: float32 [2, 4096, 1024], P(None, ('seq', 'row'))
- norm_gains_grad: float32 [2, 2048], P(None, ('seq', 'row'))
- biases_grad: float32 [2, 11264], P(None, ('seq', 'row'))
- colbert_grad: float32 [1024, 128], P(('seq', 'row'))
- log_scale_grad: float32 [1], replicated
Inputs may be any that keep to these rules, and one draw needn't show every extreme that they name: `seg_lengths`: each row's lengths sum to 1152; every query segment has exactly 32 tokens; each row has one document of 1008 tokens that begins among the first 144 positions. `seg_kinds`: each row has exactly 4 query segments and 4 documents.
All inputs are finite; a program needn't handle non-finite values.
Results may differ from a plain program's by a relative error of at most 0.033.
Values may be sent and summed in bfloat16 or wider, within the bound.
No kernel may reach another device: no remote copies, remote signals or barrier semaphores. Data moves between devices by JAX's collectives and lax.ppermute only.
A program may use at most 320 MiB of HBM per device.

v0:
```python
import math

import jax
import jax.numpy as jnp
from jax import lax
from jax.sharding import PartitionSpec as P

HEADS = 16
QLEN = 32
NQ = 4
NSD = 3


NEG_FILL = -1e30
SHARPNESS = 16.0
HIGHEST = lax.Precision.HIGHEST


def joined_2(value, axis, join):
    pieces = jax.tree.map(lambda part: lax.all_gather(part, axis), value)
    head = jax.tree.map(lambda part: part[0], pieces)
    tail = jax.tree.map(lambda part: part[1:], pieces)
    so_far, _ = lax.scan(lambda so_far, section: (join(so_far, section), None), head, tail)
    return so_far


def token_info(positions, lengths, kinds):
    ends = jnp.cumsum(lengths)
    starts = ends - lengths
    query_count = jnp.cumsum(kinds) - kinds
    doc_count = jnp.cumsum(1 - kinds) - (1 - kinds)
    segment = jnp.sum((positions[:, None] >= ends[None, :]).astype(jnp.int32), axis=1)
    onehot = segment[:, None] == jnp.arange(lengths.shape[0], dtype=jnp.int32)[None, :]
    nothing = jnp.zeros((), jnp.int32)
    seg_start = jnp.sum(jnp.where(onehot, starts[None, :], nothing), axis=1)
    is_query = jnp.sum(jnp.where(onehot, kinds[None, :], nothing), axis=1)
    query_num = jnp.sum(jnp.where(onehot, query_count[None, :], nothing), axis=1)
    doc_num = jnp.sum(jnp.where(onehot, doc_count[None, :], nothing), axis=1)
    offset = positions - seg_start
    return (segment, offset, is_query, query_num * QLEN + offset, doc_num)


def rope_tables(offset, head_dim):
    half = head_dim // 2
    inverse = jnp.exp(jnp.arange(half, dtype=jnp.float32) * (-2.0 * math.log(10000.0) / head_dim))
    angle = offset.astype(jnp.float32)[:, None] * inverse[None, :]
    return (jnp.cos(angle), jnp.sin(angle))


def rotate(flat, cos_table, sin_table):
    length = flat.shape[0]
    head_dim = flat.shape[1] // HEADS
    half = head_dim // 2
    shaped = flat.reshape(length, HEADS, head_dim)
    first_half = shaped[..., :half]
    second_half = shaped[..., half:]
    cos_three = cos_table[:, None, :]
    sin_three = sin_table[:, None, :]
    turned = jnp.concatenate(
        [
            first_half * cos_three - second_half * sin_three,
            second_half * cos_three + first_half * sin_three,
        ],
        axis=-1,
    )
    return turned.reshape(length, flat.shape[1])


def layer_norm(rows, gain, shift):
    center = rows - jnp.mean(rows, axis=-1, keepdims=True)
    variance = jnp.mean(center * center, axis=-1, keepdims=True)
    return center * lax.rsqrt(variance + 1e-05) * gain + shift


def unit_rows(rows):
    return rows * lax.rsqrt(jnp.sum(rows * rows, axis=-1, keepdims=True) + 1e-06)


def exact_gelu(values):
    return jax.nn.gelu(values, approximate=False)


def block_for(count):
    blocks = count
    while blocks > 1024 and blocks % 2 == 0:
        blocks = blocks // 2
    return blocks


def merge_pair(first, second):
    max_first, sum_first = first
    max_second, sum_second = second
    top = jnp.maximum(max_first, max_second)
    return (top, sum_first * jnp.exp(max_first - top) + sum_second * jnp.exp(max_second - top))


def matmul_left_t(left, right):
    return jnp.einsum("ti,to->io", left, right, preferred_element_type=jnp.float32)


def matmul_right_t(left, right):
    return jnp.einsum("to,io->ti", left, right, preferred_element_type=jnp.float32)


def body(
    tokens,
    attn_in,
    attn_out,
    ffn_up,
    ffn_down,
    norm_gains,
    biases,
    colbert,
    log_scale,
    cotangent,
    seg_lengths,
    seg_kinds,
    pairing,
):
    rank = lax.axis_index("seq")
    local_len = tokens.shape[1]
    model_width = tokens.shape[2]
    head_dim = model_width // HEADS
    scale = head_dim ** (-0.5)
    lengths = seg_lengths[0]
    kinds = seg_kinds[0]
    positions = rank * local_len + jnp.arange(local_len, dtype=jnp.int32)
    segment, offset, is_query, query_slot, doc_num = token_info(positions, lengths, kinds)
    cos_table, sin_table = rope_tables(offset, head_dim)
    layer_count = attn_in.shape[0]

    def split_pieces(key_piece, value_piece):
        count = key_piece.shape[0]
        blocks = block_for(count)
        key_seg = token_info(jnp.arange(count, dtype=jnp.int32), lengths, kinds)[0]
        key_blocks = key_piece.reshape(count // blocks, blocks, HEADS, head_dim)
        value_blocks = value_piece.reshape(count // blocks, blocks, HEADS, head_dim)
        seg_blocks = key_seg.reshape(count // blocks, blocks)
        return (count, blocks, key_blocks, value_blocks, seg_blocks)

    def attend_back(queries, keys, values, context, log_total, grad_context):
        query_three = queries.reshape(local_len, HEADS, head_dim)
        grad_three = grad_context.reshape(local_len, HEADS, head_dim)
        delta = jnp.sum(
            grad_three.astype(jnp.float32) * context.reshape(local_len, HEADS, head_dim), axis=-1
        ).T

        def score_grads(
            query_blk, grad_blk, key_blk, value_blk, query_seg, key_seg, total_blk, delta_blk
        ):
            scores = (
                jnp.einsum("qhd,khd->hqk", query_blk, key_blk, preferred_element_type=jnp.float32)
                * scale
            )
            allowed = (query_seg[:, None] == key_seg[None, :])[None]
            probs = jnp.where(allowed, jnp.exp(scores - total_blk[..., None]), 0.0)
            grad_probs = jnp.einsum(
                "qhd,khd->hqk", grad_blk, value_blk, preferred_element_type=jnp.float32
            )
            grad_scores = (probs * (grad_probs - delta_blk[..., None])).astype(jnp.bfloat16)
            return (probs, grad_scores)

        grad_query = jnp.zeros((local_len, HEADS, head_dim), jnp.float32)
        count, blocks, key_blocks, value_blocks, seg_blocks = split_pieces(
            lax.all_gather(keys, "seq", axis=0, tiled=True),
            lax.all_gather(values, "seq", axis=0, tiled=True),
        )

        def advance(grad_acc, item):
            key_blk, value_blk, seg_blk = item
            probs, grad_scores = score_grads(
                query_three, grad_three, key_blk, value_blk, segment, seg_blk, log_total, delta
            )
            grad_acc = grad_acc + scale * jnp.einsum(
                "hqk,khd->qhd", grad_scores, key_blk, preferred_element_type=jnp.float32
            )
            grad_key = scale * jnp.einsum(
                "hqk,qhd->khd", grad_scores, query_three, preferred_element_type=jnp.float32
            )
            grad_value = jnp.einsum(
                "hqk,qhd->khd",
                probs.astype(jnp.bfloat16),
                grad_three,
                preferred_element_type=jnp.float32,
            )
            joined = jnp.concatenate(
                [grad_key.reshape(blocks, model_width), grad_value.reshape(blocks, model_width)],
                axis=1,
            )
            return (grad_acc, joined)

        grad_query, pieces_out = lax.scan(
            advance, grad_query, (key_blocks, value_blocks, seg_blocks)
        )
        grad_rows = pieces_out.reshape(count, 2 * model_width)
        grad_query, grad_rows = (grad_query, grad_rows)
        summed = lax.psum_scatter(
            grad_rows.astype(jnp.bfloat16), "seq", scatter_dimension=0, tiled=True
        ).astype(jnp.float32)
        grad_key_out = summed[:, :model_width]
        grad_value_out = summed[:, model_width:]
        return (grad_query.reshape(local_len, model_width), grad_key_out, grad_value_out)

    def unpack(full):
        w_in, w_out, w_up, w_down, gains, bias = full[:6]
        hidden_units = w_up.shape[1]
        gains_f = gains.astype(jnp.float32)
        bias_f = bias.astype(jnp.float32)
        width_three = 3 * model_width
        return (
            w_in,
            w_out,
            w_up,
            w_down,
            hidden_units,
            gains_f[:model_width],
            gains_f[model_width:],
            bias_f[:width_three],
            bias_f[width_three : 4 * model_width],
            bias_f[4 * model_width : 4 * model_width + hidden_units],
            bias_f[4 * model_width + hidden_units : 5 * model_width + hidden_units],
            bias_f[5 * model_width + hidden_units : 6 * model_width + hidden_units],
            bias_f[6 * model_width + hidden_units :],
        )

    def layer_backward(grad_out, full, record):
        (
            w_in,
            w_out,
            w_up,
            w_down,
            hidden_units,
            gain_one,
            gain_two,
            bias_in,
            bias_out,
            bias_up,
            bias_down,
            shift_one,
            shift_two,
        ) = unpack(full)
        (
            inputs_low,
            queries,
            keys,
            values,
            context,
            context_low,
            log_total,
            first,
            normed,
            normed_low,
            pre_act,
            act_low,
            second,
        ) = record
        unused, pull_two = jax.vjp(layer_norm, second, gain_two, shift_two)
        grad_second, grad_gain_two, grad_shift_two = pull_two(grad_out)
        grad_branch_two = grad_second.astype(jnp.bfloat16)
        grad_bias_down = jnp.sum(grad_branch_two.astype(jnp.float32), axis=0)
        grad_w_down = matmul_left_t(act_low, grad_branch_two)
        grad_act = matmul_right_t(grad_branch_two, w_down)
        unused, pull_gelu = jax.vjp(exact_gelu, pre_act)
        grad_pre = pull_gelu(grad_act)[0].astype(jnp.bfloat16)
        grad_bias_up = jnp.sum(grad_pre.astype(jnp.float32), axis=0)
        grad_w_up = matmul_left_t(normed_low, grad_pre)
        grad_normed = grad_second + matmul_right_t(grad_pre, w_up)
        unused, pull_one = jax.vjp(layer_norm, first, gain_one, shift_one)
        grad_first, grad_gain_one, grad_shift_one = pull_one(grad_normed)
        grad_branch = grad_first.astype(jnp.bfloat16)
        grad_bias_out = jnp.sum(grad_branch.astype(jnp.float32), axis=0)
        grad_w_out = matmul_left_t(context_low, grad_branch)
        grad_context = matmul_right_t(grad_branch, w_out).astype(jnp.bfloat16)
        grad_query, grad_key, grad_value = attend_back(
            queries, keys, values, context, log_total, grad_context
        )
        grad_mixed = jnp.concatenate(
            [
                rotate(grad_query, cos_table, -sin_table),
                rotate(grad_key, cos_table, -sin_table),
                grad_value,
            ],
            axis=1,
        ).astype(jnp.bfloat16)
        grad_bias_in = jnp.sum(grad_mixed.astype(jnp.float32), axis=0)
        grad_w_in = matmul_left_t(inputs_low, grad_mixed)
        grad_hidden = grad_first + matmul_right_t(grad_mixed, w_in)
        grad_gains = jnp.concatenate([grad_gain_one, grad_gain_two])
        grad_bias = jnp.concatenate(
            [
                grad_bias_in,
                grad_bias_out,
                grad_bias_up,
                grad_bias_down,
                grad_shift_one,
                grad_shift_two,
            ]
        )
        return (grad_hidden, (grad_w_in, grad_w_out, grad_w_up, grad_w_down, grad_gains, grad_bias))

    hidden = tokens[0].astype(jnp.float32)
    records = []
    gathered = []
    for layer_index in range(layer_count):
        full = (
            lax.all_gather(attn_in[layer_index], ("seq", "row"), axis=0, tiled=True),
            lax.all_gather(attn_out[layer_index], ("seq", "row"), axis=0, tiled=True),
            lax.all_gather(ffn_up[layer_index], ("seq", "row"), axis=0, tiled=True),
            lax.all_gather(ffn_down[layer_index], ("seq", "row"), axis=0, tiled=True),
            lax.all_gather(norm_gains[layer_index], ("seq", "row"), axis=0, tiled=True),
            lax.all_gather(biases[layer_index], ("seq", "row"), axis=0, tiled=True),
            lax.all_gather(colbert, ("seq", "row"), axis=0, tiled=True),
        )
        gathered.append(full)
        (
            layer_w_in,
            layer_w_out,
            layer_w_up,
            layer_w_down,
            layer_hidden_units,
            layer_gain_one,
            layer_gain_two,
            layer_bias_in,
            layer_bias_out,
            layer_bias_up,
            layer_bias_down,
            layer_shift_one,
            layer_shift_two,
        ) = unpack(full)
        layer_inputs_low = hidden.astype(jnp.bfloat16)
        mixed = (
            jnp.dot(layer_inputs_low, layer_w_in, preferred_element_type=jnp.float32)
            + layer_bias_in
        )
        layer_queries = rotate(mixed[:, :model_width], cos_table, sin_table).astype(jnp.bfloat16)
        layer_keys = rotate(mixed[:, model_width : 2 * model_width], cos_table, sin_table).astype(
            jnp.bfloat16
        )
        layer_values = mixed[:, 2 * model_width :].astype(jnp.bfloat16)
        attend_query_three = layer_queries.reshape(local_len, HEADS, head_dim)
        attend_initial = (
            jnp.full((HEADS, local_len), NEG_FILL, jnp.float32),
            jnp.zeros((HEADS, local_len), jnp.float32),
            jnp.zeros((local_len, HEADS, head_dim), jnp.float32),
        )
        absorb_carry = attend_initial
        absorb_count, absorb_blocks, absorb_key_blocks, absorb_value_blocks, absorb_seg_blocks = (
            split_pieces(
                lax.all_gather(layer_keys, "seq", axis=0, tiled=True),
                lax.all_gather(layer_values, "seq", axis=0, tiled=True),
            )
        )

        def absorb_advance(state, item):
            run_max, run_sum, accum = state
            key_blk, value_blk, seg_blk = item
            scores = (
                jnp.einsum(
                    "qhd,khd->hqk", attend_query_three, key_blk, preferred_element_type=jnp.float32
                )
                * scale
            )
            allowed = (segment[:, None] == seg_blk[None, :])[None]
            scores = jnp.where(allowed, scores, NEG_FILL)
            new_max = jnp.maximum(run_max, jnp.max(scores, axis=-1))
            weights = jnp.where(allowed, jnp.exp(scores - new_max[..., None]), 0.0)
            factor = jnp.exp(run_max - new_max)
            run_sum = run_sum * factor + jnp.sum(weights, axis=-1)
            accum = accum * factor.T[:, :, None] + jnp.einsum(
                "hqk,khd->qhd",
                weights.astype(jnp.bfloat16),
                value_blk,
                preferred_element_type=jnp.float32,
            )
            return ((new_max, run_sum, accum), None)

        absorb_carry, absorb_unused = lax.scan(
            absorb_advance,
            absorb_carry,
            (absorb_key_blocks, absorb_value_blocks, absorb_seg_blocks),
        )
        run_max, run_sum, accum = absorb_carry
        attend_context = (accum / run_sum.T[:, :, None]).reshape(local_len, model_width)
        attend_log_total = run_max + jnp.log(run_sum)
        layer_context_low = attend_context.astype(jnp.bfloat16)
        layer_first = (
            hidden
            + jnp.dot(layer_context_low, layer_w_out, preferred_element_type=jnp.float32)
            + layer_bias_out
        )
        layer_normed = layer_norm(layer_first, layer_gain_one, layer_shift_one)
        layer_normed_low = layer_normed.astype(jnp.bfloat16)
        layer_pre_act = (
            jnp.dot(layer_normed_low, layer_w_up, preferred_element_type=jnp.float32)
            + layer_bias_up
        )
        layer_act_low = exact_gelu(layer_pre_act).astype(jnp.bfloat16)
        layer_second = (
            layer_normed
            + jnp.dot(layer_act_low, layer_w_down, preferred_element_type=jnp.float32)
            + layer_bias_down
        )
        output = layer_norm(layer_second, layer_gain_two, layer_shift_two)
        layer_record = (
            layer_inputs_low,
            layer_queries,
            layer_keys,
            layer_values,
            attend_context,
            layer_context_low,
            attend_log_total,
            layer_first,
            layer_normed,
            layer_normed_low,
            layer_pre_act,
            layer_act_low,
            layer_second,
        )
        hidden = output
        record = layer_record
        records.append(record)
    w_col = gathered[layer_count - 1][6]
    final_low = hidden.astype(jnp.bfloat16)
    col = jnp.dot(final_low, w_col, preferred_element_type=jnp.float32)
    full_width = w_col.shape[1]
    part_widths = (full_width, full_width * 3 // 4, full_width // 2)
    query_total = NQ * QLEN
    doc_total = NSD + 1
    selector = (is_query == 1)[None, :] & (
        query_slot[None, :] == jnp.arange(query_total, dtype=jnp.int32)[:, None]
    )
    selector_low = selector.astype(jnp.bfloat16)
    embeds = [unit_rows(col[:, :part_width]).astype(jnp.bfloat16) for part_width in part_widths]
    picked = (
        lax.psum(
            jnp.dot(selector_low, embeds[0], preferred_element_type=jnp.float32).astype(
                jnp.bfloat16
            ),
            "seq",
        ).astype(jnp.float32),
        lax.psum(
            jnp.dot(selector_low, embeds[1], preferred_element_type=jnp.float32).astype(
                jnp.bfloat16
            ),
            "seq",
        ).astype(jnp.float32),
        lax.psum(
            jnp.dot(selector_low, embeds[2], preferred_element_type=jnp.float32).astype(
                jnp.bfloat16
            ),
            "seq",
        ).astype(jnp.float32),
    )
    query_emb = [item.astype(jnp.bfloat16) for item in picked]
    sims = jnp.stack(
        [
            jnp.einsum(
                "qc,tc->qt", query_emb[part], embeds[part], preferred_element_type=jnp.float32
            )
            for part in range(3)
        ]
    )
    doc_mask = (
        (is_query == 0)[:, None]
        & (doc_num[:, None] == jnp.arange(doc_total, dtype=jnp.int32)[None, :])
    )[None, None]
    scaled = jnp.where(doc_mask, SHARPNESS * sims[..., None], NEG_FILL)
    part_max = jnp.max(scaled, axis=2)
    part_sum = jnp.sum(jnp.where(doc_mask, jnp.exp(scaled - part_max[:, :, None, :]), 0.0), axis=2)
    top, total = joined_2((part_max, part_sum), "seq", merge_pair)
    soft = (top + jnp.log(total)) / SHARPNESS
    pair_sum = jnp.sum(soft.reshape(3, NQ, QLEN, doc_total), axis=2)
    inverse_temp = jnp.exp(log_scale[0])
    logits = pair_sum * inverse_temp / QLEN
    positive = pairing[0][None, :, None] == jnp.arange(doc_total, dtype=jnp.int32)[None, None, :]
    losses = jax.nn.logsumexp(logits, axis=-1) - jnp.sum(jnp.where(positive, logits, 0.0), axis=-1)
    loss_weight = 1.0 / (3 * NQ * lax.axis_size("row"))
    grad_logits = loss_weight * (jax.nn.softmax(logits, axis=-1) - positive.astype(jnp.float32))
    loss_total, temp_grad = lax.psum(
        (jnp.sum(losses).reshape(1) * loss_weight, jnp.sum(grad_logits * logits).reshape(1)), "row"
    )
    grad_pairs = grad_logits * inverse_temp / QLEN
    grad_soft = jnp.broadcast_to(grad_pairs[:, :, None, :], (3, NQ, QLEN, doc_total)).reshape(
        3, query_total, doc_total
    )
    shares = jnp.where(doc_mask, jnp.exp(scaled - top[:, :, None, :]), 0.0) / total[:, :, None, :]
    grad_sims = jnp.sum(shares * grad_soft[:, :, None, :], axis=-1).astype(jnp.bfloat16)
    grad_query_emb = (
        lax.psum(
            jnp.dot(grad_sims[0], embeds[0], preferred_element_type=jnp.float32).astype(
                jnp.bfloat16
            ),
            "seq",
        ).astype(jnp.float32),
        lax.psum(
            jnp.dot(grad_sims[1], embeds[1], preferred_element_type=jnp.float32).astype(
                jnp.bfloat16
            ),
            "seq",
        ).astype(jnp.float32),
        lax.psum(
            jnp.dot(grad_sims[2], embeds[2], preferred_element_type=jnp.float32).astype(
                jnp.bfloat16
            ),
            "seq",
        ).astype(jnp.float32),
    )
    selector_f = selector.astype(jnp.float32)
    grad_col = jnp.zeros((local_len, full_width), jnp.float32)
    for part in range(3):
        part_width = part_widths[part]
        grad_embed = jnp.einsum(
            "qt,qc->tc", grad_sims[part], query_emb[part], preferred_element_type=jnp.float32
        )
        grad_embed = grad_embed + jnp.einsum(
            "qt,qc->tc",
            selector_f,
            grad_query_emb[part],
            precision=HIGHEST,
            preferred_element_type=jnp.float32,
        )
        unused, pull_unit = jax.vjp(unit_rows, col[:, :part_width])
        grad_col = grad_col.at[:, :part_width].add(pull_unit(grad_embed)[0])
    grad_col_low = grad_col.astype(jnp.bfloat16)
    grad_w_col = matmul_left_t(final_low, grad_col_low)
    grad_hidden = cotangent[0].astype(jnp.float32) + matmul_right_t(grad_col_low, w_col)
    shard_lists = [[] for unused_slot in range(6)]
    col_share = None
    for layer_index in reversed(range(layer_count)):
        full = (
            lax.all_gather(attn_in[layer_index], ("seq", "row"), axis=0, tiled=True),
            lax.all_gather(attn_out[layer_index], ("seq", "row"), axis=0, tiled=True),
            lax.all_gather(ffn_up[layer_index], ("seq", "row"), axis=0, tiled=True),
            lax.all_gather(ffn_down[layer_index], ("seq", "row"), axis=0, tiled=True),
            lax.all_gather(norm_gains[layer_index], ("seq", "row"), axis=0, tiled=True),
            lax.all_gather(biases[layer_index], ("seq", "row"), axis=0, tiled=True),
            lax.all_gather(colbert, ("seq", "row"), axis=0, tiled=True),
        )
        grad_hidden, layer_grads = layer_backward(grad_hidden, full, records[layer_index])
        col_term = grad_w_col if layer_index == layer_count - 1 else jnp.zeros_like(grad_w_col)
        shares_out = (
            lax.psum_scatter(layer_grads[0], ("seq", "row"), scatter_dimension=0, tiled=True),
            lax.psum_scatter(layer_grads[1], ("seq", "row"), scatter_dimension=0, tiled=True),
            lax.psum_scatter(layer_grads[2], ("seq", "row"), scatter_dimension=0, tiled=True),
            lax.psum_scatter(layer_grads[3], ("seq", "row"), scatter_dimension=0, tiled=True),
            lax.psum_scatter(layer_grads[4], ("seq", "row"), scatter_dimension=0, tiled=True),
            lax.psum_scatter(layer_grads[5], ("seq", "row"), scatter_dimension=0, tiled=True),
            lax.psum_scatter(col_term, ("seq", "row"), scatter_dimension=0, tiled=True),
        )
        for slot in range(6):
            shard_lists[slot].insert(0, shares_out[slot])
        if layer_index == layer_count - 1:
            col_share = shares_out[6]
    stacked = [jnp.stack(items) for items in shard_lists]
    return (
        hidden.astype(jnp.bfloat16)[None],
        loss_total,
        grad_hidden[None],
        stacked[0],
        stacked[1],
        stacked[2],
        stacked[3],
        stacked[4],
        stacked[5],
        col_share,
        temp_grad,
    )


def solution(mesh):
    placed = (
        P("row", "seq", None),
        P(None, ("seq", "row"), None),
        P(None, ("seq", "row"), None),
        P(None, ("seq", "row"), None),
        P(None, ("seq", "row"), None),
        P(None, ("seq", "row")),
        P(None, ("seq", "row")),
        P(("seq", "row"), None),
        P(),
        P("row", "seq", None),
        P("row", None),
        P("row", None),
        P("row", None),
    )
    return jax.shard_map(
        body,
        mesh=mesh,
        in_specs=placed,
        out_specs=(
            P("row", "seq", None),
            P(),
            P("row", "seq", None),
            P(None, ("seq", "row"), None),
            P(None, ("seq", "row"), None),
            P(None, ("seq", "row"), None),
            P(None, ("seq", "row"), None),
            P(None, ("seq", "row")),
            P(None, ("seq", "row")),
            P(("seq", "row"), None),
            P(),
        ),
        check_vma=False,
    )
```

profile of v0, /device:TPU:0, one launch (start us, length us, event | category | flops | bytes accessed | tf_op | source)
XLA Modules:
  0.0 3033.3 jit_solution(3600083021751433587)
XLA Ops:
  14.1 43.6 %all-reduce.10 = (bf16[11264]{0:T(1024)(128)(2,1)}, bf16[11264]{0:T(1024)(128)(2,1)S(1)}, bf16[2048]{0:T(1024)(128)(2,1)}, bf16[2048]{0:T(1024)(128)(2,1)}) all-reduce(bf16[11264]{0:T(1024)(128)(2,1)S(1)} %dynamic-update-slice.10, bf16[11264]{0:T(1024)(128)(2,1)S(1)} %dynamic-update-slice.8, ...), channel_id=9, replica_groups=mesh['seq'=8,'row'=4] {'seq','row'}, use_global_device_ids=true, to_apply=%add.2 | all-reduce | flops 26624 | bytes 106496
  102.5 41.2 %all-gather.27.cloned.1.call-done = bf16[1152,1024]{1,0:T(8,128)(2,1)} async-done(((bf16[144,1024]{1,0:T(8,128)(2,1)}), bf16[1152,1024]{1,0:T(8,128)(2,1)}) %all-gather.27.cloned.1.call-update) | async-done | bytes 2359312 | tf_op jit(solution)/shard_map/all_gather | solution.py:349
  257.8 77.1 %all-gather.39.cloned.1.call-done = bf16[1,1024,4096]{2,1,0:T(8,128)(2,1)} async-done(((bf16[1,32,4096]{2,1,0:T(8,128)(2,1)}), bf16[1,1024,4096]{2,1,0:T(8,128)(2,1)}) %all-gather.39.cloned.1.call-update) | async-done | bytes 8388624 | tf_op jit(solution)/shard_map/all_gather | solution.py:308
  345.1 69.2 %all-gather.41.cloned.1.call-done = bf16[1,4096,1024]{2,1,0:T(8,128)(2,1)} async-done(((bf16[1,128,1024]{2,1,0:T(8,128)(2,1)}), bf16[1,4096,1024]{2,1,0:T(8,128)(2,1)}) %all-gather.41.cloned.1.call-update) | async-done | bytes 8388624 | tf_op jit(solution)/shard_map/all_gather | solution.py:309
  419.6 65.7 %all-gather.43.cloned.1.call-done = bf16[1,1024,3072]{2,1,0:T(8,128)(2,1)} async-done(((bf16[1,32,3072]{2,1,0:T(8,128)(2,1)}), bf16[1,1024,3072]{2,1,0:T(8,128)(2,1)}) %all-gather.43.cloned.1.call-update) | async-done | bytes 6291472 | tf_op jit(solution)/shard_map/all_gather | solution.py:306
  501.2 43.2 %all_gather.93 = bf16[1024,128]{1,0:T(8,128)(2,1)} all-gather(bf16[32,128]{1,0:T(8,128)(2,1)S(1)} %copy-done.180), channel_id=1, replica_groups=mesh['seq'=8,'row'=4] {'seq','row'}, dimensions={0}, use_global_device_ids=true | all-gather | bytes 270336 | tf_op jit(solution)/shard_map/all_gather | solution.py:312
  659.6 76.7 %all-gather.47.cloned.1.call-done = bf16[1,1024,4096]{2,1,0:T(8,128)(2,1)} async-done(((bf16[1,32,4096]{2,1,0:T(8,128)(2,1)}), bf16[1,1024,4096]{2,1,0:T(8,128)(2,1)}) %all-gather.47.cloned.1.call-update) | async-done | bytes 8388624 | tf_op jit(solution)/shard_map/all_gather | solution.py:308
  746.5 68.4 %all-gather.49.cloned.1.call-done = bf16[1,4096,1024]{2,1,0:T(8,128)(2,1)} async-done(((bf16[1,128,1024]{2,1,0:T(8,128)(2,1)}), bf16[1,4096,1024]{2,1,0:T(8,128)(2,1)}) %all-gather.49.cloned.1.call-update) | async-done | bytes 8388624 | tf_op jit(solution)/shard_map/all_gather | solution.py:309
  825.7 67.6 %all-reduce.21.cloned.1.call-done = (bf16[128,64]{0,1:T(8,128)(2,1)}, bf16[128,96]{0,1:T(8,128)(2,1)}, bf16[128,128]{1,0:T(8,128)(2,1)}) async-done(((bf16[128,64]{0,1:T(8,128)(2,1)}, bf16[128,96]{0,1:T(8,128)(2,1)}, bf16[128,128]{1,0:T(8,128)(2,1)}), (bf16[128,64]{0,1:T(8,128)(2,1)}, bf16[128,96]{0,1:T(8,128)(2,1)}, bf16[128,128]{1,0:T(8,128)(2,1)})) %all-reduce.21.cloned.1.call-update) | async-done | bytes 73744 | tf_op jit(solution)/shard_map/psum | solution.py:447
  988.9 68.3 %all-reduce.19.cloned.1.call-done = (bf16[128,128]{1,0:T(8,128)(2,1)}, bf16[128,96]{0,1:T(8,128)(2,1)}, bf16[128,64]{0,1:T(8,128)(2,1)}) async-done(((bf16[128,128]{1,0:T(8,128)(2,1)}, bf16[128,96]{0,1:T(8,128)(2,1)}, bf16[128,64]{0,1:T(8,128)(2,1)}), (bf16[128,128]{1,0:T(8,128)(2,1)}, bf16[128,96]{0,1:T(8,128)(2,1)}, bf16[128,64]{0,1:T(8,128)(2,1)})) %all-reduce.19.cloned.1.call-update) | async-done | bytes 73744 | tf_op jit(solution)/shard_map/psum | solution.py:489
  1095.2 43.5 %while.75 = (s32[]{:T(128)}, f32[144,16,64]{0,2,1:T(8,128)}, bf16[2,576,2048]{2,1,0:T(8,128)(2,1)}, bf16[2,576,16,64]{1,3,2,0:T(8,128)(2,1)}, s32[144]{0:T(256)}...) while((s32[]{:T(128)}, f32[144,16,64]{0,2,1:T(8,128)}, ...), condition=%wide.region_57.58_spmd.clone, body=%wide.region_56.57_spmd.clone.sunk | while | flops 869041152 | bytes 58898436 | solution.py:192
  1140.7 93.4 %reduce-scatter.16.cloned.1.call-done = bf16[144,2048]{1,0:T(8,128)(2,1)} async-done(((bf16[1152,2048]{1,0:T(8,128)(2,1)}), bf16[144,2048]{1,0:T(8,128)(2,1)}) %reduce-scatter.16.cloned.1.call-update) | async-done | bytes 589840 | tf_op jit(solution)/shard_map/reduce_scatter | solution.py:197
  1275.1 43.3 %while.76 = (s32[]{:T(128)}, f32[144,16,64]{0,2,1:T(8,128)}, bf16[2,576,2048]{2,1,0:T(8,128)(2,1)}, bf16[2,576,16,64]{1,3,2,0:T(8,128)(2,1)}, s32[144]{0:T(256)}...) while((s32[]{:T(128)}, f32[144,16,64]{0,2,1:T(8,128)}, ...), condition=%wide.region_65.66_spmd.clone, body=%wide.region_64.65_spmd.clone.sunk | while | flops 869041152 | bytes 58972220 | solution.py:192
  1329.0 84.7 %reduce-scatter.18.cloned.1.call-done = bf16[144,2048]{1,0:T(8,128)(2,1)} async-done(((bf16[1152,2048]{1,0:T(8,128)(2,1)}), bf16[144,2048]{1,0:T(8,128)(2,1)}) %reduce-scatter.18.cloned.1.call-update) | async-done | bytes 589840 | tf_op jit(solution)/shard_map/reduce_scatter | solution.py:197
  1503.7 52.7 %reduce-scatter.22.cloned.1.call-done = f32[32,1024]{1,0:T(8,128)} async-done(((f32[1024,1024]{1,0:T(8,128)}), f32[32,1024]{1,0:T(8,128)}) %reduce-scatter.22.cloned.1.call-update) | async-done | bytes 131088 | tf_op jit(solution)/shard_map/reduce_scatter | solution.py:543
  1556.4 138.9 %reduce-scatter.20.cloned.1.call-done = f32[32,1024]{1,0:T(8,128)} async-done(((f32[1024,1024]{1,0:T(8,128)}), f32[32,1024]{1,0:T(8,128)}) %reduce-scatter.20.cloned.1.call-update) | async-done | bytes 131088 | tf_op jit(solution)/shard_map/reduce_scatter | solution.py:543
  1702.8 117.2 %all-reduce.17.cloned.1.call-done = (f32[2048]{0:T(1024)}, f32[2048]{0:T(1024)}, f32[11264]{0:T(1024)}, f32[11264]{0:T(1024)}) async-done(((f32[2048]{0:T(1024)}, f32[2048]{0:T(1024)}, f32[11264]{0:T(1024)}, f32[11264]{0:T(1024)}), (f32[2048]{0:T(1024)}, f32[2048]{0:T(1024)}, f32[11264]{0:T(1024)}, f32[11264]{0:T(1024)})) %all-reduce.17.cloned.1.call-update) | async-done | bytes 106512
  1824.2 158.0 %reduce-scatter.36.cloned.1.call-done = f32[32,3072]{1,0:T(8,128)} async-done(((f32[1024,3072]{1,0:T(8,128)}), f32[32,3072]{1,0:T(8,128)}) %reduce-scatter.36.cloned.1.call-update) | async-done | bytes 393232
  1984.1 159.7 %reduce-scatter.34.cloned.1.call-done = f32[32,3072]{1,0:T(8,128)} async-done(((f32[1024,3072]{1,0:T(8,128)}), f32[32,3072]{1,0:T(8,128)}) %reduce-scatter.34.cloned.1.call-update) | async-done | bytes 393232
  2146.7 181.4 %reduce-scatter.30.cloned.1.call-done = f32[128,1024]{1,0:T(8,128)} async-done(((f32[4096,1024]{1,0:T(8,128)}), f32[128,1024]{1,0:T(8,128)}) %reduce-scatter.30.cloned.1.call-update) | async-done | bytes 524304 | tf_op jit(solution)/shard_map/reduce_scatter | solution.py:545
  2328.1 186.8 %reduce-scatter.28.cloned.1.call-done = f32[128,1024]{1,0:T(8,128)} async-done(((f32[4096,1024]{1,0:T(8,128)}), f32[128,1024]{1,0:T(8,128)}) %reduce-scatter.28.cloned.1.call-update) | async-done | bytes 524304 | tf_op jit(solution)/shard_map/reduce_scatter | solution.py:545
  2517.2 184.4 %reduce-scatter.26.cloned.1.call-done = f32[32,4096]{1,0:T(8,128)} async-done(((f32[1024,4096]{1,0:T(8,128)}), f32[32,4096]{1,0:T(8,128)}) %reduce-scatter.26.cloned.1.call-update) | async-done | bytes 524304 | tf_op jit(solution)/shard_map/reduce_scatter | solution.py:544
  2701.6 186.7 %reduce-scatter.24.cloned.1.call-done = f32[32,4096]{1,0:T(8,128)} async-done(((f32[1024,4096]{1,0:T(8,128)}), f32[32,4096]{1,0:T(8,128)}) %reduce-scatter.24.cloned.1.call-update) | async-done | bytes 524304 | tf_op jit(solution)/shard_map/reduce_scatter | solution.py:544
  2890.5 136.1 %reduce-scatter.32.cloned.1.call-done = f32[32,128]{1,0:T(8,128)} async-done(((f32[1024,128]{1,0:T(8,128)}), f32[32,128]{1,0:T(8,128)}) %reduce-scatter.32.cloned.1.call-update) | async-done | bytes 16400 | tf_op jit(solution)/shard_map/reduce_scatter | solution.py:548
  (817 shorter events, 776.5 us)
Async XLA Ops:
  9.0 134.6 %all-gather.27.cloned.1.call-start = ((), (), s32[]{:S(2)}) async-start(), calls=%async_computation.11 | async-start | bytes 2654208 | tf_op jit(solution)/shard_map/all_gather | solution.py:349
  94.8 160.6 %all-gather.37.cloned.1.call-start = ((), (), s32[]{:S(2)}) async-start(), calls=%async_computation.25 | async-start | bytes 2162688 | tf_op jit(solution)/shard_map/all_gather | solution.py:307
  95.5 239.4 %all-gather.39.cloned.1.call-start = ((), (), s32[]{:S(2)}) async-start(), calls=%async_computation.26 | async-start | bytes 8650752 | tf_op jit(solution)/shard_map/all_gather | solution.py:308
  96.5 317.8 %all-gather.41.cloned.1.call-start = ((), (), s32[]{:S(2)}) async-start(), calls=%async_computation.27 | async-start | bytes 8650752 | tf_op jit(solution)/shard_map/all_gather | solution.py:309
  97.4 387.9 %all-gather.43.cloned.1.call-start = ((), (), s32[]{:S(2)}) async-start(), calls=%async_computation.28 | async-start | bytes 6488064 | tf_op jit(solution)/shard_map/all_gather | solution.py:306
  98.1 448.5 %all-gather.31.cloned.1.call-start = ((), (), s32[]{:S(2)}) async-start(), calls=%async_computation.13 | async-start | bytes 2654208 | tf_op jit(solution)/shard_map/all_gather | solution.py:349
  495.2 104.2 %all-gather.33.cloned.1.call-start = ((), (), s32[]{:S(2)}) async-start(), calls=%async_computation.14 | async-start | bytes 2654208 | tf_op jit(solution)/shard_map/all_gather | solution.py:350
  497.1 160.0 %all-gather.45.cloned.1.call-start = ((), (), s32[]{:S(2)}) async-start(), calls=%async_computation.29 | async-start | bytes 2162688 | tf_op jit(solution)/shard_map/all_gather | solution.py:307
  497.6 238.6 %all-gather.47.cloned.1.call-start = ((), (), s32[]{:S(2)}) async-start(), calls=%async_computation.30 | async-start | bytes 8650752 | tf_op jit(solution)/shard_map/all_gather | solution.py:308
  498.4 316.5 %all-gather.49.cloned.1.call-start = ((), (), s32[]{:S(2)}) async-start(), calls=%async_computation.31 | async-start | bytes 8650752 | tf_op jit(solution)/shard_map/all_gather | solution.py:309
  499.0 394.4 %all-reduce.21.cloned.1.call-start = ((), (), s32[]{:S(2)}) async-start(), calls=%async_computation.36 | async-start | bytes 147456 | tf_op jit(solution)/shard_map/psum | solution.py:447
  825.1 232.2 %all-reduce.19.cloned.1.call-start = ((), (), s32[]{:S(2)}) async-start(), calls=%async_computation.35 | async-start | bytes 147456 | tf_op jit(solution)/shard_map/psum | solution.py:489
  987.9 246.2 %reduce-scatter.16.cloned.1.call-start = ((), (), s32[]{:S(2)}) async-start(), calls=%async_computation.15 | async-start | bytes 5308416 | tf_op jit(solution)/shard_map/reduce_scatter | solution.py:197
  1138.7 275.0 %reduce-scatter.18.cloned.1.call-start = ((), (), s32[]{:S(2)}) async-start(), calls=%async_computation.16 | async-start | bytes 5308416 | tf_op jit(solution)/shard_map/reduce_scatter | solution.py:197
  1318.5 237.9 %reduce-scatter.22.cloned.1.call-start = ((), (), s32[]{:S(2)}) async-start(), calls=%async_computation.18 | async-start | bytes 4325376 | tf_op jit(solution)/shard_map/reduce_scatter | solution.py:543
  1322.3 373.0 %reduce-scatter.20.cloned.1.call-start = ((), (), s32[]{:S(2)}) async-start(), calls=%async_computation.17 | async-start | bytes 4325376 | tf_op jit(solution)/shard_map/reduce_scatter | solution.py:543
  1326.1 493.9 %all-reduce.17.cloned.1.call-start = ((), (), s32[]{:S(2)}) async-start(), calls=%async_computation.34 | async-start | bytes 212992
  1425.2 557.0 %reduce-scatter.36.cloned.1.call-start = ((), (), s32[]{:S(2)}) async-start(), calls=%async_computation.33 | async-start | bytes 12976128
  1432.4 711.5 %reduce-scatter.34.cloned.1.call-start = ((), (), s32[]{:S(2)}) async-start(), calls=%async_computation.32 | async-start | bytes 12976128
  1452.5 875.6 %reduce-scatter.30.cloned.1.call-start = ((), (), s32[]{:S(2)}) async-start(), calls=%async_computation.22 | async-start | bytes 17301504 | tf_op jit(solution)/shard_map/reduce_scatter | solution.py:545
  1462.0 1052.9 %reduce-scatter.28.cloned.1.call-start = ((), (), s32[]{:S(2)}) async-start(), calls=%async_computation.21 | async-start | bytes 17301504 | tf_op jit(solution)/shard_map/reduce_scatter | solution.py:545
  1471.6 1230.0 %reduce-scatter.26.cloned.1.call-start = ((), (), s32[]{:S(2)}) async-start(), calls=%async_computation.20 | async-start | bytes 17301504 | tf_op jit(solution)/shard_map/reduce_scatter | solution.py:544
  1481.4 1406.9 %reduce-scatter.24.cloned.1.call-start = ((), (), s32[]{:S(2)}) async-start(), calls=%async_computation.19 | async-start | bytes 17301504 | tf_op jit(solution)/shard_map/reduce_scatter | solution.py:544
  1491.2 1535.4 %reduce-scatter.32.cloned.1.call-start = ((), (), s32[]{:S(2)}) async-start(), calls=%async_computation.23 | async-start | bytes 540672 | tf_op jit(solution)/shard_map/reduce_scatter | solution.py:548
  (212 other events, 6883.9 us)
Sparse Core Ops, SparseCore 0:
  11.4 72.2 all-gather.34
  146.4 50.5 all-gather.28
  200.3 54.9 all-gather.36
  258.6 76.2 all-gather.38
  338.2 76.0 all-gather.40
  417.1 68.0 all-gather.42
  495.3 51.2 all-gather.30
  602.1 54.8 all-gather.44
  659.9 76.2 all-gather.46
  739.0 75.8 all-gather.48
  825.2 68.0 all-reduce.20
  988.0 69.1 all-reduce.18
  1138.8 95.2 reduce-scatter.15
  1318.6 94.9 reduce-scatter.17
  1415.8 140.5 reduce-scatter.21
  1558.5 136.7 reduce-scatter.19
  1702.0 117.9 all-reduce.16
  1825.9 156.2 reduce-scatter.35
  1989.3 154.4 reduce-scatter.33
  2146.1 181.9 reduce-scatter.29
  2330.4 184.4 reduce-scatter.27
  2517.1 184.4 reduce-scatter.25
  2703.9 184.3 reduce-scatter.23
  2890.9 135.6 reduce-scatter.31
  (2 shorter events, 101.0 us)
where the time goes:
time: 3040 us; the launch traced here: 3030 us
  waiting for transfers between devices  2340 us (77%)
  matrix products  243 us (8%)
  local copies, waits for them, and re-layouts  177 us (6%)
  blocking collectives  156 us (5%)
  other arithmetic  94.3 us (3%)
    unnamed x29, waiting for transfers between devices  438 us
    reduce_scatter x2, waiting for transfers between devices, body(): lax.psum_scatter(layer_grads[2], ('seq', 'row'), scatter_dimension=0, til...  371 us
    reduce_scatter x2, waiting for transfers between devices, body(): lax.psum_scatter(layer_grads[3], ('seq', 'row'), scatter_dimension=0, til...  368 us
    reduce_scatter x2, waiting for transfers between devices, body(): lax.psum_scatter(layer_grads[1], ('seq', 'row'), scatter_dimension=0, til...  192 us
    reduce_scatter x2, waiting for transfers between devices, attend_back(): lax.psum_scatter(grad_rows.astype(jnp.bfloat16), 'seq', scatter_dimension...  178 us
    all_gather x2, waiting for transfers between devices, body(): lax.all_gather(ffn_up[layer_index], ('seq', 'row'), axis=0, tiled=True)  154 us
    all_gather x2, waiting for transfers between devices, body(): lax.all_gather(ffn_down[layer_index], ('seq', 'row'), axis=0, tiled=True)  138 us
    reduce_scatter x1, waiting for transfers between devices, body(): lax.psum_scatter(col_term, ('seq', 'row'), scatter_dimension=0, tiled=True)  136 us
  transfers between devices with their start and end apart: 26, of which 26 were waited for; matrix products, arithmetic and copies ran while one was open for 9% of the time, Pallas kernels for 0%

commit v1 on v0

--- a/solution.py
+++ b/solution.py
@@ -3,6 +3,8 @@
 import jax
 import jax.numpy as jnp
 from jax import lax
+from jax.experimental import pallas as pl
+from jax.experimental.pallas import tpu as pltpu
 from jax.sharding import PartitionSpec as P
 
 HEADS = 16
@@ -10,18 +12,67 @@
 NQ = 4
 NSD = 3
 
-
 NEG_FILL = -1e30
 SHARPNESS = 16.0
 HIGHEST = lax.Precision.HIGHEST
-
-
-def joined_2(value, axis, join):
-    pieces = jax.tree.map(lambda part: lax.all_gather(part, axis), value)
-    head = jax.tree.map(lambda part: part[0], pieces)
-    tail = jax.tree.map(lambda part: part[1:], pieces)
-    so_far, _ = lax.scan(lambda so_far, section: (join(so_far, section), None), head, tail)
-    return so_far
+BF = jnp.bfloat16
+F32 = jnp.float32
+
+def dot(left, right):
+    return jnp.dot(left, right, preferred_element_type=F32)
+
+
+def dot_lt(left, right):
+    return lax.dot_general(left, right, (((0,), (0,)), ((), ())), preferred_element_type=F32)
+
+
+def dot_rt(left, right):
+    return lax.dot_general(left, right, (((1,), (1,)), ((), ())), preferred_element_type=F32)
+
+
+PLANE = 8
+BOTH = ("seq", "row")
+
+
+def across(x, mask):
+    size = lax.axis_size("seq") * lax.axis_size("row")
+    return lax.ppermute(x, BOTH, [(d, d ^ mask) for d in range(size)])
+
+
+def turned(x):
+    size = lax.axis_size("seq") * lax.axis_size("row")
+    rows = lax.axis_size("row")
+    pairs = []
+    for d in range(size):
+        o, i, r = d // PLANE, d % PLANE // rows, d % rows
+        pairs.append((d, r * PLANE + i * rows + o))
+    return lax.ppermute(x, BOTH, pairs)
+
+
+def plane_gather(x):
+    other = {0: x, 2: across(x, 2), 4: across(x, 4), 6: across(x, 6)}
+    return jnp.stack([other[k & 6] if k % 2 == 0 else across(other[k & 6], 1) for k in range(PLANE)])
+
+
+def plane_scatter(parts):
+    parts = parts.astype(BF)
+    core = across(parts[1::2], 1).astype(F32) + parts[0::2].astype(F32)
+    sent = core[1:].astype(BF)
+    return core[0] + sum(across(sent[k - 1], 2 * k).astype(F32) for k in (1, 2, 3))
+
+
+def plane_exchange(x, relative):
+    x = jnp.take(x, relative, axis=0)
+    core = across(x[1::2], 1)
+    mine = [x[0], core[0]]
+    for k in (1, 2, 3):
+        got = across(jnp.stack([x[2 * k], core[k]]), 2 * k)
+        mine += [got[0], got[1]]
+    return jnp.take(jnp.stack(mine), relative, axis=0)
+
+
+def tie(*values):
+    return lax.optimization_barrier(values)
 
 
 def token_info(positions, lengths, kinds):
@@ -38,6 +89,541 @@
     doc_num = jnp.sum(jnp.where(onehot, doc_count[None, :], nothing), axis=1)
     offset = positions - seg_start
     return (segment, offset, is_query, query_num * QLEN + offset, doc_num)
+
+
+def rope_lanes(offset, head_dim):
+    half = head_dim // 2
+    inverse = jnp.exp(jnp.arange(half, dtype=F32) * (-2.0 * math.log(10000.0) / head_dim))
+    angle = offset.astype(F32)[:, None] * inverse[None, :]
+    cos, sin = jnp.cos(angle), jnp.sin(angle)
+    return (
+        jnp.concatenate([cos, cos, cos, cos], axis=1),
+        jnp.concatenate([-sin, -sin, sin, sin], axis=1),
+    )
+
+
+def swap_halves(x):
+    half = x.shape[-1] // 2
+    return jnp.concatenate([x[..., half:], x[..., :half]], axis=-1)
+
+
+def layer_norm(rows, gain, shift):
+    center = rows - jnp.mean(rows, axis=-1, keepdims=True)
+    variance = jnp.mean(center * center, axis=-1, keepdims=True)
+    return center * lax.rsqrt(variance + 1e-05) * gain + shift
+
+
+def unit_rows(rows):
+    return rows * lax.rsqrt(jnp.sum(rows * rows, axis=-1, keepdims=True) + 1e-06)
+
+
+def exact_gelu(values):
+    return jax.nn.gelu(values, approximate=False)
+
+
+def head_masks(width):
+    lane = lax.broadcasted_iota(jnp.int32, (1, width), 1)
+    first_qk = (lane % (width // 2)) < (width // 4)
+    first_v = lane < (width // 2)
+    return first_qk, first_v
+
+
+def pair_probs(query, keys, allowed, scale):
+    scores = dot_rt(query, keys) * scale
+    scores = jnp.where(allowed, scores, NEG_FILL)
+    top = jnp.max(scores, axis=-1, keepdims=True)
+    weights = jnp.exp(scores - top)
+    return weights / jnp.sum(weights, axis=-1, keepdims=True)
+
+
+def pair_forward(query, keys, values, allowed, scale):
+    first_qk, first_v = head_masks(query.shape[1])
+    zero = jnp.zeros((), query.dtype)
+    outs = []
+    for head in range(2):
+        mine = first_qk if head == 0 else jnp.logical_not(first_qk)
+        probs = pair_probs(jnp.where(mine, query, zero), keys, allowed, scale)
+        outs.append(dot(probs.astype(BF), values))
+    return jnp.where(first_v, outs[0], outs[1])
+
+
+def pair_backward(query, keys, values, grad, allowed, scale):
+    first_qk, first_v = head_masks(query.shape[1])
+    zero = jnp.zeros((), query.dtype)
+    grad_query, grad_keys, grad_values = [], 0.0, 0.0
+    for head in range(2):
+        mine = first_qk if head == 0 else jnp.logical_not(first_qk)
+        mine_v = first_v if head == 0 else jnp.logical_not(first_v)
+        query_h = jnp.where(mine, query, zero)
+        grad_h = jnp.where(mine_v, grad, zero)
+        probs = pair_probs(query_h, keys, allowed, scale)
+        grad_probs = dot_rt(grad_h, values)
+        delta = jnp.sum(probs * grad_probs, axis=-1, keepdims=True)
+        grad_scores = (probs * (grad_probs - delta)).astype(BF)
+        grad_query.append(dot(grad_scores, keys))
+        grad_keys = grad_keys + dot_lt(grad_scores, query_h)
+        grad_values = grad_values + dot_lt(probs.astype(BF), grad_h)
+    return (
+        jnp.where(first_qk, grad_query[0], grad_query[1]) * scale,
+        grad_keys * scale,
+        grad_values,
+    )
+
+
+def block_of(count):
+    for blocks in (3, 4, 2):
+        if count % (blocks * 128) == 0 and count // blocks <= 512:
+            return count // blocks
+    return 128
+
+
+def attend_kernel(scale, seg_q, seg_k, query, keys, values, out):
+    allowed = seg_q[...] == seg_k[...]
+    out[...] = pair_forward(query[...], keys[...], values[...], allowed, scale).astype(out.dtype)
+
+
+def attend(qkv, seg_col, seg_row, scale):
+    count = qkv.shape[0]
+    wide = qkv.shape[1] // 3
+    block = block_of(count)
+
+    def kernel(seg_q, seg_k, query, keys, values, out):
+        attend_kernel(scale, seg_q, seg_k, query, keys, values, out)
+
+    return pl.pallas_call(
+        kernel,
+        grid=(count // block,),
+        in_specs=[
+            pl.BlockSpec((block, 1), lambda i: (i, 0)),
+            pl.BlockSpec((1, count), lambda i: (0, 0)),
+            pl.BlockSpec((block, wide), lambda i: (i, 0)),
+            pl.BlockSpec((count, wide), lambda i: (0, 1)),
+            pl.BlockSpec((count, wide), lambda i: (0, 2)),
+        ],
+        out_specs=pl.BlockSpec((block, wide), lambda i: (i, 0)),
+        out_shape=jax.ShapeDtypeStruct((count, wide), BF),
+        compiler_params=pltpu.CompilerParams(vmem_limit_bytes=40 * 1024 * 1024),
+        cost_estimate=pl.CostEstimate(
+            flops=8 * count * count * wide, bytes_accessed=8 * count * wide, transcendentals=2 * count * count
+        ),
+    )(seg_col, seg_row, qkv, qkv, qkv)
+
+
+def attend_back(qkv, grad, seg_col, seg_row, cos, sin, scale):
+    count = qkv.shape[0]
+    wide = qkv.shape[1] // 3
+    block = block_of(count)
+    steps = count // block
+
+    def kernel(seg_q, seg_k, query, keys, values, grad_ref, cos_b, sin_b, cos_all, sin_all, dq, dk, dv, acc_k, acc_v):
+        step = pl.program_id(0)
+        allowed = seg_q[...] == seg_k[...]
+        grad_query, grad_keys, grad_values = pair_backward(
+            query[...], keys[...], values[...], grad_ref[...], allowed, scale
+        )
+        dq[...] = (grad_query * cos_b[...] - swap_halves(grad_query) * sin_b[...]).astype(BF)
+
+        @pl.when(step == 0)
+        def _():
+            acc_k[...] = grad_keys
+            acc_v[...] = grad_values
+
+        @pl.when(step > 0)
+        def _():
+            acc_k[...] += grad_keys
+            acc_v[...] += grad_values
+
+        @pl.when(step == steps - 1)
+        def _():
+            total = acc_k[...]
+            dk[...] = (total * cos_all[...] - swap_halves(total) * sin_all[...]).astype(BF)
+            dv[...] = acc_v[...].astype(BF)
+
+    whole = pl.BlockSpec((count, wide), lambda i: (0, 0))
+    part = pl.BlockSpec((block, wide), lambda i: (i, 0))
+    return pl.pallas_call(
+        kernel,
+        grid=(steps,),
+        in_specs=[
+            pl.BlockSpec((block, 1), lambda i: (i, 0)),
+            pl.BlockSpec((1, count), lambda i: (0, 0)),
+            part,
+            pl.BlockSpec((count, wide), lambda i: (0, 1)),
+            pl.BlockSpec((count, wide), lambda i: (0, 2)),
+            part,
+            part,
+            part,
+            whole,
+            whole,
+        ],
+        out_specs=(part, whole, whole),
+        out_shape=tuple(jax.ShapeDtypeStruct((count, wide), BF) for _ in range(3)),
+        scratch_shapes=[pltpu.VMEM((count, wide), F32), pltpu.VMEM((count, wide), F32)],
+        compiler_params=pltpu.CompilerParams(vmem_limit_bytes=48 * 1024 * 1024),
+        cost_estimate=pl.CostEstimate(
+            flops=20 * count * count * wide, bytes_accessed=20 * count * wide, transcendentals=2 * count * count
+        ),
+    )(seg_col, seg_row, qkv, qkv, qkv, grad, cos, sin, cos, sin)
+
+
+def body(
+    tokens,
+    attn_in,
+    attn_out,
+    ffn_up,
+    ffn_down,
+    norm_gains,
+    biases,
+    colbert,
+    log_scale,
+    cotangent,
+    seg_lengths,
+    seg_kinds,
+    pairing,
+):
+    S = lax.axis_size("seq")
+    R = lax.axis_size("row")
+    O = S * R // PLANE
+    place = lax.axis_index("seq") * R + lax.axis_index("row")
+    plane, far = place % PLANE, place // PLANE
+    relative = jnp.bitwise_xor(plane, jnp.arange(PLANE, dtype=jnp.int32))
+    T = tokens.shape[1]
+    D = tokens.shape[2]
+    N = PLANE * T
+    L = attn_in.shape[0]
+    head_dim = D // HEADS
+    half = head_dim // 2
+    scale = head_dim ** (-0.5)
+    wide = 2 * head_dim
+    in_cols = 3 * wide
+    in_rows = attn_in.shape[1]
+    rows_in = PLANE * in_rows
+    FF = ffn_up.shape[2]
+    up_cols = FF // (S * R)
+    hidden_cols = O * up_cols
+    gain_part = norm_gains.shape[1]
+    bias_part = biases.shape[1]
+    part = gain_part + bias_part
+    along_z = [[o * (S // O) + i for o in range(O)] for i in range(S // O)]
+    is_mine = jnp.arange(PLANE, dtype=jnp.int32) == plane
+
+    def padded_rows(vector, width=D):
+        rows = -(-vector.shape[0] // (16 * width)) * 16
+        return jnp.pad(vector, (0, rows * width - vector.shape[0])).reshape(rows, width)
+
+    def pack_columns(w):
+        lead = w.shape[:-1]
+        n = len(lead)
+        qk = w[..., : 2 * D].reshape(*lead, 2, PLANE, 2, 2, half)
+        qk = qk.transpose((n + 1,) + tuple(range(n)) + (n, n + 3, n + 2, n + 4)).reshape(PLANE, *lead, 2 * wide)
+        v = w[..., 2 * D :].reshape(*lead, PLANE, wide)
+        v = v.transpose((n,) + tuple(range(n)) + (n + 1,))
+        return jnp.concatenate([qk, v], axis=-1)
+
+    def unpack_columns(w):
+        rows = w.shape[1]
+        qk = w[:, :, : 2 * wide].reshape(PLANE, rows, 2, 2, 2, half)
+        qk = qk.transpose(1, 2, 0, 4, 3, 5).reshape(rows, 2 * D)
+        v = w[:, :, 2 * wide :].transpose(1, 0, 2).reshape(rows, D)
+        return jnp.concatenate([qk, v], axis=1)
+
+    def pack_hidden(w):
+        rows = w.shape[0]
+        return w.reshape(rows, O, PLANE, up_cols).transpose(2, 0, 1, 3).reshape(PLANE, rows, hidden_cols)
+
+    def unpack_hidden(w):
+        rows = w.shape[1]
+        return w.reshape(PLANE, rows, O, up_cols).transpose(1, 2, 0, 3).reshape(rows, FF)
+
+    def fold(w):
+        n = w.shape[-2] // 2
+        return jnp.concatenate([w[..., :n, :], w[..., n:, :]], axis=-1)
+
+    def unfold(w):
+        n = w.shape[-1] // 2
+        return jnp.concatenate([w[..., :n], w[..., n:]], axis=-2)
+
+    shard_in = [plane_exchange(pack_columns(attn_in[0]), relative).reshape(rows_in, in_cols)]
+    small = jnp.concatenate(
+        [norm_gains.reshape(-1), biases.reshape(-1), colbert.reshape(-1)]
+    )
+    count_small = L * part
+    small = jnp.take(plane_gather(small), relative, axis=0)
+    params_plane = jnp.concatenate(
+        [
+            small[:, : L * gain_part].reshape(PLANE, L, gain_part),
+            small[:, L * gain_part : count_small].reshape(PLANE, L, bias_part),
+        ],
+        axis=2,
+    ).reshape(-1)
+    col_plane = small[:, count_small:].reshape(-1)
+    to_group = [(b, (b % O) * PLANE + b // O) for b in range(O * PLANE)]
+    from_group = [(d, b) for b, d in to_group]
+    shard_out = lax.ppermute(attn_out, BOTH, to_group)
+    table = turned(jnp.concatenate([seg_lengths[0], seg_kinds[0], pairing[0]]))
+    seg_count = seg_lengths.shape[1]
+    lengths, kinds = table[:seg_count], table[seg_count : 2 * seg_count]
+    pairs_of = table[2 * seg_count :]
+    hidden_low = turned(tokens[0])
+
+    def gather_far(parts):
+        return lax.all_gather(jnp.concatenate(parts, axis=0), "seq", axis=0, axis_index_groups=along_z)
+
+    rest = jnp.concatenate(
+        [pack_hidden(ffn_up[0])]
+        + [piece for layer in range(1, L) for piece in (pack_columns(attn_in[layer]), pack_hidden(ffn_up[layer]))],
+        axis=-1,
+    )
+    rest = plane_exchange(rest, relative).reshape(rows_in, -1)
+    shard_up = [rest[:, :hidden_cols]]
+    at = hidden_cols
+    for layer in range(1, L):
+        shard_in.append(rest[:, at : at + in_cols])
+        shard_up.append(rest[:, at + in_cols : at + in_cols + hidden_cols])
+        at += in_cols + hidden_cols
+
+    def attn_block(layer):
+        out = shard_out[layer].reshape(in_rows, PLANE, wide).transpose(1, 0, 2).reshape(rows_in, wide)
+        return jnp.concatenate([shard_in[layer], out], axis=1)
+
+    w_ins, w_outs, w_ups, w_downs = [], [], [], []
+    for layer in range(L):
+        own = [attn_block(layer)]
+        if layer == 0:
+            own.append(padded_rows(params_plane, in_cols + wide))
+        full = gather_far(own)
+        w_ins.append(full[:, :rows_in, :in_cols].reshape(D, in_cols))
+        w_out = full[:, :rows_in, in_cols:].reshape(O, PLANE, in_rows, wide).transpose(0, 2, 1, 3)
+        w_outs.append(w_out.reshape(wide, D))
+        if layer == 0:
+            params = full[:, rows_in:].reshape(O, -1)[:, : PLANE * L * part].reshape(O, PLANE, L, part)
+        own = [fold(shard_up[layer]), ffn_down[layer]]
+        if layer == L - 1:
+            own.append(padded_rows(col_plane))
+        full = gather_far(own)
+        w_ups.append(unfold(full[:, : rows_in // 2]).reshape(D, hidden_cols))
+        w_downs.append(full[:, rows_in // 2 : rows_in // 2 + up_cols].reshape(hidden_cols, D))
+        if layer == L - 1:
+            w_col = full[:, rows_in // 2 + up_cols :].reshape(O, -1)[:, : col_plane.size]
+            w_col = w_col.reshape(D, colbert.shape[1])
+    params = params.transpose(2, 0, 1, 3).astype(F32)
+    gains_all = params[..., :gain_part].reshape(L, D * 2)
+    bias_all = params[..., gain_part:].reshape(L, S * R * bias_part)
+
+    block_at = (relative % R) * (PLANE // R) + relative // R
+    positions = (block_at[:, None] * T + jnp.arange(T, dtype=jnp.int32)[None, :]).reshape(N)
+    held_segment, held_offset = token_info(positions, lengths, kinds)[:2]
+    cos, sin = rope_lanes(held_offset, head_dim)
+    seg_col, seg_row = held_segment[:, None], held_segment[None, :]
+
+    def layer_params(layer):
+        bias = bias_all[layer]
+        gains = gains_all[layer]
+        bias_in = jnp.take(pack_columns(bias[: 3 * D]), plane, axis=0)
+        bias_up = jnp.take(pack_hidden(bias[None, 4 * D : 4 * D + FF]), plane, axis=0)[0]
+        rest_at = 4 * D + FF
+        return (
+            gains[:D],
+            gains[D:],
+            bias_in,
+            bias[3 * D : 4 * D],
+            bias_up,
+            bias[rest_at : rest_at + D],
+            bias[rest_at + D : rest_at + 2 * D],
+            bias[rest_at + 2 * D :],
+        )
+
+    def gathered(x):
+        return plane_gather(x).reshape(N, x.shape[1])
+
+    def scattered(x):
+        return plane_scatter(x.reshape(PLANE, T, D))
+
+    hidden = hidden_low.astype(F32)
+    records = []
+    for layer in range(L):
+        gain_one, gain_two, bias_in, bias_out, bias_up, bias_down, shift_one, shift_two = layer_params(layer)
+        x_all = gathered(hidden_low)
+        mixed = (dot(x_all, w_ins[layer]) + bias_in).reshape(N, 3, wide)
+        qk = mixed[:, :2]
+        qk = qk * cos[:, None] + swap_halves(qk) * sin[:, None]
+        qkv = jnp.concatenate([qk, mixed[:, 2:]], axis=1).astype(BF).reshape(N, in_cols)
+        context = attend(qkv, seg_col, seg_row, scale)
+        first = hidden + scattered(dot(context, w_outs[layer])) + bias_out
+        normed = layer_norm(first, gain_one, shift_one)
+        normed_all = gathered(normed.astype(BF))
+        pre = dot(normed_all, w_ups[layer]) + bias_up
+        act = exact_gelu(pre).astype(BF)
+        second = normed + scattered(dot(act, w_downs[layer])) + bias_down
+        records.append((x_all, qkv, context, first, normed_all, pre, act, second))
+        hidden = layer_norm(second, gain_two, shift_two)
+        hidden_low = hidden.astype(BF)
+    hidden_out = turned(hidden_low)
+
+    full_width = w_col.shape[1]
+    part_widths = (full_width, full_width * 3 // 4, full_width // 2)
+    query_total = NQ * QLEN
+    doc_total = NSD + 1
+    col = dot(hidden_low, w_col)
+    in_order = jnp.arange(PLANE, dtype=jnp.int32)
+    in_order = jnp.bitwise_xor((in_order % (PLANE // R)) * R + in_order // (PLANE // R), plane)
+    col_row = jnp.take(plane_gather(col.astype(BF)), in_order, axis=0).reshape(N, full_width).astype(F32)
+    own_at = block_at[0] * T
+    row_positions = jnp.arange(N, dtype=jnp.int32)
+    segment, offset, is_query, query_slot, doc_num = token_info(row_positions, lengths, kinds)
+    slots = jnp.arange(query_total, dtype=jnp.int32)[:, None]
+    selector = (is_query == 1)[None, :] & (query_slot[None, :] == slots)
+    selector_low = selector.astype(BF)
+    own_selector = lax.dynamic_slice(selector.astype(F32), (0, own_at), (query_total, T))
+    embeds = [unit_rows(col_row[:, :width]).astype(BF) for width in part_widths]
+    query_emb = [dot(selector_low, embed).astype(BF) for embed in embeds]
+    powers = jnp.exp(SHARPNESS * jnp.stack([dot_rt(query_emb[m], embeds[m]) for m in range(3)]))
+    doc_code = jnp.where(is_query == 0, doc_num, -1)[None, None, :]
+    totals = jnp.stack([jnp.sum(jnp.where(doc_code == d, powers, 0.0), axis=2) for d in range(doc_total)], axis=2)
+    soft = jnp.log(totals) / SHARPNESS
+    pair_sum = jnp.sum(soft.reshape(3, NQ, QLEN, doc_total), axis=2)
+    inverse_temp = jnp.exp(log_scale[0])
+    logits = pair_sum * inverse_temp / QLEN
+    positive = pairs_of[None, :, None] == jnp.arange(doc_total, dtype=jnp.int32)[None, None, :]
+    losses = jax.nn.logsumexp(logits, axis=-1) - jnp.sum(jnp.where(positive, logits, 0.0), axis=-1)
+    loss_weight = 1.0 / (3 * NQ * R)
+    grad_logits = loss_weight * (jax.nn.softmax(logits, axis=-1) - positive.astype(F32))
+    loss_terms = jnp.stack([jnp.sum(losses) * loss_weight, jnp.sum(grad_logits * logits)])
+    loss_terms = loss_terms + across(loss_terms, PLANE)
+    loss_terms = loss_terms + across(loss_terms, 2 * PLANE)
+    grad_pairs = grad_logits * inverse_temp / QLEN
+    grad_soft = jnp.broadcast_to(grad_pairs[:, :, None, :], (3, NQ, QLEN, doc_total)).reshape(
+        3, query_total, doc_total
+    )
+    ratio = grad_soft / totals
+    weight = sum(jnp.where(doc_code == d, ratio[:, :, d : d + 1], 0.0) for d in range(doc_total))
+    grad_sims = (powers * weight).astype(BF)
+    own_sims = lax.dynamic_slice(grad_sims, (0, 0, own_at), (3, query_total, T))
+    grad_col = jnp.zeros((T, full_width), F32)
+    for m in range(3):
+        width = part_widths[m]
+        grad_query = dot(grad_sims[m], embeds[m])
+        grad_embed = dot_lt(own_sims[m], query_emb[m]) + lax.dot_general(
+            own_selector, grad_query, (((0,), (0,)), ((), ())), precision=HIGHEST, preferred_element_type=F32
+        )
+        pull_unit = jax.vjp(unit_rows, col[:, :width])[1]
+        grad_col = grad_col + jnp.pad(pull_unit(grad_embed)[0], ((0, 0), (0, full_width - width)))
+    grad_col_low = grad_col.astype(BF)
+    col_parts = dot_lt(hidden_low, grad_col_low).reshape(O, PLANE, in_rows, full_width).transpose(1, 0, 2, 3)
+    col_parts = plane_scatter(jnp.take(col_parts.reshape(PLANE, O * in_rows, full_width), relative, axis=0))
+    col_rows = jax.vmap(padded_rows)(col_parts.reshape(O, in_rows * full_width)).astype(BF)
+    grad_hidden = turned(cotangent[0]).astype(F32) + dot_rt(grad_col_low, w_col)
+
+    def joined_blocks(parts):
+        return jnp.concatenate([item.astype(BF) for item in parts], axis=1)
+
+    def scatter_far(whole):
+        whole = whole.reshape(-1, whole.shape[-1])
+        return lax.psum_scatter(whole, "seq", scatter_dimension=0, tiled=True, axis_index_groups=along_z)
+
+    def scatter_far_direct(whole):
+        total = jnp.take(whole, far, axis=0).astype(F32)
+        for step in range(1, O):
+            total = total + across(jnp.take(whole, far ^ step, axis=0), PLANE * step).astype(F32)
+        return total
+
+    outs = [[None] * L for _ in range(7)]
+
+    def finish_ffn(layer, shares):
+        back_up = plane_exchange(unfold(shares[: rows_in // 2]).reshape(PLANE, in_rows, hidden_cols), relative)
+        outs[2][layer] = unpack_hidden(back_up).astype(F32)
+        at = rows_in // 2 + up_cols
+        outs[3][layer] = shares[rows_in // 2 : at].astype(F32)
+        outs[1][layer] = lax.ppermute(shares[at : at + in_rows], BOTH, from_group).astype(F32)
+        if layer == L - 1:
+            col_share = shares[at + in_rows :].reshape(-1)[: in_rows * full_width]
+            outs[6][layer] = col_share.reshape(in_rows, full_width).astype(F32)
+
+    def finish_in(layer, shares):
+        vector = shares[rows_in:].reshape(-1)[: PLANE * part].reshape(PLANE, part)
+        vector = plane_scatter(jnp.take(vector, relative, axis=0))
+        outs[4][layer] = vector[:gain_part]
+        outs[5][layer] = vector[gain_part:]
+        back_in = plane_exchange(shares[:rows_in].astype(BF).reshape(PLANE, in_rows, in_cols), relative)
+        outs[0][layer] = unpack_columns(back_in).astype(F32)
+
+    shares_in = None
+    for layer in reversed(range(L)):
+        gain_one, gain_two, bias_in, bias_out, bias_up, bias_down, shift_one, shift_two = layer_params(layer)
+        x_all, qkv, context, first, normed_all, pre, act, second = records[layer]
+        pull_two = jax.vjp(layer_norm, second, gain_two, shift_two)[1]
+        grad_second, grad_gain_two, grad_shift_two = pull_two(grad_hidden)
+        grad_ffo = grad_second.astype(BF)
+        grad_bias_down = jnp.sum(grad_ffo.astype(F32), axis=0)
+        ffo_all = gathered(grad_ffo)
+        grad_act = dot_rt(ffo_all, w_downs[layer])
+        pull_gelu = jax.vjp(exact_gelu, pre)[1]
+        grad_pre = pull_gelu(grad_act)[0].astype(BF)
+        grad_bias_up = jnp.sum(grad_pre.astype(F32), axis=0)
+        grad_normed = grad_second + scattered(dot_rt(grad_pre, w_ups[layer]))
+        pull_one = jax.vjp(layer_norm, first, gain_one, shift_one)[1]
+        grad_first, grad_gain_one, grad_shift_one = pull_one(grad_normed)
+        grad_branch = grad_first.astype(BF)
+        grad_bias_out = jnp.sum(grad_branch.astype(F32), axis=0)
+        branch_all = gathered(grad_branch)
+        grad_context = dot_rt(branch_all, w_outs[layer]).astype(BF)
+        blocks = [
+            fold(dot_lt(normed_all, grad_pre).reshape(O, rows_in, hidden_cols)),
+            dot_lt(act, ffo_all).reshape(O, up_cols, D),
+            dot_lt(context, branch_all).reshape(O, in_rows, D),
+        ]
+        if layer == L - 1:
+            blocks.append(col_rows)
+        grad_context, blocks = tie(grad_context, joined_blocks(blocks))
+        shares_ffn = scatter_far(blocks)
+        if shares_in is not None:
+            grad_context, shares_in = tie(grad_context, shares_in)
+            finish_in(layer + 1, shares_in)
+        dq, dk, dv = attend_back(qkv, grad_context, seg_col, seg_row, cos, sin, scale)
+        grad_mixed = jnp.concatenate([dq, dk, dv], axis=1)
+        grad_hidden = grad_first + scattered(dot_rt(grad_mixed, w_ins[layer]))
+        grad_bias_in = jnp.sum(grad_mixed.astype(F32), axis=0)
+        if layer > 0:
+            grad_hidden, shares_ffn = tie(grad_hidden, shares_ffn)
+        finish_ffn(layer, shares_ffn)
+
+        spot = is_mine[:, None, None].astype(F32)
+        natural = unpack_columns(spot * grad_bias_in.reshape(1, 1, in_cols))[0]
+        spread_up = unpack_hidden(spot * grad_bias_up.reshape(1, 1, hidden_cols))[0]
+        vector_gain = jnp.concatenate([grad_gain_one, grad_gain_two]).reshape(O, PLANE, gain_part)
+        vector_bias = jnp.concatenate(
+            [natural, grad_bias_out, spread_up, grad_bias_down, grad_shift_one, grad_shift_two]
+        ).reshape(O, PLANE, bias_part)
+        vector = jnp.concatenate([vector_gain, vector_bias], axis=2).reshape(O, PLANE * part)
+        grad_in = dot_lt(x_all, grad_mixed).reshape(O, rows_in, in_cols)
+        blocks = joined_blocks([grad_in, jax.vmap(lambda row: padded_rows(row, in_cols))(vector)])
+        grad_hidden, blocks = tie(grad_hidden, blocks)
+        if layer > 0:
+            shares_in = scatter_far(blocks)
+    finish_in(0, scatter_far_direct(blocks))
+    col_share = outs.pop()[L - 1]
+    stacked = [jnp.stack(items) for items in outs]
+    return (
+        hidden_out[None],
+        loss_terms[:1],
+        turned(grad_hidden.astype(BF)).astype(F32)[None],
+        stacked[0],
+        stacked[1],
+        stacked[2],
+        stacked[3],
+        stacked[4],
+        stacked[5],
+        col_share,
+        loss_terms[1:],
+    )
+
+
+def joined_2(value, axis, join):
+    pieces = jax.tree.map(lambda part: lax.all_gather(part, axis), value)
+    head = jax.tree.map(lambda part: part[0], pieces)
+    tail = jax.tree.map(lambda part: part[1:], pieces)
+    so_far, _ = lax.scan(lambda so_far, section: (join(so_far, section), None), head, tail)
+    return so_far
 
 
 def rope_tables(offset, head_dim):
@@ -66,20 +652,6 @@
     return turned.reshape(length, flat.shape[1])
 
 
-def layer_norm(rows, gain, shift):
-    center = rows - jnp.mean(rows, axis=-1, keepdims=True)
-    variance = jnp.mean(center * center, axis=-1, keepdims=True)
-    return center * lax.rsqrt(variance + 1e-05) * gain + shift
-
-
-def unit_rows(rows):
-    return rows * lax.rsqrt(jnp.sum(rows * rows, axis=-1, keepdims=True) + 1e-06)
-
-
-def exact_gelu(values):
-    return jax.nn.gelu(values, approximate=False)
-
-
 def block_for(count):
     blocks = count
     while blocks > 1024 and blocks % 2 == 0:
@@ -102,7 +674,7 @@
     return jnp.einsum("to,io->ti", left, right, preferred_element_type=jnp.float32)
 
 
-def body(
+def body_wide(
     tokens,
     attn_in,
     attn_out,
@@ -583,8 +1155,9 @@
         P("row", None),
         P("row", None),
     )
+    planes = mesh.shape["row"] == 4 and mesh.shape["seq"] * 4 == 4 * PLANE and HEADS == 2 * PLANE
     return jax.shard_map(
-        body,
+        body if planes else body_wide,
         mesh=mesh,
         in_specs=placed,
         out_specs=(

time: 3040 us -> 820 us (0.27)
  waiting for transfers between devices: 2340 us -> 210 us
  matrix products: 243 us -> 66.7 us
  starting transfers between devices: 1.82 us -> 169 us
  blocking collectives: 156 us -> 0 us
  Pallas kernels: 0 us -> 38.9 us
    reduce_scatter x9 -> x3, waiting for transfers between devices: 1250 us -> 0.04 us  [scatter_far(): lax.psum_scatter(whole, 'seq', scatter_dimension=0, tiled=True, axis_inde...]
    all_gather x12 -> x4, waiting for transfers between devices: 522 us -> 1.84 us  [gather_far(): lax.all_gather(jnp.concatenate(parts, axis=0), 'seq', axis=0, axis_index_...]
    unnamed x29 -> x7, waiting for transfers between devices: 438 us -> 0.12 us
    ppermute x0 -> x151, waiting for transfers between devices: none -> 208 us  [the longest x143 208 us: across(): return lax.ppermute(x, BOTH, [(d, d ^ mask) for d in range(size)])]
    dot_general x69 -> x42, matrix products: 237 us -> 66.7 us  [the longest x15 29.9 us: dot(): return jnp.dot(left, right, preferred_element_type=F32)]
    ppermute x0 -> x151, starting transfers between devices: none -> 168 us  [the longest x143 152 us: across(): return lax.ppermute(x, BOTH, [(d, d ^ mask) for d in range(size)])]
    psum x2 -> x0, waiting for transfers between devices: 136 us -> none  [the longest x1 68.3 us: body(): lax.psum(jnp.dot(grad_sims[0], embeds[0], preferred_element_type=jnp.floa...]
    all_gather x3 -> x0, blocking collectives: 105 us -> none  [the longest x2 61.3 us: joined_2(): pieces = jax.tree.map(lambda part: lax.all_gather(part, axis), value)]
  transfers between devices with their start and end apart: 26 -> 158, of which waited for: 26 -> 54; matrix products, arithmetic and copies ran while one was open for 9% -> 39% of each run, Pallas kernels for 0% -> 5%
where the time goes in v1:
time: 820 us; the launch traced here: 809 us
  waiting for transfers between devices  210 us (26%)
  local copies, waits for them, and re-layouts  187 us (23%)
  starting transfers between devices  169 us (21%)
  other arithmetic  117 us (14%)
  matrix products  66.7 us (8%)
  Pallas kernels  38.9 us (5%)
  between operations  20 us (2%)
    ppermute x143, waiting for transfers between devices, across(): return lax.ppermute(x, BOTH, [(d, d ^ mask) for d in range(size)])  208 us
    ppermute x143, starting transfers between devices, across(): return lax.ppermute(x, BOTH, [(d, d ^ mask) for d in range(size)])  152 us
    unnamed x440, local copies, waits for them, and re-layouts  59.2 us
    dot_general x15, matrix products, dot(): return jnp.dot(left, right, preferred_element_type=F32)  29.9 us
    dot_general x8, local copies, waits for them, and re-layouts, dot_lt(): lax.dot_general(left, right, (((0,), (0,)), ((), ())), preferred_element_...  24.3 us
    pallas_call x2, Pallas kernels, attend_back(): pl.pallas_call(kernel, grid=(steps,), in_specs=[pl.BlockSpec((block, 1),...  23.8 us
    add x6, other arithmetic, plane_scatter(): core = across(parts[1::2], 1).astype(F32) + parts[0::2].astype(F32)  18.2 us
    dot_general x12, matrix products, dot_lt(): lax.dot_general(left, right, (((0,), (0,)), ((), ())), preferred_element_...  18.2 us
  transfers between devices with their start and end apart: 158, of which 54 were waited for; matrix products, arithmetic and copies ran while one was open for 39% of the time, Pallas kernels for 5%

profile of v1, /device:TPU:0, one launch (start us, length us, event | category | flops | bytes accessed | tf_op | source)
XLA Modules:
  0.0 808.8 jit_solution(11955484533684877117)
XLA Ops:
  75.1 8.1 collective-permute-done.33
  113.6 7.5 shard_map.212
  146.7 5.6 collective-permute-done.23
  159.4 5.6 collective-permute-done.26
  165.0 7.1 collective-permute-done.28
  186.7 9.4 %multiply_convert_fusion.1 = (bf16[1152,512]{1,0:T(8,128)(2,1)S(1)}, f32[1152,512]{1,0:T(8,128)}, f32[1152,512]{1,0:T(8,128)}) fusion(f32[512]{0:T(512)S(1)} %bitcast.913, bf16[1152,1024]{1,0:T(8,128)(2,1)} %bitcast.44, bf16[1024,512]{1,0:T(8,128)(2,1)S(1)} %bitcast.857), kind=kOutput, calls=%fused_computation.98 | convolution fusion | flops 1246887936 | bytes 9308160 | tf_op jit(solution)/shard_map/dot_general | solution.py:22
  218.0 6.7 collective-permute-done.38
  261.4 7.6 shard_map.213
  290.2 6.5 collective-permute-done.49
  317.8 7.6 multiply_convert_fusion
  428.7 5.9 fusion.4
  457.8 5.8 collective-permute-done.82
  469.4 6.2 collective-permute-done.85
  475.6 7.3 collective-permute-done.87
  488.0 7.0 fusion.7
  515.7 11.9 %shard_map.214 = (bf16[1152,128]{1,0:T(8,128)(2,1)S(1)}, bf16[1152,128]{1,0:T(8,128)(2,1)S(1)}, bf16[1152,128]{1,0:T(8,128)(2,1)S(1)}) custom-call(s32[1152,1]{1,0:T(8,128)S(1)} %broadcast_in_dim.484.seg_q, s32[1,1152]{1,0:T(1,128)S(1)} %broadcast_in_dim.367.seg_k, bf16[1152,384]{1,0:T(8,128)(2,1)S(1)} %copy.261.query.keys.values, ...), custom_call_target="tpu_custom_call" | custom-call | flops 3397386240 | bytes 2949120 | tf_op jit(solution)/shard_map/pallas_call | solution.py:244
  572.0 7.6 collective-permute-done.102
  615.7 7.3 collective-permute-done.108
  636.6 6.0 collective-permute-done.115
  650.2 11.9 %shard_map.215 = (bf16[1152,128]{1,0:T(8,128)(2,1)S(1)}, bf16[1152,128]{1,0:T(8,128)(2,1)S(1)}, bf16[1152,128]{1,0:T(8,128)(2,1)S(1)}) custom-call(s32[1152,1]{1,0:T(8,128)S(1)} %broadcast_in_dim.484.seg_q, s32[1,1152]{1,0:T(1,128)S(1)} %broadcast_in_dim.367.seg_k, bf16[1152,384]{1,0:T(8,128)(2,1)S(1)} %copy-done.1, bf16[1152,384]{1,0:T(8,128)(2,1)S(1)} %copy-done.1, ...), custom_call_target="tpu_custom_call" | custom-call | flops 3397386240 | bytes 2949120 | tf_op jit(solution)/shard_map/pallas_call | solution.py:244
  679.8 6.6 collective-permute-done.119
  697.7 23.5 %collective-permute-done.123 = bf16[272,384]{1,0:T(8,128)(2,1)S(1)} collective-permute-done((bf16[272,384]{1,0:T(8,128)(2,1)S(1)}, bf16[272,384]{1,0:T(8,128)(2,1)S(1)}, u32[]{:S(2)}, u32[]{:S(2)}) %collective-permute-start.123) | collective-permute-done | bytes 208928 | tf_op jit(solution)/shard_map/ppermute | solution.py:39
  737.9 19.1 %collective-permute-start.132 = (bf16[2,32,384]{2,1,0:T(8,128)(2,1)S(1)}, bf16[2,32,384]{2,1,0:T(8,128)(2,1)S(1)}, u32[]{:S(2)}, u32[]{:S(2)}) collective-permute-start(bf16[2,32,384]{2,1,0:T(8,128)(2,1)S(1)} %pad_maximum_fusion.35), channel_id=1, source_target_pairs={{0,6},{1,7},{2,4},{3,5},{4,2},{5,3},{6,0},{7,1},{8,14},{9,15},{10,... | collective-permute-start | bytes 147464 | tf_op jit(solution)/shard_map/ppermute | solution.py:39
  778.5 8.3 %collective-permute-start.142 = (bf16[2,32,512]{2,1,0:T(8,128)(2,1)S(1)}, bf16[2,32,512]{2,1,0:T(8,128)(2,1)S(1)}, u32[]{:S(2)}, u32[]{:S(2)}) collective-permute-start(bf16[2,32,512]{2,1,0:T(8,128)(2,1)S(1)} %pad_maximum_fusion.26), channel_id=1, source_target_pairs={{0,6},{1,7},{2,4},{3,5},{4,2},{5,3},{6,0},{7,1},{8,14},{9,15},{10,... | collective-permute-start | bytes 196616 | tf_op jit(solution)/shard_map/ppermute | solution.py:39
  (1236 shorter events, 582.7 us)
Async XLA Ops:
  7.2 91.1 %all-gather.9.cloned.1.call-start = ((), (), s32[]{:S(2)}) async-start(), calls=%async_computation.6 | async-start | bytes 1392640 | tf_op jit(solution)/shard_map/all_gather | solution.py:370
  9.6 25.3 %collective-permute-start.15 = (bf16[4928]{0:T(1024)(128)(2,1)S(1)}, bf16[4928]{0:T(1024)(128)(2,1)S(1)}, u32[]{:S(2)}, u32[]{:S(2)}) collective-permute-start(bf16[4928]{0:T(1024)(128)(2,1)S(1)} %concatenate.174), channel_id=1, source_target_pairs={{0,2},{1,3},{2,0},{3,1},{4,6},{5,7},{6,4},{7,5},{8,10},{9,11},{10,... | collective-permute-start | bytes 29576 | tf_op jit(solution)/shard_map/ppermute | solution.py:39
  26.6 41.5 %collective-permute-start.32 = (bf16[4,32,1408]{2,1,0:T(8,128)(2,1)}, bf16[4,32,1408]{2,1,0:T(8,128)(2,1)}, u32[]{:S(2)}, u32[]{:S(2)}) collective-permute-start(bf16[4,32,1408]{2,1,0:T(8,128)(2,1)} %slice.929), channel_id=1, source_target_pairs={{0,1},{1,0},{2,3},{3,2},{4,5},{5,4},{6,7},{7,6},{8,9},{9,8},{10,11... | collective-permute-start | bytes 1081352 | tf_op jit(solution)/shard_map/ppermute | solution.py:39
  61.8 115.0 %all-gather.11.cloned.1.call-start = ((), (), s32[]{:S(2)}) async-start(), calls=%async_computation.7 | async-start | bytes 2621440 | tf_op jit(solution)/shard_map/all_gather | solution.py:370
  62.1 30.9 %collective-permute-start.2 = (bf16[144,1024]{1,0:T(8,128)(2,1)S(1)}, bf16[144,1024]{1,0:T(8,128)(2,1)S(1)}, u32[]{:S(2)}, u32[]{:S(2)}) collective-permute-start(bf16[144,1024]{1,0:T(8,128)(2,1)S(1)} %collective-permute-done), channel_id=1, source_target_pairs={{0,1},{1,0},{2,3},{3,2},{4,5},{5,4},{6,7},{7,6},{8,9},{9,8},{10,11... | collective-permute-start | bytes 884744 | tf_op jit(solution)/shard_map/ppermute | solution.py:39
  63.3 29.2 %collective-permute-start.3 = (bf16[144,1024]{1,0:T(8,128)(2,1)S(1)}, bf16[144,1024]{1,0:T(8,128)(2,1)S(1)}, u32[]{:S(2)}, u32[]{:S(2)}) collective-permute-start(bf16[144,1024]{1,0:T(8,128)(2,1)S(1)} %collective-permute-done), channel_id=1, source_target_pairs={{0,2},{1,3},{2,0},{3,1},{4,6},{5,7},{6,4},{7,5},{8,10},{9,11},{10,... | collective-permute-start | bytes 884744 | tf_op jit(solution)/shard_map/ppermute | solution.py:39
  65.7 26.8 %collective-permute-start.5 = (bf16[144,1024]{1,0:T(8,128)(2,1)S(1)}, bf16[144,1024]{1,0:T(8,128)(2,1)S(1)}, u32[]{:S(2)}, u32[]{:S(2)}) collective-permute-start(bf16[144,1024]{1,0:T(8,128)(2,1)S(1)} %collective-permute-done), channel_id=1, source_target_pairs={{0,4},{1,5},{2,6},{3,7},{4,0},{5,1},{6,2},{7,3},{8,12},{9,13},{10,... | collective-permute-start | bytes 884744 | tf_op jit(solution)/shard_map/ppermute | solution.py:39
  67.4 25.6 %collective-permute-start.7 = (bf16[144,1024]{1,0:T(8,128)(2,1)S(1)}, bf16[144,1024]{1,0:T(8,128)(2,1)S(1)}, u32[]{:S(2)}, u32[]{:S(2)}) collective-permute-start(bf16[144,1024]{1,0:T(8,128)(2,1)S(1)} %collective-permute-done), channel_id=1, source_target_pairs={{0,6},{1,7},{2,4},{3,5},{4,2},{5,3},{6,0},{7,1},{8,14},{9,15},{10,... | collective-permute-start | bytes 884744 | tf_op jit(solution)/shard_map/ppermute | solution.py:39
  89.3 35.6 %collective-permute-start.35 = (bf16[2,32,1408]{2,1,0:T(8,128)(2,1)}, bf16[2,32,1408]{2,1,0:T(8,128)(2,1)}, u32[]{:S(2)}, u32[]{:S(2)}) collective-permute-start(bf16[2,32,1408]{2,1,0:T(8,128)(2,1)} %pad_maximum_fusion.20), channel_id=1, source_target_pairs={{0,6},{1,7},{2,4},{3,5},{4,2},{5,3},{6,0},{7,1},{8,14},{9,15},{10,... | collective-permute-start | bytes 540680 | tf_op jit(solution)/shard_map/ppermute | solution.py:39
  130.9 102.3 %all-gather.13.cloned.1.call-start = ((), (), s32[]{:S(2)}) async-start(), calls=%async_computation.8 | async-start | bytes 1310720 | tf_op jit(solution)/shard_map/all_gather | solution.py:370
  201.9 83.6 %all-gather.15.cloned.1.call-start = ((), (), s32[]{:S(2)}) async-start(), calls=%async_computation.9 | async-start | bytes 2949120 | tf_op jit(solution)/shard_map/all_gather | solution.py:370
  232.7 324.7 %reduce-scatter.4.cloned.1.call-start = ((), (), s32[]{:S(2)}) async-start(), calls=%async_computation.3 | async-start | bytes 3112960 | tf_op jit(solution)/shard_map/reduce_scatter | solution.py:522
  329.5 67.5 %collective-permute-start.72 = (bf16[144,1024]{1,0:T(8,128)(2,1)}, bf16[144,1024]{1,0:T(8,128)(2,1)}, u32[]{:S(2)}, u32[]{:S(2)}) collective-permute-start(bf16[144,1024]{1,0:T(8,128)(2,1)} %bitcast.134), channel_id=1, source_target_pairs={{0,0},{1,8},{2,16},{3,24},{4,4},{5,12},{6,20},{7,28},{8,1},{9,9},{... | collective-permute-start | bytes 884744 | tf_op jit(solution)/shard_map/ppermute | solution.py:49
  412.5 28.8 %collective-permute-start.92 = (bf16[128,128]{1,0:T(8,128)(2,1)}, bf16[128,128]{1,0:T(8,128)(2,1)}, u32[]{:S(2)}, u32[]{:S(2)}) collective-permute-start(bf16[128,128]{1,0:T(8,128)(2,1)} %get-tuple-element.281), channel_id=1, source_target_pairs={{0,2},{1,3},{2,0},{3,1},{4,6},{5,7},{6,4},{7,5},{8,10},{9,11},{10,... | collective-permute-start | bytes 98312 | tf_op jit(solution)/shard_map/ppermute | solution.py:39
  412.5 28.8 %collective-permute-start.93 = (bf16[128,128]{1,0:T(8,128)(2,1)}, bf16[128,128]{1,0:T(8,128)(2,1)}, u32[]{:S(2)}, u32[]{:S(2)}) collective-permute-start(bf16[128,128]{1,0:T(8,128)(2,1)} %get-tuple-element.283), channel_id=1, source_target_pairs={{0,4},{1,5},{2,6},{3,7},{4,0},{5,1},{6,2},{7,3},{8,12},{9,13},{10,... | collective-permute-start | bytes 98312 | tf_op jit(solution)/shard_map/ppermute | solution.py:39
  488.0 161.9 %reduce-scatter.6.cloned.1.call-start = ((), (), s32[]{:S(2)}) async-start(), calls=%async_computation.4 | async-start | bytes 1044480 | tf_op jit(solution)/shard_map/reduce_scatter | solution.py:522
  506.1 84.4 %collective-permute-start.62 = (bf16[144,1024]{1,0:T(8,128)(2,1)}, bf16[144,1024]{1,0:T(8,128)(2,1)}, u32[]{:S(2)}, u32[]{:S(2)}) collective-permute-start(bf16[144,1024]{1,0:T(8,128)(2,1)} %copy-done.24), channel_id=1, source_target_pairs={{0,0},{1,8},{2,16},{3,24},{4,4},{5,12},{6,20},{7,28},{8,1},{9,9},{... | collective-permute-start | bytes 884744 | tf_op jit(solution)/shard_map/ppermute | solution.py:49
  514.4 50.3 %collective-permute-start.70 = (f32[2]{0:T(128)}, f32[2]{0:T(128)}, u32[]{:S(2)}, u32[]{:S(2)}) collective-permute-start(f32[2]{0:T(128)} %pad_maximum_fusion.41), channel_id=1, source_target_pairs={{0,8},{1,9},{2,10},{3,11},{4,12},{5,13},{6,14},{7,15},{8,0},{9,1},... | collective-permute-start | bytes 32 | tf_op jit(solution)/shard_map/ppermute | solution.py:39
  590.6 182.1 %reduce-scatter.8.cloned.1.call-start = ((), (), s32[]{:S(2)}) async-start(), calls=%async_computation.5 | async-start | bytes 2949120 | tf_op jit(solution)/shard_map/reduce_scatter | solution.py:522
  595.0 181.9 %collective-permute-start.134 = (bf16[32,1024]{1,0:T(8,128)(2,1)}, bf16[32,1024]{1,0:T(8,128)(2,1)}, u32[]{:S(2)}, u32[]{:S(2)}) collective-permute-start(bf16[32,1024]{1,0:T(8,128)(2,1)} %slice.1074), channel_id=1, source_target_pairs={{0,0},{8,1},{16,2},{24,3},{1,4},{9,5},{17,6},{25,7},{2,8},{10,9},{... | collective-permute-start | bytes 196616 | tf_op jit(solution)/shard_map/ppermute | solution.py:537
  688.4 32.8 %collective-permute-start.123 = (bf16[272,384]{1,0:T(8,128)(2,1)S(1)}, bf16[272,384]{1,0:T(8,128)(2,1)S(1)}, u32[]{:S(2)}, u32[]{:S(2)}) collective-permute-start(bf16[272,384]{1,0:T(8,128)(2,1)S(1)} %get-tuple-element.228), channel_id=1, source_target_pairs={{0,16},{1,17},{2,18},{3,19},{4,20},{5,21},{6,22},{7,23},{8,24},{9,... | collective-permute-start | bytes 626696 | tf_op jit(solution)/shard_map/ppermute | solution.py:39
  690.1 31.1 %collective-permute-start.124 = (bf16[272,384]{1,0:T(8,128)(2,1)S(1)}, bf16[272,384]{1,0:T(8,128)(2,1)}, u32[]{:S(2)}, u32[]{:S(2)}) collective-permute-start(bf16[272,384]{1,0:T(8,128)(2,1)S(1)} %get-tuple-element.227), channel_id=1, source_target_pairs={{0,24},{1,25},{2,26},{3,27},{4,28},{5,29},{6,30},{7,31},{8,16},{9,... | collective-permute-start | bytes 626696 | tf_op jit(solution)/shard_map/ppermute | solution.py:39
  694.7 42.3 %collective-permute-start.121 = (bf16[144,1024]{1,0:T(8,128)(2,1)S(1)}, bf16[144,1024]{1,0:T(8,128)(2,1)S(1)}, u32[]{:S(2)}, u32[]{:S(2)}) collective-permute-start(bf16[144,1024]{1,0:T(8,128)(2,1)S(1)} %fusion.58), channel_id=1, source_target_pairs={{0,0},{1,8},{2,16},{3,24},{4,4},{5,12},{6,20},{7,28},{8,1},{9,9},{... | collective-permute-start | bytes 884744 | tf_op jit(solution)/shard_map/ppermute | solution.py:49
  737.9 25.5 %collective-permute-start.132 = (bf16[2,32,384]{2,1,0:T(8,128)(2,1)S(1)}, bf16[2,32,384]{2,1,0:T(8,128)(2,1)S(1)}, u32[]{:S(2)}, u32[]{:S(2)}) collective-permute-start(bf16[2,32,384]{2,1,0:T(8,128)(2,1)S(1)} %pad_maximum_fusion.35), channel_id=1, source_target_pairs={{0,6},{1,7},{2,4},{3,5},{4,2},{5,3},{6,0},{7,1},{8,14},{9,15},{10,... | collective-permute-start | bytes 147464 | tf_op jit(solution)/shard_map/ppermute | solution.py:39
  (304 other events, 3122.9 us)
Sparse Core Ops, SparseCore 0:
  62.0 31.2 all-gather.8
  131.0 45.8 all-gather.10
  201.9 26.7 all-gather.12
  232.8 48.5 all-gather.14
  488.1 55.8 reduce-scatter.3
  590.7 25.2 reduce-scatter.5
  694.2 62.4 reduce-scatter.7

commit v2 on v0

--- a/solution.py
+++ b/solution.py
@@ -3,6 +3,8 @@
 import jax
 import jax.numpy as jnp
 from jax import lax
+from jax.experimental import pallas as pl
+from jax.experimental.pallas import tpu as pltpu
 from jax.sharding import PartitionSpec as P
 
 HEADS = 16
@@ -10,18 +12,81 @@
 NQ = 4
 NSD = 3
 
-
 NEG_FILL = -1e30
 SHARPNESS = 16.0
 HIGHEST = lax.Precision.HIGHEST
-
-
-def joined_2(value, axis, join):
-    pieces = jax.tree.map(lambda part: lax.all_gather(part, axis), value)
-    head = jax.tree.map(lambda part: part[0], pieces)
-    tail = jax.tree.map(lambda part: part[1:], pieces)
-    so_far, _ = lax.scan(lambda so_far, section: (join(so_far, section), None), head, tail)
-    return so_far
+BF = jnp.bfloat16
+F32 = jnp.float32
+
+def dot(left, right):
+    return jnp.dot(left, right, preferred_element_type=F32)
+
+
+def dot_lt(left, right):
+    return lax.dot_general(left, right, (((0,), (0,)), ((), ())), preferred_element_type=F32)
+
+
+def dot_rt(left, right):
+    return lax.dot_general(left, right, (((1,), (1,)), ((), ())), preferred_element_type=F32)
+
+
+PLANE = 8
+BOTH = ("seq", "row")
+
+
+def across(x, mask):
+    size = lax.axis_size("seq") * lax.axis_size("row")
+    return lax.ppermute(x, BOTH, [(d, d ^ mask) for d in range(size)])
+
+
+def turned(x):
+    size = lax.axis_size("seq") * lax.axis_size("row")
+    rows = lax.axis_size("row")
+    pairs = []
+    for d in range(size):
+        o, i, r = d // PLANE, d % PLANE // rows, d % rows
+        pairs.append((d, r * PLANE + i * rows + o))
+    return lax.ppermute(x, BOTH, pairs)
+
+
+def plane_gather(x):
+    blocks = [x, None, across(x, 2), None, across(x, 4), None, across(x, 6), None]
+    for k in range(0, PLANE, 2):
+        blocks[k + 1] = across(blocks[k], 1)
+    return blocks
+
+
+def plane_scatter(even, odd, beside=None, first=False):
+    core = across(odd, 1)
+    if first:
+        core, beside = tie(core, beside)
+    parts = core_add(even, core)
+    got = [across(parts[j], 2 * j) for j in (1, 2, 3)]
+    if beside is not None:
+        got, beside = tie(got, beside)
+    return [parts[0]] + got, beside
+
+
+def plane_sum(parts):
+    parts = parts.astype(BF)
+    core = across(parts[1::2], 1).astype(F32) + parts[0::2].astype(F32)
+    sent = core[1:].astype(BF)
+    return core[0] + sum(across(sent[k - 1], 2 * k).astype(F32) for k in (1, 2, 3))
+
+
+def plane_exchange(x, relative):
+    x = pick(x, relative)
+    core = across(x[1::2], 1)
+    got = tie(*[across(jnp.stack([x[2 * k], core[k]]), 2 * k) for k in (1, 2, 3)])
+    return pick(jnp.concatenate([x[:1], core[:1], *got]), relative)
+
+
+def pick(x, index, axis=0):
+    return x.at[(slice(None),) * axis + (index,)].get(mode="promise_in_bounds")
+
+
+def tie(*values):
+    return lax.optimization_barrier(values)
 
 
 def token_info(positions, lengths, kinds):
@@ -38,6 +103,885 @@
     doc_num = jnp.sum(jnp.where(onehot, doc_count[None, :], nothing), axis=1)
     offset = positions - seg_start
     return (segment, offset, is_query, query_num * QLEN + offset, doc_num)
+
+
+def rope_angles(offset, head_dim):
+    half = head_dim // 2
+    inverse = jnp.exp(jnp.arange(half, dtype=F32) * (-2.0 * math.log(10000.0) / head_dim))
+    angle = offset.astype(F32)[:, None] * inverse[None, :]
+    return jnp.cos(angle), jnp.sin(angle)
+
+
+def layer_norm(rows, gain, shift):
+    center = rows - jnp.mean(rows, axis=-1, keepdims=True)
+    variance = jnp.mean(center * center, axis=-1, keepdims=True)
+    return center * lax.rsqrt(variance + 1e-05) * gain + shift
+
+
+def unit_rows(rows):
+    return rows * lax.rsqrt(jnp.sum(rows * rows, axis=-1, keepdims=True) + 1e-06)
+
+
+def exact_gelu(values):
+    return jax.nn.gelu(values, approximate=False)
+
+
+def head_masks(width):
+    lane = lax.broadcasted_iota(jnp.int32, (1, width), 1)
+    first_qk = (lane % (width // 2)) < (width // 4)
+    first_v = lane < (width // 2)
+    return first_qk, first_v
+
+
+BIG, SMALL = 62, 16
+
+IN_VMEM = pl.BlockSpec(memory_space=pltpu.VMEM)
+IN_HBM = pl.BlockSpec(memory_space=pltpu.HBM)
+
+
+def near(x):
+    return (x, "near")
+
+
+def held(x):
+    return (x, "held")
+
+
+def raw(x):
+    return (x, "raw")
+
+
+def call(kernel, ins, outs, scratch, flops, limit=BIG):
+    arrays = [a for a, _ in ins]
+    kept = [i for i, (_, kind) in enumerate(ins) if kind == "held"]
+    left = [i for i, out in enumerate(outs) if len(out) == 3]
+    pieces = [1 if outs[i][2] is True else outs[i][2] for i in left]
+    moved = sum(a.size * a.dtype.itemsize for a in arrays)
+    moved += sum(math.prod(out[0]) * jnp.dtype(out[1]).itemsize for out in outs)
+
+    def wrapped(*refs):
+        in_refs = list(refs[: len(ins)])
+        out_refs = list(refs[len(ins) : len(ins) + len(outs)])
+        rest = refs[len(ins) + len(outs) :]
+        own, rest = rest[: len(scratch)], rest[len(scratch) :]
+        in_bufs, out_bufs = rest[: len(kept)], rest[len(kept) : len(kept) + len(left)]
+        sems = rest[len(kept) + len(left)] if kept or left else None
+        pending = {}
+        for k, i in enumerate(kept):
+            pending[i] = pltpu.make_async_copy(in_refs[i], in_bufs[k], sems.at[k])
+            pending[i].start()
+
+        def getter(i, buf):
+            def get():
+                if i in pending:
+                    pending.pop(i).wait()
+                return buf
+
+            return get
+
+        for k, i in enumerate(kept):
+            in_refs[i] = getter(i, in_bufs[k])
+        leaving = {}
+
+        def flusher(i, k, target):
+            def flush(j=0):
+                buf = out_bufs[k]
+                if pieces[k] > 1:
+                    buf, target_j = buf.at[j], target.at[j]
+                else:
+                    target_j = target
+                leaving[i, j] = pltpu.make_async_copy(buf, target_j, sems.at[len(kept) + sum(pieces[:k]) + j])
+                leaving[i, j].start()
+
+            return flush
+
+        for k, i in enumerate(left):
+            out_refs[i] = (out_bufs[k], flusher(i, k, out_refs[i]))
+        kernel(in_refs, out_refs, own)
+        assert not pending and len(leaving) == sum(pieces)
+        for copy in leaving.values():
+            copy.wait()
+
+    buffers = [pltpu.VMEM(*item) if isinstance(item, tuple) else item for item in scratch]
+    buffers += [pltpu.VMEM(arrays[i].shape, arrays[i].dtype) for i in kept]
+    buffers += [pltpu.VMEM(*outs[i][:2]) for i in left]
+    if kept or left:
+        buffers.append(pltpu.SemaphoreType.DMA((len(kept) + sum(pieces),)))
+    return pl.pallas_call(
+        wrapped,
+        in_specs=[IN_VMEM if kind == "near" else IN_HBM for _, kind in ins],
+        out_specs=tuple(IN_HBM if len(out) == 3 else IN_VMEM for out in outs),
+        out_shape=tuple(jax.ShapeDtypeStruct(out[0], out[1]) for out in outs),
+        scratch_shapes=buffers,
+        compiler_params=pltpu.CompilerParams(vmem_limit_bytes=limit * 1024 * 1024),
+        cost_estimate=pl.CostEstimate(flops=flops, bytes_accessed=moved, transcendentals=0),
+    )(*arrays)
+
+
+def core_add(even, got):
+    count, T, D = even.shape
+
+    def kernel(ins, outs, _):
+        for j in range(count):
+            outs[j][...] = (ins[0][j].astype(F32) + ins[1][j].astype(F32)).astype(outs[j].dtype)
+
+    outs = [((T, D), F32)] + [((T, D), BF)] * (count - 1)
+    return call(kernel, [near(even), near(got)], outs, [], even.size, SMALL)
+
+
+def add_norm(parts, params, bias_at, gain_at, shift_at):
+    T, D = parts[0].shape
+
+    def kernel(ins, outs, _):
+        params = ins[-1]
+        (total, leave), normed, low = outs
+        rows = params[:, bias_at : bias_at + D]
+        for ref in ins[:-1]:
+            rows = rows + ref[...].astype(F32)
+        total[...] = rows
+        leave()
+        result = layer_norm(rows, params[:, gain_at : gain_at + D], params[:, shift_at : shift_at + D])
+        normed[...] = result
+        low[...] = result.astype(BF)
+
+    outs = [((T, D), F32, True), ((T, D), F32), ((T, D), BF)]
+    return call(kernel, [near(item) for item in (*parts, params)], outs, [], 10 * T * D, SMALL)
+
+
+def norm_back(parts, rows, params, gain_at):
+    T, D = rows.shape
+
+    def kernel(ins, outs, _):
+        rows, params = ins[-2:]
+        wide_out, low_out, sums = outs
+        grad = ins[0][...].astype(F32)
+        for ref in ins[1:-2]:
+            grad = grad + ref[...].astype(F32)
+        rows = rows()[...]
+        center = rows - jnp.mean(rows, axis=-1, keepdims=True)
+        inverse = lax.rsqrt(jnp.mean(center * center, axis=-1, keepdims=True) + 1e-05)
+        unit = center * inverse
+        sums[:, :D] = jnp.sum(grad * unit, axis=0, keepdims=True)
+        sums[:, D : 2 * D] = jnp.sum(grad, axis=0, keepdims=True)
+        grad = grad * params[:, gain_at : gain_at + D]
+        along = jnp.mean(grad * unit, axis=-1, keepdims=True)
+        grad = inverse * (grad - jnp.mean(grad, axis=-1, keepdims=True) - unit * along)
+        wide_out[...] = grad
+        low = grad.astype(BF)
+        low_out[...] = low
+        sums[:, 2 * D :] = jnp.sum(low.astype(F32), axis=0, keepdims=True)
+
+    outs = [((T, D), F32), ((T, D), BF), ((1, 3 * D), F32)]
+    return call(kernel, [near(item) for item in parts] + [held(rows), near(params)], outs, [], 20 * T * D, SMALL)
+
+
+def roll_halves(x):
+    return pltpu.roll(x, x.shape[1] // 2, 1)
+
+
+def load_attn(full, w_in, w_out):
+    far = full.shape[0]
+    D, cols = w_in.shape
+    rows, wide = D // far, w_out.shape[0]
+    part = wide // far
+    for o in range(far):
+        w_in[o * rows : (o + 1) * rows] = full[o, :rows, :cols]
+        for j in range(rows // part):
+            w_out[o * part : (o + 1) * part, j * wide : (j + 1) * wide] = full[o, j * part : (j + 1) * part, cols:]
+
+
+def load_ffn(full, w_up, w_down):
+    far = full.shape[0]
+    D, H = w_up.shape
+    up, down = D // far, H // far
+    for o in range(far):
+        w_up[o * up : o * up + up // 2] = full[o, : up // 2, :H]
+        w_up[o * up + up // 2 : (o + 1) * up] = full[o, : up // 2, H:]
+        w_down[o * down : (o + 1) * down] = full[o, up // 2 : up // 2 + down]
+
+
+def rotary(table, rows, half):
+    cos, sin = table[rows, :half], table[rows, half : 2 * half]
+    return jnp.concatenate([cos, cos, cos, cos], axis=1), jnp.concatenate([-sin, -sin, sin, sin], axis=1)
+
+
+def attn_forward(blocks, full, bias, bias_at, table, seg_row, half, scale):
+    n = len(blocks)
+    T, D = blocks[0].shape
+    wide = 4 * half
+    N = n * T
+    step = 4
+    across_block = N
+
+    def kernel(ins, outs, scratch):
+        full, table, bias, seg_row = ins[n:]
+        (qkv, leave_qkv), (context, leave_context), (logs, leave_logs), even, odd = outs
+        w_in, w_out, x, values_t, context_t, x_sems = scratch
+        copies = block_copies(ins[:n], x, x_sems)
+        start_all(copies)
+        load_attn(full(), w_in, w_out)
+        table = table()
+        for k in range(0, n, step):
+            wait_all(copies[k : k + step])
+            rows = slice(k * T, (k + step) * T)
+            mixed = dot(x[rows], w_in[...]) + bias[:, bias_at : bias_at + 3 * wide]
+            cos, sin = rotary(table, rows, half)
+            for t, factor in ((0, scale), (1, 1.0)):
+                part = mixed[:, t * wide : (t + 1) * wide]
+                part = (part * cos + roll_halves(part) * sin).astype(BF)
+                qkv[rows, t * wide : (t + 1) * wide] = part * jnp.asarray(factor, BF)
+            qkv[rows, 2 * wide :] = mixed[:, 2 * wide :].astype(BF)
+        leave_qkv()
+        values_t[...] = qkv[:, 2 * wide :].T
+        first_qk, _ = head_masks(wide)
+        zero = jnp.zeros((), BF)
+
+        def part(c, carry):
+            at = pl.ds(pl.multiple_of(c * across_block, 128), across_block)
+            allowed = table[:, 2 * half : 2 * half + 1] == seg_row[:, at]
+            for head in range(2):
+                mine = first_qk if head == 0 else jnp.logical_not(first_qk)
+                query = jnp.where(mine, qkv[at, :wide], zero)
+                scores = jnp.where(allowed, dot_rt(qkv[:, wide : 2 * wide], query), NEG_FILL)
+                top = jnp.max(scores, axis=0, keepdims=True)
+                weights = jnp.exp(scores - top)
+                total = jnp.sum(weights, axis=0, keepdims=True)
+                heads = slice(head * 2 * half, (head + 1) * 2 * half)
+                context_t[heads, at] = dot(values_t[heads, :], weights.astype(BF)) * (1.0 / total)
+                logs[head : head + 1, at] = top + jnp.log(total)
+            return carry
+
+        lax.fori_loop(0, N // across_block, part, 0)
+        leave_logs()
+        context[...] = context_t[...].T.astype(BF)
+        leave_context()
+        for k in range(0, n, step):
+            put_blocks(dot(context[k * T : (k + step) * T], w_out[...]).astype(BF), k, (even, odd), T)
+
+    outs = [((N, 3 * wide), BF, True), ((N, wide), BF, True), ((2, N), F32, True)]
+    outs += [((n // 2, T, D), BF, n // 2), ((n // 2, T, D), BF, n // 2)]
+    flops = 2 * N * D * 4 * wide + 8 * N * N * wide
+    sems = pltpu.SemaphoreType.DMA
+    scratch = [((D, 3 * wide), BF), ((wide, D), BF), ((N, D), BF), ((wide, N), BF), ((wide, N), F32), sems((n,))]
+    ins = [raw(item) for item in blocks] + [held(full), held(table), near(bias), near(seg_row)]
+    return call(kernel, ins, outs, scratch, flops)
+
+
+def lanes_of(count):
+    return max(w for w in (384, 256, 128) if count % w == 0)
+
+
+def fetch_ffn(full, w_up, w_down, sems):
+    far = full.shape[0]
+    D, H = w_up.shape
+    up, down = D // far, H // far
+    first, second = [], []
+    for o in range(far):
+        for part in range(2):
+            first.append(
+                pltpu.make_async_copy(
+                    full.at[o, pl.ds(0, up // 2), pl.ds(part * H, H)],
+                    w_up.at[pl.ds(o * up + part * (up // 2), up // 2)],
+                    sems.at[3 * o + part],
+                )
+            )
+        second.append(
+            pltpu.make_async_copy(
+                full.at[o, pl.ds(up // 2, down)], w_down.at[pl.ds(o * down, down)], sems.at[3 * o + 2]
+            )
+        )
+    return first, second
+
+
+def start_all(copies):
+    for copy in copies:
+        copy.start()
+
+
+def wait_all(copies):
+    for copy in copies:
+        copy.wait()
+
+
+def block_copies(blocks, whole, sems):
+    T = blocks[0].shape[0]
+    return [pltpu.make_async_copy(block, whole.at[pl.ds(k * T, T)], sems.at[k]) for k, block in enumerate(blocks)]
+
+
+def ffn_forward(blocks, full, bias, bias_at, H):
+    n = len(blocks)
+    T, D = blocks[0].shape
+    step = 4
+
+    def kernel(ins, outs, scratch):
+        full, bias = ins[n:]
+        (act, leave_act), (slope, leave_slope), even, odd = outs
+        w_up, w_down, x, w_sems, x_sems = scratch
+        first, second = fetch_ffn(full, w_up, w_down, w_sems)
+        copies = block_copies(ins[:n], x, x_sems)
+        start_all(first)
+        start_all(copies)
+        start_all(second)
+        wait_all(first)
+        for k in range(0, n, step):
+            wait_all(copies[k : k + step])
+            rows = slice(k * T, (k + step) * T)
+            pre = dot(x[rows], w_up[...]) + bias[:, bias_at : bias_at + H]
+            below = 0.5 * (1.0 + lax.erf(pre * math.sqrt(0.5)))
+            result = (pre * below).astype(BF)
+            act[rows] = result
+            slope[rows] = (below + pre * (math.sqrt(0.5 / math.pi) * jnp.exp(-0.5 * pre * pre))).astype(BF)
+            if k == 0:
+                wait_all(second)
+            back = dot(act[rows], w_down[...]).astype(BF)
+            put_blocks(back, k, (even, odd), T)
+        leave_act()
+        leave_slope()
+
+    outs = [((n * T, H), BF, True), ((n * T, H), BF, True), ((n // 2, T, D), BF, n // 2), ((n // 2, T, D), BF, n // 2)]
+    ins = [raw(item) for item in blocks] + [raw(full), near(bias)]
+    sems = pltpu.SemaphoreType.DMA
+    scratch = [((D, H), BF), ((H, D), BF), ((n * T, D), BF), sems((3 * full.shape[0],)), sems((n,))]
+    return call(kernel, ins, outs, scratch, 4 * n * T * D * H)
+
+
+def put_blocks(rows, first, halves, T):
+    for i in range(rows.shape[0] // T):
+        out, leave = halves[(first + i) % 2]
+        out[(first + i) // 2] = rows[i * T : (i + 1) * T]
+        leave((first + i) // 2)
+
+
+def ffn_back(blocks, full, slope):
+    n = len(blocks)
+    T, D = blocks[0].shape
+    H = slope.shape[1]
+    step = 4
+
+    def kernel(ins, outs, scratch):
+        full, slope = ins[n:]
+        grad_pre, bias_grad, even, odd = outs
+        w_up, w_down, x, w_sems, x_sems = scratch
+        first, second = fetch_ffn(full, w_up, w_down, w_sems)
+        copies = block_copies(ins[:n], x, x_sems)
+        start_all(second)
+        start_all(copies)
+        start_all(first)
+        wait_all(second)
+        total = jnp.zeros((1, H), F32)
+        for k in range(0, n, step):
+            wait_all(copies[k : k + step])
+            rows = slice(k * T, (k + step) * T)
+            grad = (dot_rt(x[rows], w_down[...]) * slope()[rows].astype(F32)).astype(BF)
+            grad_pre[rows] = grad
+            total = total + jnp.sum(grad.astype(F32), axis=0, keepdims=True)
+            if k == 0:
+                wait_all(first)
+            put_blocks(dot_rt(grad_pre[rows], w_up[...]).astype(BF), k, (even, odd), T)
+        bias_grad[...] = total
+
+    outs = [((n * T, H), BF), ((1, H), F32), ((n // 2, T, D), BF, n // 2), ((n // 2, T, D), BF, n // 2)]
+    ins = [raw(item) for item in blocks] + [raw(full), held(slope)]
+    sems = pltpu.SemaphoreType.DMA
+    scratch = [((D, H), BF), ((H, D), BF), ((n * T, D), BF), sems((3 * full.shape[0],)), sems((n,))]
+    return call(kernel, ins, outs, scratch, 4 * n * T * D * H)
+
+
+def ffn_weights(normed, grads, act, grad_pre, far, extra):
+    n = len(normed)
+    T, D = normed[0].shape
+    N = n * T
+    H = act.shape[1]
+    up, down = D // far, H // far
+    more = [] if extra is None else [near(extra)]
+    count = up // 2 + down + (0 if extra is None else extra.shape[1])
+
+    def kernel(ins, outs, scratch):
+        act, grad_pre = ins[2 * n : 2 * n + 2]
+        left, right, left_sems, right_sems = scratch
+        out = outs[0]
+        copies = block_copies(ins[:n], left, left_sems)
+        later = block_copies(ins[n : 2 * n], right, right_sems)
+        start_all(copies)
+        start_all(later)
+        wait_all(copies)
+        for o in range(far):
+            block = dot_lt(left[:, o * up : (o + 1) * up], grad_pre[...]).astype(BF)
+            out[o, : up // 2, :H] = block[: up // 2]
+            out[o, : up // 2, H:] = block[up // 2 :]
+        wait_all(later)
+        act = act()
+        for o in range(far):
+            block = dot_lt(act[:, o * down : (o + 1) * down], right[...]).astype(BF)
+            out[o, up // 2 : up // 2 + down] = block
+            if more:
+                out[o, up // 2 + down :] = ins[2 * n + 2][o]
+
+    sems = pltpu.SemaphoreType.DMA
+    scratch = [((N, D), BF), ((N, D), BF), sems((n,)), sems((n,))]
+    ins = [raw(item) for item in (*normed, *grads)] + [held(act), near(grad_pre)] + more
+    return call(kernel, ins, [((far, count, D), BF)], scratch, 4 * N * D * H)[0]
+
+
+def attn_back(blocks, full, qkv, context, logs, table, seg_row, half, scale):
+    n = len(blocks)
+    T, D = blocks[0].shape
+    wide = 4 * half
+    N = n * T
+    step = 4
+    across_block = lanes_of(N)
+
+    def kernel(ins, outs, scratch):
+        full, table, qkv, context, logs, seg_row = ins[n:]
+        mixed, bias_grad, even, odd = outs
+        w_in, w_out, x, grad, delta, cos, sin, acc_k, acc_v, x_sems = scratch
+        copies = block_copies(ins[:n], x, x_sems)
+        start_all(copies)
+        load_attn(full(), w_in, w_out)
+        for k in range(0, n, step):
+            wait_all(copies[k : k + step])
+            rows = slice(k * T, (k + step) * T)
+            grad[rows] = dot_rt(x[rows], w_out[...]).astype(BF)
+        table = table()
+        cos[...], sin[...] = rotary(table, slice(None), half)
+        acc_k[...] = jnp.zeros_like(acc_k)
+        acc_v[...] = jnp.zeros_like(acc_v)
+        qkv, logs = qkv(), logs()
+        product = (grad[...].astype(F32) * context()[...].astype(F32)).T
+        delta[0:1] = jnp.sum(product[: 2 * half], axis=0, keepdims=True)
+        delta[1:2] = jnp.sum(product[2 * half :], axis=0, keepdims=True)
+        first_qk, first_v = head_masks(wide)
+        zero = jnp.zeros((), BF)
+
+        def part(c, carry):
+            at = pl.ds(pl.multiple_of(c * across_block, 128), across_block)
+            allowed = table[:, 2 * half : 2 * half + 1] == seg_row[:, at]
+            grad_query = []
+            for head in range(2):
+                mine = first_qk if head == 0 else jnp.logical_not(first_qk)
+                mine_v = first_v if head == 0 else jnp.logical_not(first_v)
+                query = jnp.where(mine, qkv[at, :wide], zero)
+                grad_h = jnp.where(mine_v, grad[at, :], zero)
+                scores = dot_rt(qkv[:, wide : 2 * wide], query) - logs[head : head + 1, at]
+                probs = jnp.exp(jnp.where(allowed, scores, NEG_FILL))
+                grad_probs = dot_rt(qkv[:, 2 * wide :], grad_h)
+                grad_scores = (probs * (grad_probs - delta[head : head + 1, at])).astype(BF)
+                acc_k[...] += dot(grad_scores, query)
+                acc_v[...] += dot(probs.astype(BF), grad_h)
+                grad_query.append(dot_lt(grad_scores, qkv[:, wide : 2 * wide]))
+            result = jnp.where(first_qk, grad_query[0], grad_query[1]) * scale
+            mixed[at, :wide] = (result * cos[at, :] - roll_halves(result) * sin[at, :]).astype(BF)
+            return carry
+
+        lax.fori_loop(0, N // across_block, part, 0)
+        total = acc_k[...]
+        mixed[:, wide : 2 * wide] = (total * cos[...] - roll_halves(total) * sin[...]).astype(BF)
+        mixed[:, 2 * wide :] = acc_v[...].astype(BF)
+        sums = jnp.zeros((1, 3 * wide), F32)
+        for k in range(0, n, step):
+            rows = slice(k * T, (k + step) * T)
+            sums = sums + jnp.sum(mixed[rows].astype(F32), axis=0, keepdims=True)
+            put_blocks(dot_rt(mixed[rows], w_in[...]).astype(BF), k, (even, odd), T)
+        bias_grad[...] = sums
+
+    outs = [((N, 3 * wide), BF), ((1, 3 * wide), F32), ((n // 2, T, D), BF, n // 2), ((n // 2, T, D), BF, n // 2)]
+    scratch = [((D, 3 * wide), BF), ((wide, D), BF), ((N, D), BF), ((N, wide), BF), ((2, N), F32)]
+    scratch += [((N, wide), F32)] * 4 + [pltpu.SemaphoreType.DMA((n,))]
+    flops = 2 * N * D * 4 * wide + 20 * N * N * wide
+    ins = [raw(item) for item in blocks] + [held(item) for item in (full, table, qkv, context, logs)] + [near(seg_row)]
+    return call(kernel, ins, outs, scratch, flops)
+
+
+def attn_weights(inputs, grads, context, mixed, bias_grad, far, relative):
+    n = len(inputs)
+    T, D = inputs[0].shape
+    N = n * T
+    wide = context.shape[1]
+    rows = D // far
+    part = wide // far
+    size = lax.axis_size("row")
+
+    def kernel(ins, outs, scratch):
+        context, mixed, bias_grad = ins[2 * n :]
+        left, right, left_sems, right_sems = scratch
+        here = (lax.axis_index("seq") * size + lax.axis_index("row")) // PLANE
+        copies = block_copies(ins[:n], left, left_sems)
+        later = block_copies(ins[n : 2 * n], right, right_sems)
+        start_all(copies)
+        start_all(later)
+        wait_all(copies)
+        for k in range(far):
+            if relative:
+                lanes = pl.ds(pl.multiple_of((here ^ k) * rows, 128), rows)
+                outs[k][:rows, : 3 * wide] = dot_lt(left[:, lanes], mixed[...]).astype(BF)
+            else:
+                outs[0][k, :rows, : 3 * wide] = dot_lt(left[:, k * rows : (k + 1) * rows], mixed[...]).astype(BF)
+        wait_all(later)
+        whole = dot_lt(context()[...], right[...]).astype(BF)
+        extra = jnp.broadcast_to(bias_grad[...], (16, 3 * wide)).astype(BF)
+        if relative:
+            right[:wide, :D] = whole
+        for k in range(far):
+            out = outs[k] if relative else outs[0].at[k]
+            if relative:
+                block = right[pl.ds(pl.multiple_of((here ^ k) * part, 16), part), :]
+            else:
+                block = whole[k * part : (k + 1) * part]
+            for j in range(rows // part):
+                out[j * part : (j + 1) * part, 3 * wide :] = block[:, j * wide : (j + 1) * wide]
+            out[rows:, : 3 * wide] = extra
+            out[rows:, 3 * wide :] = jnp.zeros((16, wide), BF)
+
+    sems = pltpu.SemaphoreType.DMA
+    scratch = [((N, D), BF), ((N, D), BF), sems((n,)), sems((n,))]
+    ins = [raw(item) for item in (*inputs, *grads)] + [held(context), near(mixed), near(bias_grad)]
+    if relative:
+        outs = [((rows + 16, 4 * wide), BF)] * far
+    else:
+        outs = [((far, rows + 16, 4 * wide), BF)]
+    return call(kernel, ins, outs, scratch, 8 * N * D * wide)
+
+
+def body(
+    tokens,
+    attn_in,
+    attn_out,
+    ffn_up,
+    ffn_down,
+    norm_gains,
+    biases,
+    colbert,
+    log_scale,
+    cotangent,
+    seg_lengths,
+    seg_kinds,
+    pairing,
+):
+    S = lax.axis_size("seq")
+    R = lax.axis_size("row")
+    O = S * R // PLANE
+    place = lax.axis_index("seq") * R + lax.axis_index("row")
+    plane, far = place % PLANE, place // PLANE
+    relative = jnp.bitwise_xor(plane, jnp.arange(PLANE, dtype=jnp.int32))
+    T = tokens.shape[1]
+    D = tokens.shape[2]
+    N = PLANE * T
+    L = attn_in.shape[0]
+    head_dim = D // HEADS
+    half = head_dim // 2
+    scale = head_dim ** (-0.5)
+    wide = 2 * head_dim
+    in_cols = 3 * wide
+    in_rows = attn_in.shape[1]
+    rows_in = PLANE * in_rows
+    FF = ffn_up.shape[2]
+    up_cols = FF // (S * R)
+    hidden_cols = O * up_cols
+    gain_part = norm_gains.shape[1]
+    bias_part = biases.shape[1]
+    part = gain_part + bias_part
+    along_z = [[o * (S // O) + i for o in range(O)] for i in range(S // O)]
+    is_mine = jnp.arange(PLANE, dtype=jnp.int32) == plane
+
+    def padded_rows(vector, width=D):
+        rows = -(-vector.shape[0] // (16 * width)) * 16
+        return jnp.pad(vector, (0, rows * width - vector.shape[0])).reshape(rows, width)
+
+    def pack_columns(w):
+        lead = w.shape[:-1]
+        n = len(lead)
+        qk = w[..., : 2 * D].reshape(*lead, 2, PLANE, 2, 2, half)
+        qk = qk.transpose((n + 1,) + tuple(range(n)) + (n, n + 3, n + 2, n + 4)).reshape(PLANE, *lead, 2 * wide)
+        v = w[..., 2 * D :].reshape(*lead, PLANE, wide)
+        v = v.transpose((n,) + tuple(range(n)) + (n + 1,))
+        return jnp.concatenate([qk, v], axis=-1)
+
+    def unpack_columns(w):
+        rows = w.shape[1]
+        qk = w[:, :, : 2 * wide].reshape(PLANE, rows, 2, 2, 2, half)
+        qk = qk.transpose(1, 2, 0, 4, 3, 5).reshape(rows, 2 * D)
+        v = w[:, :, 2 * wide :].transpose(1, 0, 2).reshape(rows, D)
+        return jnp.concatenate([qk, v], axis=1)
+
+    def pack_hidden(w):
+        rows = w.shape[0]
+        return w.reshape(rows, O, PLANE, up_cols).transpose(2, 0, 1, 3).reshape(PLANE, rows, hidden_cols)
+
+    def unpack_hidden(w):
+        rows = w.shape[1]
+        return w.reshape(PLANE, rows, O, up_cols).transpose(1, 2, 0, 3).reshape(rows, FF)
+
+    def fold(w):
+        n = w.shape[-2] // 2
+        return jnp.concatenate([w[..., :n, :], w[..., n:, :]], axis=-1)
+
+    def unfold(w):
+        n = w.shape[-1] // 2
+        return jnp.concatenate([w[..., :n], w[..., n:]], axis=-2)
+
+    to_group = [(b, (b % O) * PLANE + b // O) for b in range(O * PLANE)]
+    from_group = [(d, b) for b, d in to_group]
+    small = jnp.concatenate([norm_gains.reshape(-1), biases.reshape(-1), colbert.reshape(-1)])
+    small = jnp.broadcast_to(padded_rows(small, in_cols), (PLANE, *padded_rows(small, in_cols).shape))
+    first_in = plane_exchange(jnp.concatenate([pack_columns(attn_in[0]), small], axis=1), relative)
+    first_in, small = first_in[:, :in_rows].reshape(rows_in, in_cols), first_in[:, in_rows:].reshape(PLANE, -1)
+    shard_out = lax.ppermute(attn_out, BOTH, to_group)
+    table = turned(jnp.concatenate([seg_lengths[0], seg_kinds[0], pairing[0]]))
+    seg_count = seg_lengths.shape[1]
+    lengths, kinds = table[:seg_count], table[seg_count : 2 * seg_count]
+    pairs_of = table[2 * seg_count :]
+    hidden_low = turned(tokens[0])
+    cot = turned(cotangent[0])
+
+    def attn_block(layer, shard):
+        out = shard_out[layer].reshape(in_rows, PLANE, wide).transpose(1, 0, 2).reshape(rows_in, wide)
+        return jnp.concatenate([shard, out], axis=1)
+
+    def gather_far(x):
+        return lax.all_gather(x, "seq", axis=0, axis_index_groups=along_z)
+
+    own = attn_block(0, first_in)
+    full_attn = [gather_far(own)]
+
+    count_small = L * part
+    col_plane = small[:, count_small : count_small + colbert.size].reshape(-1)
+    params = small[None, :, :count_small]
+    step = 1
+    while step < O:
+        other = across(params, PLANE * step)
+        low_side = (far & step) == 0
+        params = jnp.concatenate([jnp.where(low_side, params, other), jnp.where(low_side, other, params)], axis=0)
+        step *= 2
+    params = params.reshape(O * PLANE, count_small).astype(F32)
+    gains_all = params[:, : L * gain_part].reshape(O * PLANE, L, gain_part).transpose(1, 0, 2).reshape(L, 2 * D)
+    bias_all = params[:, L * gain_part :].reshape(O * PLANE, L, bias_part).transpose(1, 0, 2).reshape(L, -1)
+    in_biases = pick(pack_columns(bias_all[:, : 3 * D]), plane, axis=0).reshape(1, L * in_cols)
+    up_biases = pick(pack_hidden(bias_all[:, 4 * D : 4 * D + FF]), plane, axis=0).reshape(1, L * hidden_cols)
+    rest_at = 4 * D + FF
+    params = jnp.concatenate([gains_all, bias_all[:, 3 * D : 4 * D], bias_all[:, rest_at:]], axis=1).reshape(1, -1)
+    GAIN_ONE, GAIN_TWO, BIAS_OUT, BIAS_DOWN, SHIFT_ONE, SHIFT_TWO = range(6)
+
+    def at(layer, which):
+        return (layer * 6 + which) * D
+
+    rest = jnp.concatenate(
+        [pack_hidden(ffn_up[0])]
+        + [piece for layer in range(1, L) for piece in (pack_columns(attn_in[layer]), pack_hidden(ffn_up[layer]))],
+        axis=-1,
+    )
+    rest = plane_exchange(rest, relative).reshape(rows_in, -1)
+    full_ffn = []
+    start = 0
+    for layer in range(L):
+        if layer > 0:
+            full_attn.append(gather_far(attn_block(layer, rest[:, start : start + in_cols])))
+            start += in_cols
+        own = [fold(rest[:, start : start + hidden_cols]), ffn_down[layer]]
+        start += hidden_cols
+        if layer == L - 1:
+            own.append(padded_rows(col_plane))
+        full_ffn.append(gather_far(jnp.concatenate(own, axis=0)))
+    w_col = full_ffn[L - 1][:, rows_in // 2 + up_cols :].reshape(O, -1)[:, : col_plane.size]
+    w_col = w_col.reshape(D, colbert.shape[1])
+
+    block_at = (relative % R) * (PLANE // R) + relative // R
+    positions = (block_at[:, None] * T + jnp.arange(T, dtype=jnp.int32)[None, :]).reshape(N)
+    held_segment, held_offset = token_info(positions, lengths, kinds)[:2]
+    cos, sin = rope_angles(held_offset, head_dim)
+    seg_row = held_segment.astype(F32)[None, :]
+    table = jnp.concatenate([cos, sin, jnp.broadcast_to(seg_row.T, (N, wide - 2 * half))], axis=1)
+
+    hidden = hidden_low
+    records = []
+    for layer in range(L):
+        x_all = plane_gather(hidden_low)
+        if layer == 0:
+            x_all, cot = tie(x_all, cot)
+        qkv, context, logs, even, odd = attn_forward(
+            x_all, full_attn[layer], in_biases, layer * in_cols, table, seg_row, half, scale
+        )
+        terms, _ = plane_scatter(even, odd)
+        first, normed, normed_low = add_norm(
+            [hidden] + terms, params, at(layer, BIAS_OUT), at(layer, GAIN_ONE), at(layer, SHIFT_ONE)
+        )
+        normed_all = plane_gather(normed_low)
+        act, slope, even, odd = ffn_forward(
+            normed_all, full_ffn[layer], up_biases, layer * hidden_cols, hidden_cols
+        )
+        terms, _ = plane_scatter(even, odd)
+        second, hidden, hidden_low = add_norm(
+            [normed] + terms, params, at(layer, BIAS_DOWN), at(layer, GAIN_TWO), at(layer, SHIFT_TWO)
+        )
+        records.append((x_all, qkv, context, logs, first, normed_all, act, slope, second))
+    hidden_out = turned(hidden_low)
+
+    full_width = w_col.shape[1]
+    part_widths = (full_width, full_width * 3 // 4, full_width // 2)
+    query_total = NQ * QLEN
+    doc_total = NSD + 1
+    col = dot(hidden_low, w_col)
+    in_order = jnp.arange(PLANE, dtype=jnp.int32)
+    in_order = jnp.bitwise_xor((in_order % (PLANE // R)) * R + in_order // (PLANE // R), plane)
+    col_row = pick(jnp.stack(plane_gather(col.astype(BF))), in_order, axis=0).reshape(N, full_width).astype(F32)
+    own_at = block_at[0] * T
+    row_positions = jnp.arange(N, dtype=jnp.int32)
+    segment, offset, is_query, query_slot, doc_num = token_info(row_positions, lengths, kinds)
+    slots = jnp.arange(query_total, dtype=jnp.int32)[:, None]
+    selector = (is_query == 1)[None, :] & (query_slot[None, :] == slots)
+    selector_low = selector.astype(BF)
+    own_selector = lax.dynamic_slice(selector.astype(F32), (0, own_at), (query_total, T))
+    embeds = [unit_rows(col_row[:, :width]).astype(BF) for width in part_widths]
+    query_emb = [dot(selector_low, embed).astype(BF) for embed in embeds]
+    powers = jnp.exp(SHARPNESS * jnp.stack([dot_rt(query_emb[m], embeds[m]) for m in range(3)]))
+    doc_code = jnp.where(is_query == 0, doc_num, -1)[None, None, :]
+    totals = jnp.stack([jnp.sum(jnp.where(doc_code == d, powers, 0.0), axis=2) for d in range(doc_total)], axis=2)
+    soft = jnp.log(totals) / SHARPNESS
+    pair_sum = jnp.sum(soft.reshape(3, NQ, QLEN, doc_total), axis=2)
+    inverse_temp = jnp.exp(log_scale[0])
+    logits = pair_sum * inverse_temp / QLEN
+    positive = pairs_of[None, :, None] == jnp.arange(doc_total, dtype=jnp.int32)[None, None, :]
+    losses = jax.nn.logsumexp(logits, axis=-1) - jnp.sum(jnp.where(positive, logits, 0.0), axis=-1)
+    loss_weight = 1.0 / (3 * NQ * R)
+    grad_logits = loss_weight * (jax.nn.softmax(logits, axis=-1) - positive.astype(F32))
+    loss_terms = jnp.stack([jnp.sum(losses) * loss_weight, jnp.sum(grad_logits * logits)])
+    grad_pairs = grad_logits * inverse_temp / QLEN
+    grad_soft = jnp.broadcast_to(grad_pairs[:, :, None, :], (3, NQ, QLEN, doc_total)).reshape(
+        3, query_total, doc_total
+    )
+    ratio = grad_soft / totals
+    weight = sum(jnp.where(doc_code == d, ratio[:, :, d : d + 1], 0.0) for d in range(doc_total))
+    grad_sims = (powers * weight).astype(BF)
+    own_sims = lax.dynamic_slice(grad_sims, (0, 0, own_at), (3, query_total, T))
+    grad_col = jnp.zeros((T, full_width), F32)
+    for m in range(3):
+        width = part_widths[m]
+        grad_query = dot(grad_sims[m], embeds[m])
+        grad_embed = dot_lt(own_sims[m], query_emb[m]) + lax.dot_general(
+            own_selector, grad_query, (((0,), (0,)), ((), ())), precision=HIGHEST, preferred_element_type=F32
+        )
+        pull_unit = jax.vjp(unit_rows, col[:, :width])[1]
+        grad_col = grad_col + jnp.pad(pull_unit(grad_embed)[0], ((0, 0), (0, full_width - width)))
+    grad_col_low = grad_col.astype(BF)
+    col_parts = dot_lt(hidden_low, grad_col_low).reshape(O, PLANE, in_rows, full_width).transpose(1, 0, 2, 3)
+    col_parts = plane_sum(pick(col_parts.reshape(PLANE, O * in_rows, full_width), relative, axis=0))
+    col_rows = jax.vmap(padded_rows)(col_parts.reshape(O, in_rows * full_width)).astype(BF)
+    grad_parts = [cot, dot_rt(grad_col_low, w_col)]
+
+    def scatter_far(whole):
+        whole = whole.reshape(-1, whole.shape[-1])
+        return lax.psum_scatter(whole, "seq", scatter_dimension=0, tiled=True, axis_index_groups=along_z)
+
+    outs = [[None] * L for _ in range(6)]
+
+    def up_share(shares):
+        return unfold(shares[: rows_in // 2]).reshape(PLANE, in_rows, hidden_cols)
+
+    def in_share(shares):
+        return shares[:rows_in, :in_cols].reshape(PLANE, in_rows, in_cols)
+
+    def finish_out(layer, shares):
+        share_out = shares[:rows_in, in_cols:].astype(BF).reshape(PLANE, in_rows, wide)
+        share_out = share_out.transpose(1, 0, 2).reshape(in_rows, D)
+        outs[1][layer] = lax.ppermute(share_out, BOTH, from_group).astype(F32)
+
+    def bias_in_entries(rows):
+        natural = jnp.pad(unpack_columns(rows[:, None].astype(F32))[0], (0, O * PLANE * bias_part - 3 * D))
+        return pick(natural.reshape(O * PLANE, bias_part), place)
+
+    def as_rows(x, width):
+        return jax.vmap(lambda row: padded_rows(row, width))(x)
+
+    shares_ffn, shares_attn = [None] * L, [None] * L
+    vectors = [None] * L
+    for layer in reversed(range(L)):
+        x_all, qkv, context, logs, first, normed_all, act, slope, second = records[layer]
+        grad_second, grad_ffo, sums_two = norm_back(grad_parts, second, params, at(layer, GAIN_TWO))
+        ffo_all = plane_gather(grad_ffo)
+        if layer == L - 1:
+            ffo_all, hidden_out = tie(ffo_all, hidden_out)
+        grad_pre, grad_bias_up, even, odd = ffn_back(ffo_all, full_ffn[layer], slope)
+        blocks = ffn_weights(normed_all, ffo_all, act, grad_pre, O, col_rows if layer == L - 1 else None)
+        terms, blocks = plane_scatter(even, odd, blocks)
+        shares_ffn[layer] = scatter_far(blocks)
+        grad_first, grad_branch, sums_one = norm_back([grad_second] + terms, first, params, at(layer, GAIN_ONE))
+        branch_all = plane_gather(grad_branch)
+        if layer < L - 1:
+            branch_all, shares_attn[layer + 1] = tie(branch_all, shares_attn[layer + 1])
+        grad_mixed, grad_bias_in, even, odd = attn_back(
+            branch_all, full_attn[layer], qkv, context, logs, table, seg_row, half, scale
+        )
+
+        gain_two, shift_two, down, gain_one, shift_one, out = [
+            sums[0, k * D : (k + 1) * D] for sums in (sums_two, sums_one) for k in range(3)
+        ]
+        own_up = unpack_hidden(is_mine[:, None, None].astype(F32) * grad_bias_up[None])[0]
+        gains = jnp.concatenate([gain_one, gain_two]).reshape(O, PLANE, gain_part)
+        bias = jnp.concatenate([jnp.zeros((3 * D,), F32), out, own_up, down, shift_one, shift_two])
+        vectors[layer] = jnp.concatenate([gains, bias.reshape(O, PLANE, bias_part)], axis=2)
+
+        blocks = attn_weights(x_all, branch_all, context, grad_mixed, grad_bias_in, O, layer == 0)
+        terms, blocks = plane_scatter(even, odd, blocks, layer == 0)
+        terms, shares_ffn[layer] = tie(terms, shares_ffn[layer])
+        if layer > 0:
+            shares_attn[layer] = scatter_far(blocks[0])
+            grad_parts = [grad_first] + terms
+
+    got = [across(blocks[step], PLANE * step) for step in range(1, O)]
+    entries = jnp.concatenate(vectors, axis=2).transpose(1, 0, 2).reshape(PLANE, O * L * part).astype(BF)
+    pieces = [in_share(shares_attn[layer]) for layer in range(1, L)] + [up_share(item) for item in shares_ffn]
+    pieces = jnp.concatenate(pieces, axis=2)
+    got, terms, entries, pieces = tie(got, terms, entries, pieces)
+    grad_tokens = turned((grad_first + sum(item.astype(F32) for item in terms)).astype(BF))
+    shares_attn[0] = (blocks[0].astype(F32) + sum(item.astype(F32) for item in got)).astype(BF)
+    pieces = jnp.concatenate([in_share(shares_attn[0]), pieces], axis=2)
+    bias_rows = [jnp.broadcast_to(item[None, rows_in, :in_cols], (PLANE, in_cols)) for item in shares_attn]
+    more = as_rows(jnp.concatenate([entries] + bias_rows, axis=1), pieces.shape[2])
+    back = plane_exchange(jnp.concatenate([pieces, more], axis=1), relative)
+    more = back[:, in_rows:].reshape(PLANE, -1)
+    entries = jnp.sum(more[:, : O * L * part].astype(F32), axis=0).reshape(O, L * part)
+    entries = jnp.concatenate([entries, jnp.broadcast_to(loss_terms[None], (O, 2))], axis=1)
+    mine = pick(entries, far)
+    for step in range(1, O):
+        mine = mine + across(pick(entries, far ^ step), PLANE * step)
+    start = 0
+    for layer in range(L):
+        outs[0][layer] = unpack_columns(back[:, :in_rows, start : start + in_cols])
+        start += in_cols
+    for layer in range(L):
+        outs[2][layer] = unpack_hidden(back[:, :in_rows, start : start + hidden_cols])
+        start += hidden_cols
+        at_row = rows_in // 2
+        outs[3][layer] = shares_ffn[layer][at_row : at_row + up_cols]
+        finish_out(layer, shares_attn[layer])
+        at_row = O * L * part + layer * in_cols
+        bias_in = bias_in_entries(more[:, at_row : at_row + in_cols])
+        outs[4][layer] = mine[layer * part : layer * part + gain_part]
+        outs[5][layer] = mine[layer * part + gain_part : (layer + 1) * part] + bias_in
+    col_share = shares_ffn[L - 1][rows_in // 2 + up_cols :].reshape(-1)[: in_rows * full_width]
+    col_share = col_share.reshape(in_rows, full_width).astype(F32)
+    loss_terms = mine[L * part :]
+    stacked = [jnp.stack(items).astype(F32) for items in outs]
+    return (
+        hidden_out[None],
+        loss_terms[:1],
+        grad_tokens.astype(F32)[None],
+        stacked[0],
+        stacked[1],
+        stacked[2],
+        stacked[3],
+        stacked[4],
+        stacked[5],
+        col_share,
+        loss_terms[1:],
+    )
+
+
+def joined_2(value, axis, join):
+    pieces = jax.tree.map(lambda part: lax.all_gather(part, axis), value)
+    head = jax.tree.map(lambda part: part[0], pieces)
+    tail = jax.tree.map(lambda part: part[1:], pieces)
+    so_far, _ = lax.scan(lambda so_far, section: (join(so_far, section), None), head, tail)
+    return so_far
 
 
 def rope_tables(offset, head_dim):
@@ -66,20 +1010,6 @@
     return turned.reshape(length, flat.shape[1])
 
 
-def layer_norm(rows, gain, shift):
-    center = rows - jnp.mean(rows, axis=-1, keepdims=True)
-    variance = jnp.mean(center * center, axis=-1, keepdims=True)
-    return center * lax.rsqrt(variance + 1e-05) * gain + shift
-
-
-def unit_rows(rows):
-    return rows * lax.rsqrt(jnp.sum(rows * rows, axis=-1, keepdims=True) + 1e-06)
-
-
-def exact_gelu(values):
-    return jax.nn.gelu(values, approximate=False)
-
-
 def block_for(count):
     blocks = count
     while blocks > 1024 and blocks % 2 == 0:
@@ -102,7 +1032,7 @@
     return jnp.einsum("to,io->ti", left, right, preferred_element_type=jnp.float32)
 
 
-def body(
+def body_wide(
     tokens,
     attn_in,
     attn_out,
@@ -583,8 +1513,9 @@
         P("row", None),
         P("row", None),
     )
+    planes = mesh.shape["row"] == 4 and mesh.shape["seq"] * 4 == 4 * PLANE and HEADS == 2 * PLANE
     return jax.shard_map(
-        body,
+        body if planes else body_wide,
         mesh=mesh,
         in_specs=placed,
         out_specs=(

time: 3040 us -> 626 us (0.21)
  waiting for transfers between devices: 2340 us -> 245 us
  matrix products: 243 us -> 5.36 us
  blocking collectives: 156 us -> 0 us
  Pallas kernels: 0 us -> 130 us
  starting transfers between devices: 1.82 us -> 123 us
  local copies, waits for them, and re-layouts: 177 us -> 68.3 us
  other arithmetic: 94.3 us -> 28.2 us
    reduce_scatter x9 -> x3, waiting for transfers between devices: 1250 us -> 0.01 us  [scatter_far(): lax.psum_scatter(whole, 'seq', scatter_dimension=0, tiled=True, axis_inde...]
    all_gather x12 -> x4, waiting for transfers between devices: 522 us -> 0.01 us  [gather_far(): return lax.all_gather(x, 'seq', axis=0, axis_index_groups=along_z)]
    unnamed x29 -> x7, waiting for transfers between devices: 438 us -> 0.12 us
    ppermute x0 -> x127, waiting for transfers between devices: none -> 245 us  [the longest x119 245 us: across(): return lax.ppermute(x, BOTH, [(d, d ^ mask) for d in range(size)])]
    dot_general x69 -> x18, matrix products: 237 us -> 5.36 us  [the longest x7 1.86 us: dot(): return jnp.dot(left, right, preferred_element_type=F32)]
    psum x2 -> x0, waiting for transfers between devices: 136 us -> none  [the longest x1 68.3 us: body(): lax.psum(jnp.dot(grad_sims[0], embeds[0], preferred_element_type=jnp.floa...]
    pallas_call x0 -> x28, Pallas kernels: none -> 130 us  [call(): pl.pallas_call(wrapped, in_specs=[IN_VMEM if kind == 'near' else IN_HBM f...]
    ppermute x0 -> x127, starting transfers between devices: none -> 122 us  [the longest x119 112 us: across(): return lax.ppermute(x, BOTH, [(d, d ^ mask) for d in range(size)])]
  transfers between devices with their start and end apart: 26 -> 134, of which waited for: 26 -> 65; matrix products, arithmetic and copies ran while one was open for 9% -> 9% of each run, Pallas kernels for 0% -> 18%
where the time goes in v2:
time: 626 us; the launch traced here: 618 us
  waiting for transfers between devices  245 us (39%)
  Pallas kernels  130 us (21%)
  starting transfers between devices  123 us (20%)
  local copies, waits for them, and re-layouts  68.3 us (11%)
  other arithmetic  28.2 us (5%)
  between operations  18.9 us (3%)
    ppermute x119, waiting for transfers between devices, across(): return lax.ppermute(x, BOTH, [(d, d ^ mask) for d in range(size)])  245 us
    pallas_call x28, Pallas kernels, call(): pl.pallas_call(wrapped, in_specs=[IN_VMEM if kind == 'near' else IN_HBM f...  130 us
    ppermute x119, starting transfers between devices, across(): return lax.ppermute(x, BOTH, [(d, d ^ mask) for d in range(size)])  112 us
    unnamed x311, local copies, waits for them, and re-layouts  32.3 us
  transfers between devices with their start and end apart: 134, of which 65 were waited for; matrix products, arithmetic and copies ran while one was open for 9% of the time, Pallas kernels for 18%

profile of v2, /device:TPU:0, one launch (start us, length us, event | category | flops | bytes accessed | tf_op | source)
XLA Modules:
  0.0 618.3 jit_solution(18366181594430136238)
XLA Ops:
  25.7 11.2 %collective-permute-start.13 = (bf16[2,48,384]{2,1,0:T(8,128)(2,1)S(1)}, bf16[2,48,384]{2,1,0:T(8,128)(2,1)S(1)}, u32[]{:S(2)}, u32[]{:S(2)}) collective-permute-start(bf16[2,48,384]{2,1,0:T(8,128)(2,1)S(1)} %pad_maximum_fusion.19), channel_id=1, source_target_pairs={{0,6},{1,7},{2,4},{3,5},{4,2},{5,3},{6,0},{7,1},{8,14},{9,15},{10,... | collective-permute-start | bytes 221192 | tf_op jit(solution)/shard_map/ppermute | solution.py:39
  82.8 7.7 %collective-permute-done.4.refs_4_ = bf16[144,1024]{1,0:T(8,128)(2,1)S(1)} collective-permute-done((bf16[144,1024]{1,0:T(8,128)(2,1)S(1)}, bf16[144,1024]{1,0:T(8,128)(2,1)S(1)}, u32[]{:S(2)}, u32[]{:S(2)}) %collective-permute-start.4) | collective-permute-done | bytes 294944 | tf_op jit(solution)/shard_map/ppermute | solution.py:39
  93.8 10.3 %shard_map.212 = (bf16[1152,384]{1,0:T(8,128)(2,1)}, bf16[1152,128]{1,0:T(8,128)(2,1)}, f32[2,1152]{1,0:T(2,128)}, bf16[4,144,1024]{2,1,0:T(8,128)(2,1)}, bf16[4,144,1024]{2,1,0:T(8,128)(2,1)}) custom-call(bf16[144,1024]{1,0:T(8,128)(2,1)} %copy-done, bf16[144,1024]{1,0:T(8,128)(2,1)} %copy-done.61, bf16[144,1024]{1,0:T(8,128)(2,1)} %copy-done.58, ...), custom_call_target="tpu_custom_call" | custom-call | flops 2566914048 | bytes 7553536 | tf_op jit(solution)/shard_map/pallas_call | solution.py:210
  144.2 8.1 %shard_map.215 = (bf16[1152,512]{1,0:T(8,128)(2,1)}, bf16[1152,512]{1,0:T(8,128)(2,1)}, bf16[4,144,1024]{2,1,0:T(8,128)(2,1)}, bf16[4,144,1024]{2,1,0:T(8,128)(2,1)}) custom-call(bf16[144,1024]{1,0:T(8,128)(2,1)} %copy-done.22, bf16[144,1024]{1,0:T(8,128)(2,1)} %copy-done.68, bf16[144,1024]{1,0:T(8,128)(2,1)} %copy-done.65, bf16[144,1024]{1,0:T(8,128)(2,1)} %copy-done.69, ...), custom_call_target="tpu_custom_call" | custom-call | flops 2415919104 | bytes 9179136 | tf_op jit(solution)/shard_map/pallas_call | solution.py:210
  176.9 6.5 %collective-permute-done.37.refs_2_ = bf16[144,1024]{1,0:T(8,128)(2,1)S(1)} collective-permute-done((bf16[144,1024]{1,0:T(8,128)(2,1)S(1)}, bf16[144,1024]{1,0:T(8,128)(2,1)S(1)}, u32[]{:S(2)}, u32[]{:S(2)}) %collective-permute-start.37) | collective-permute-done | bytes 294944 | tf_op jit(solution)/shard_map/ppermute | solution.py:39
  191.9 10.3 %shard_map.218 = (bf16[1152,384]{1,0:T(8,128)(2,1)}, bf16[1152,128]{1,0:T(8,128)(2,1)}, f32[2,1152]{1,0:T(2,128)}, bf16[4,144,1024]{2,1,0:T(8,128)(2,1)}, bf16[4,144,1024]{2,1,0:T(8,128)(2,1)}) custom-call(bf16[144,1024]{1,0:T(8,128)(2,1)} %copy-done.23, bf16[144,1024]{1,0:T(8,128)(2,1)} %copy-done.75, bf16[144,1024]{1,0:T(8,128)(2,1)} %copy-done.72, ...), custom_call_target="tpu_custom_call" | custom-call | flops 2566914048 | bytes 7553536 | tf_op jit(solution)/shard_map/pallas_call | solution.py:210
  227.7 6.5 %collective-permute-done.48.refs_2_ = bf16[144,1024]{1,0:T(8,128)(2,1)S(1)} collective-permute-done((bf16[144,1024]{1,0:T(8,128)(2,1)S(1)}, bf16[144,1024]{1,0:T(8,128)(2,1)S(1)}, u32[]{:S(2)}, u32[]{:S(2)}) %collective-permute-start.48) | collective-permute-done | bytes 294944 | tf_op jit(solution)/shard_map/ppermute | solution.py:39
  242.5 8.1 %shard_map.221 = (bf16[1152,512]{1,0:T(8,128)(2,1)}, bf16[1152,512]{1,0:T(8,128)(2,1)}, bf16[4,144,1024]{2,1,0:T(8,128)(2,1)}, bf16[4,144,1024]{2,1,0:T(8,128)(2,1)}) custom-call(bf16[144,1024]{1,0:T(8,128)(2,1)} %copy-done.24, bf16[144,1024]{1,0:T(8,128)(2,1)} %copy-done.82, bf16[144,1024]{1,0:T(8,128)(2,1)} %copy-done.79, bf16[144,1024]{1,0:T(8,128)(2,1)} %copy-done.83, ...), custom_call_target="tpu_custom_call" | custom-call | flops 2415919104 | bytes 9441280 | tf_op jit(solution)/shard_map/pallas_call | solution.py:210
  306.8 6.7 %collective-permute-done.68.refs_4_.refs_12_ = bf16[144,1024]{1,0:T(8,128)(2,1)S(1)} collective-permute-done((bf16[144,1024]{1,0:T(8,128)(2,1)S(1)}, bf16[144,1024]{1,0:T(8,128)(2,1)S(1)}, u32[]{:S(2)}, u32[]{:S(2)}) %collective-permute-start.68) | collective-permute-done | bytes 294944 | tf_op jit(solution)/shard_map/ppermute | solution.py:39
  320.0 7.2 %shard_map.225 = (bf16[1152,512]{1,0:T(8,128)(2,1)}, f32[1,512]{1,0:T(1,128)}, bf16[4,144,1024]{2,1,0:T(8,128)(2,1)}, bf16[4,144,1024]{2,1,0:T(8,128)(2,1)}) custom-call(bf16[144,1024]{1,0:T(8,128)(2,1)} %copy-done.25, bf16[144,1024]{1,0:T(8,128)(2,1)} %copy-done.89, bf16[144,1024]{1,0:T(8,128)(2,1)} %copy-done.86, bf16[144,1024]{1,0:T(8,128)(2,1)} %copy-done.90, ...), custom_call_target="tpu_custom_call" | custom-call | flops 2415919104 | bytes 9439232 | tf_op jit(solution)/shard_map/pallas_call | solution.py:210
  340.3 8.5 %shard_map.227 = bf16[4,272,1024]{2,1,0:T(8,128)(2,1)} custom-call(bf16[144,1024]{1,0:T(8,128)(2,1)} %copy-done.24, bf16[144,1024]{1,0:T(8,128)(2,1)} %copy-done.82, bf16[144,1024]{1,0:T(8,128)(2,1)} %copy-done.79, bf16[144,1024]{1,0:T(8,128)(2,1)} %copy-done.83, bf16[144,1024]{1,0:T(8,128)(2,1)} %copy-done.80, bf16[144,1024]{1,0:T(8,128)(2,1)} %copy-done.84, ...), custom_call_target="tpu_custom_call" | custom-call | flops 2415919104 | bytes 9437184 | tf_op jit(solution)/shard_map/pallas_call | solution.py:210
  359.3 6.5 %collective-permute-done.82.refs_2_.refs_10_ = bf16[144,1024]{1,0:T(8,128)(2,1)S(1)} collective-permute-done((bf16[144,1024]{1,0:T(8,128)(2,1)S(1)}, bf16[144,1024]{1,0:T(8,128)(2,1)S(1)}, u32[]{:S(2)}, u32[]{:S(2)}) %collective-permute-start.82) | collective-permute-done | bytes 294944 | tf_op jit(solution)/shard_map/ppermute | solution.py:39
  372.8 17.1 %shard_map.229 = (bf16[1152,384]{1,0:T(8,128)(2,1)}, f32[1,384]{1,0:T(1,128)}, bf16[4,144,1024]{2,1,0:T(8,128)(2,1)}, bf16[4,144,1024]{2,1,0:T(8,128)(2,1)}) custom-call(bf16[144,1024]{1,0:T(8,128)(2,1)} %copy-done.28, bf16[144,1024]{1,0:T(8,128)(2,1)} %copy-done.108, bf16[144,1024]{1,0:T(8,128)(2,1)} %copy-done.105, bf16[144,1024]{1,0:T(8,128)(2,1)} %copy-done.110, ...), custom_call_target="tpu_custom_call" | custom-call | flops 4605345792 | bytes 8436736 | tf_op jit(solution)/shard_map/pallas_call | solution.py:210
  398.8 6.7 %shard_map.231 = bf16[4,272,512]{2,1,0:T(8,128)(2,1)} custom-call(bf16[144,1024]{1,0:T(8,128)(2,1)} %copy-done.23, bf16[144,1024]{1,0:T(8,128)(2,1)} %copy-done.75, bf16[144,1024]{1,0:T(8,128)(2,1)} %copy-done.72, bf16[144,1024]{1,0:T(8,128)(2,1)} %copy-done.76, bf16[144,1024]{1,0:T(8,128)(2,1)} %copy-done.73, bf16[144,1024]{1,0:T(8,128)(2,1)} %copy-done.77, ...), custom_call_target="tpu_custom_call" | custom-call | flops 1207959552 | bytes 7013888 | tf_op jit(solution)/shard_map/pallas_call | solution.py:210
  405.5 6.6 %collective-permute-done.90.refs_3_ = bf16[144,1024]{1,0:T(8,128)(2,1)} collective-permute-done((bf16[144,1024]{1,0:T(8,128)(2,1)}, bf16[144,1024]{1,0:T(8,128)(2,1)}, u32[]{:S(2)}, u32[]{:S(2)}) %collective-permute-start.90) | collective-permute-done | bytes 294944 | tf_op jit(solution)/shard_map/ppermute | solution.py:39
  432.6 7.2 %shard_map.233 = (bf16[1152,512]{1,0:T(8,128)(2,1)}, f32[1,512]{1,0:T(1,128)}, bf16[4,144,1024]{2,1,0:T(8,128)(2,1)}, bf16[4,144,1024]{2,1,0:T(8,128)(2,1)}) custom-call(bf16[144,1024]{1,0:T(8,128)(2,1)} %copy-done.27, bf16[144,1024]{1,0:T(8,128)(2,1)} %copy-done.109, bf16[144,1024]{1,0:T(8,128)(2,1)} %copy-done.102, bf16[144,1024]{1,0:T(8,128)(2,1)} %copy-done.111, ...), custom_call_target="tpu_custom_call" | custom-call | flops 2415919104 | bytes 9177088 | tf_op jit(solution)/shard_map/pallas_call | solution.py:210
  448.6 8.4 %shard_map.235 = bf16[4,256,1024]{2,1,0:T(8,128)(2,1)} custom-call(bf16[144,1024]{1,0:T(8,128)(2,1)} %copy-done.22, bf16[144,1024]{1,0:T(8,128)(2,1)} %copy-done.68, bf16[144,1024]{1,0:T(8,128)(2,1)} %copy-done.65, bf16[144,1024]{1,0:T(8,128)(2,1)} %copy-done.69, bf16[144,1024]{1,0:T(8,128)(2,1)} %copy-done.66, bf16[144,1024]{1,0:T(8,128)(2,1)} %copy-done.70, ...), custom_call_target="tpu_custom_call" | custom-call | flops 2415919104 | bytes 9175040 | tf_op jit(solution)/shard_map/pallas_call | solution.py:210
  486.4 17.1 %shard_map.237 = (bf16[1152,384]{1,0:T(8,128)(2,1)}, f32[1,384]{1,0:T(1,128)}, bf16[4,144,1024]{2,1,0:T(8,128)(2,1)}, bf16[4,144,1024]{2,1,0:T(8,128)(2,1)}) custom-call(bf16[144,1024]{1,0:T(8,128)(2,1)} %copy-done.26, bf16[144,1024]{1,0:T(8,128)(2,1)} %copy-done.98, bf16[144,1024]{1,0:T(8,128)(2,1)} %copy-done.91, bf16[144,1024]{1,0:T(8,128)(2,1)} %copy-done.99, ...), custom_call_target="tpu_custom_call" | custom-call | flops 4605345792 | bytes 8436736 | tf_op jit(solution)/shard_map/pallas_call | solution.py:210
  504.7 6.8 %shard_map.238 = (bf16[272,512]{1,0:T(8,128)(2,1)}, bf16[272,512]{1,0:T(8,128)(2,1)}, bf16[272,512]{1,0:T(8,128)(2,1)}, bf16[272,512]{1,0:T(8,128)(2,1)}) custom-call(bf16[144,1024]{1,0:T(8,128)(2,1)} %copy-done, bf16[144,1024]{1,0:T(8,128)(2,1)} %copy-done.61, bf16[144,1024]{1,0:T(8,128)(2,1)} %copy-done.58, bf16[144,1024]{1,0:T(8,128)(2,1)} %copy-done.62, ...), custom_call_target="tpu_custom_call" | custom-call | flops 1207959552 | bytes 7013888 | tf_op jit(solution)/shard_map/pallas_call | solution.py:210
  523.0 7.0 %collective-permute-done.112 = bf16[144,1024]{1,0:T(8,128)(2,1)} collective-permute-done((bf16[144,1024]{1,0:T(8,128)(2,1)S(1)}, bf16[144,1024]{1,0:T(8,128)(2,1)}, u32[]{:S(2)}, u32[]{:S(2)}) %collective-permute-start.112) | collective-permute-done | bytes 294944 | tf_op jit(solution)/shard_map/ppermute | solution.py:39
  536.0 9.0 %collective-permute-done.114 = bf16[272,512]{1,0:T(8,128)(2,1)} collective-permute-done((bf16[272,512]{1,0:T(8,128)(2,1)}, bf16[272,512]{1,0:T(8,128)(2,1)}, u32[]{:S(2)}, u32[]{:S(2)}) %collective-permute-start.114) | collective-permute-done | bytes 278560 | tf_op jit(solution)/shard_map/ppermute | solution.py:39
  545.0 8.3 %collective-permute-done.116 = bf16[272,512]{1,0:T(8,128)(2,1)} collective-permute-done((bf16[272,512]{1,0:T(8,128)(2,1)}, bf16[272,512]{1,0:T(8,128)(2,1)}, u32[]{:S(2)}, u32[]{:S(2)}) %collective-permute-start.116) | collective-permute-done | bytes 278560 | tf_op jit(solution)/shard_map/ppermute | solution.py:39
  562.5 12.5 %collective-permute-start.120 = (bf16[2,48,1792]{2,1,0:T(8,128)(2,1)S(1)}, bf16[2,48,1792]{2,1,0:T(8,128)(2,1)S(1)}, u32[]{:S(2)}, u32[]{:S(2)}) collective-permute-start(bf16[2,48,1792]{2,1,0:T(8,128)(2,1)S(1)} %pad_maximum_fusion.8), channel_id=1, source_target_pairs={{0,6},{1,7},{2,4},{3,5},{4,2},{5,3},{6,0},{7,1},{8,14},{9,15},{10,... | collective-permute-start | bytes 1032200 | tf_op jit(solution)/shard_map/ppermute | solution.py:39
  577.3 11.3 %collective-permute-done.120 = bf16[2,48,1792]{2,1,0:T(8,128)(2,1)S(1)} collective-permute-done((bf16[2,48,1792]{2,1,0:T(8,128)(2,1)S(1)}, bf16[2,48,1792]{2,1,0:T(8,128)(2,1)S(1)}, u32[]{:S(2)}, u32[]{:S(2)}) %collective-permute-start.120) | collective-permute-done | bytes 344096 | tf_op jit(solution)/shard_map/ppermute | solution.py:39
  (875 shorter events, 383.9 us)
Async XLA Ops:
  7.2 85.9 %all-gather.9.cloned.1.call-start = ((), (), s32[]{:S(2)}) async-start(), calls=%async_computation.6 | async-start | bytes 1310720 | tf_op jit(solution)/shard_map/all_gather | solution.py:741
  11.6 36.3 %collective-permute-start.28 = (bf16[4,32,1408]{2,1,0:T(8,128)(2,1)}, bf16[4,32,1408]{2,1,0:T(8,128)(2,1)S(1)}, u32[]{:S(2)}, u32[]{:S(2)}) collective-permute-start(bf16[4,32,1408]{2,1,0:T(8,128)(2,1)} %slice.449), channel_id=1, source_target_pairs={{0,1},{1,0},{2,3},{3,2},{4,5},{5,4},{6,7},{7,6},{8,9},{9,8},{10,11... | collective-permute-start | bytes 1081352 | tf_op jit(solution)/shard_map/ppermute | solution.py:39
  15.0 22.9 %collective-permute-start.14 = (bf16[2,32,1024]{2,1,0:T(8,128)(2,1)}, bf16[2,32,1024]{2,1,0:T(8,128)(2,1)}, u32[]{:S(2)}, u32[]{:S(2)}) collective-permute-start(bf16[2,32,1024]{2,1,0:T(8,128)(2,1)} %param.15), channel_id=1, source_target_pairs={{0,0},{1,8},{2,16},{3,24},{4,1},{5,9},{6,17},{7,25},{8,2},{9,10},{... | collective-permute-start | bytes 393224 | tf_op jit(solution)/shard_map/ppermute | solution.py:728
  17.9 53.7 %collective-permute-start = (bf16[144,1024]{1,0:T(8,128)(2,1)}, bf16[144,1024]{1,0:T(8,128)(2,1)S(1)}, u32[]{:S(2)}, u32[]{:S(2)}) collective-permute-start(bf16[144,1024]{1,0:T(8,128)(2,1)} %bitcast), channel_id=1, source_target_pairs={{0,0},{1,8},{2,16},{3,24},{4,4},{5,12},{6,20},{7,28},{8,1},{9,9},{... | collective-permute-start | bytes 884744 | tf_op jit(solution)/shard_map/ppermute | solution.py:49
  39.9 51.7 %collective-permute-start.8 = (bf16[144,1024]{1,0:T(8,128)(2,1)}, bf16[144,1024]{1,0:T(8,128)(2,1)S(1)}, u32[]{:S(2)}, u32[]{:S(2)}) collective-permute-start(bf16[144,1024]{1,0:T(8,128)(2,1)} %bitcast.431), channel_id=1, source_target_pairs={{0,0},{1,8},{2,16},{3,24},{4,4},{5,12},{6,20},{7,28},{8,1},{9,9},{... | collective-permute-start | bytes 884744 | tf_op jit(solution)/shard_map/ppermute | solution.py:49
  47.9 94.7 %all-gather.11.cloned.1.call-start = ((), (), s32[]{:S(2)}) async-start(), calls=%async_computation.7 | async-start | bytes 2621440 | tf_op jit(solution)/shard_map/all_gather | solution.py:741
  69.0 120.5 %all-gather.13.cloned.1.call-start = ((), (), s32[]{:S(2)}) async-start(), calls=%async_computation.8 | async-start | bytes 1310720 | tf_op jit(solution)/shard_map/all_gather | solution.py:741
  74.9 15.6 %collective-permute-start.4 = (bf16[144,1024]{1,0:T(8,128)(2,1)S(1)}, bf16[144,1024]{1,0:T(8,128)(2,1)S(1)}, u32[]{:S(2)}, u32[]{:S(2)}) collective-permute-start(bf16[144,1024]{1,0:T(8,128)(2,1)S(1)} %collective-permute-done.refs_0_), channel_id=1, source_target_pairs={{0,4},{1,5},{2,6},{3,7},{4,0},{5,1},{6,2},{7,3},{8,12},{9,13},{10,... | collective-permute-start | bytes 884744 | tf_op jit(solution)/shard_map/ppermute | solution.py:39
  131.1 108.9 %all-gather.15.cloned.1.call-start = ((), (), s32[]{:S(2)}) async-start(), calls=%async_computation.9 | async-start | bytes 2949120 | tf_op jit(solution)/shard_map/all_gather | solution.py:741
  155.5 256.7 %reduce-scatter.4.cloned.1.call-start = ((), (), s32[]{:S(2)}) async-start(), calls=%async_computation.3 | async-start | bytes 2785280 | tf_op jit(solution)/shard_map/reduce_scatter | solution.py:872
  299.1 18.6 %collective-permute-start.70 = (bf16[144,1024]{1,0:T(8,128)(2,1)S(1)}, bf16[144,1024]{1,0:T(8,128)(2,1)S(1)}, u32[]{:S(2)}, u32[]{:S(2)}) collective-permute-start(bf16[144,1024]{1,0:T(8,128)(2,1)S(1)} %get-tuple-element.233.refs_0_.refs_8_), channel_id=1, source_target_pairs={{0,6},{1,7},{2,4},{3,5},{4,2},{5,3},{6,0},{7,1},{8,14},{9,15},{10,... | collective-permute-start | bytes 884744 | tf_op jit(solution)/shard_map/ppermute | solution.py:39
  300.4 17.2 %collective-permute-start.72 = (bf16[144,1024]{1,0:T(8,128)(2,1)S(1)}, bf16[144,1024]{1,0:T(8,128)(2,1)S(1)}, u32[]{:S(2)}, u32[]{:S(2)}) collective-permute-start(bf16[144,1024]{1,0:T(8,128)(2,1)S(1)} %get-tuple-element.228), channel_id=1, source_target_pairs={{0,0},{1,8},{2,16},{3,24},{4,4},{5,12},{6,20},{7,28},{8,1},{9,9},{... | collective-permute-start | bytes 884744 | tf_op jit(solution)/shard_map/ppermute | solution.py:49
  301.5 16.1 %collective-permute-start.65 = (bf16[144,1024]{1,0:T(8,128)(2,1)S(1)}, bf16[144,1024]{1,0:T(8,128)(2,1)S(1)}, u32[]{:S(2)}, u32[]{:S(2)}) collective-permute-start(bf16[144,1024]{1,0:T(8,128)(2,1)S(1)} %get-tuple-element.233.refs_0_.refs_8_), channel_id=1, source_target_pairs={{0,1},{1,0},{2,3},{3,2},{4,5},{5,4},{6,7},{7,6},{8,9},{9,8},{10,11... | collective-permute-start | bytes 884744 | tf_op jit(solution)/shard_map/ppermute | solution.py:39
  352.1 132.8 %reduce-scatter.6.cloned.1.call-start = ((), (), s32[]{:S(2)}) async-start(), calls=%async_computation.4 | async-start | bytes 1392640 | tf_op jit(solution)/shard_map/reduce_scatter | solution.py:872
  396.7 15.4 %collective-permute-start.90 = (bf16[144,1024]{1,0:T(8,128)(2,1)}, bf16[144,1024]{1,0:T(8,128)(2,1)}, u32[]{:S(2)}, u32[]{:S(2)}) collective-permute-start(bf16[144,1024]{1,0:T(8,128)(2,1)} %get-tuple-element.263), channel_id=1, source_target_pairs={{0,4},{1,5},{2,6},{3,7},{4,0},{5,1},{6,2},{7,3},{8,12},{9,13},{10,... | collective-permute-start | bytes 884744 | tf_op jit(solution)/shard_map/ppermute | solution.py:39
  418.5 116.3 %reduce-scatter.8.cloned.1.call-start = ((), (), s32[]{:S(2)}) async-start(), calls=%async_computation.5 | async-start | bytes 2621440 | tf_op jit(solution)/shard_map/reduce_scatter | solution.py:872
  514.5 15.5 %collective-permute-start.112 = (bf16[144,1024]{1,0:T(8,128)(2,1)S(1)}, bf16[144,1024]{1,0:T(8,128)(2,1)}, u32[]{:S(2)}, u32[]{:S(2)}) collective-permute-start(bf16[144,1024]{1,0:T(8,128)(2,1)S(1)} %get-tuple-element.314), channel_id=1, source_target_pairs={{0,4},{1,5},{2,6},{3,7},{4,0},{5,1},{6,2},{7,3},{8,12},{9,13},{10,... | collective-permute-start | bytes 884744 | tf_op jit(solution)/shard_map/ppermute | solution.py:39
  518.9 56.7 %collective-permute-start.126 = (bf16[32,1024]{1,0:T(8,128)(2,1)S(1)}, bf16[32,1024]{1,0:T(8,128)(2,1)S(1)}, u32[]{:S(2)}, u32[]{:S(2)}) collective-permute-start(bf16[32,1024]{1,0:T(8,128)(2,1)S(1)} %bitcast.399), channel_id=1, source_target_pairs={{0,0},{8,1},{16,2},{24,3},{1,4},{9,5},{17,6},{25,7},{2,8},{10,9},{... | collective-permute-start | bytes 196616 | tf_op jit(solution)/shard_map/ppermute | solution.py:885
  533.3 20.0 %collective-permute-start.116 = (bf16[272,512]{1,0:T(8,128)(2,1)}, bf16[272,512]{1,0:T(8,128)(2,1)}, u32[]{:S(2)}, u32[]{:S(2)}) collective-permute-start(bf16[272,512]{1,0:T(8,128)(2,1)} %get-tuple-element.323), channel_id=1, source_target_pairs={{0,24},{1,25},{2,26},{3,27},{4,28},{5,29},{6,30},{7,31},{8,16},{9,... | collective-permute-start | bytes 835592 | tf_op jit(solution)/shard_map/ppermute | solution.py:39
  558.2 17.5 %collective-permute-start.125 = (bf16[32,1024]{1,0:T(8,128)(2,1)S(1)}, bf16[32,1024]{1,0:T(8,128)(2,1)S(1)}, u32[]{:S(2)}, u32[]{:S(2)}) collective-permute-start(bf16[32,1024]{1,0:T(8,128)(2,1)S(1)} %bitcast.400), channel_id=1, source_target_pairs={{0,0},{8,1},{16,2},{24,3},{1,4},{9,5},{17,6},{25,7},{2,8},{10,9},{... | collective-permute-start | bytes 196616 | tf_op jit(solution)/shard_map/ppermute | solution.py:885
  560.3 16.2 %collective-permute-start.124 = (bf16[144,1024]{1,0:T(8,128)(2,1)S(1)}, bf16[144,1024]{1,0:T(8,128)(2,1)S(1)}, u32[]{:S(2)}, u32[]{:S(2)}) collective-permute-start(bf16[144,1024]{1,0:T(8,128)(2,1)S(1)} %add_convert_fusion), channel_id=1, source_target_pairs={{0,0},{1,8},{2,16},{3,24},{4,4},{5,12},{6,20},{7,28},{8,1},{9,9},{... | collective-permute-start | bytes 884744 | tf_op jit(solution)/shard_map/ppermute | solution.py:49
  562.5 26.2 %collective-permute-start.120 = (bf16[2,48,1792]{2,1,0:T(8,128)(2,1)S(1)}, bf16[2,48,1792]{2,1,0:T(8,128)(2,1)S(1)}, u32[]{:S(2)}, u32[]{:S(2)}) collective-permute-start(bf16[2,48,1792]{2,1,0:T(8,128)(2,1)S(1)} %pad_maximum_fusion.8), channel_id=1, source_target_pairs={{0,6},{1,7},{2,4},{3,5},{4,2},{5,3},{6,0},{7,1},{8,14},{9,15},{10,... | collective-permute-start | bytes 1032200 | tf_op jit(solution)/shard_map/ppermute | solution.py:39
  575.0 16.3 %collective-permute-start.119 = (bf16[2,48,1792]{2,1,0:T(8,128)(2,1)S(1)}, bf16[2,48,1792]{2,1,0:T(8,128)(2,1)S(1)}, u32[]{:S(2)}, u32[]{:S(2)}) collective-permute-start(bf16[2,48,1792]{2,1,0:T(8,128)(2,1)S(1)} %pad_maximum_fusion.7), channel_id=1, source_target_pairs={{0,4},{1,5},{2,6},{3,7},{4,0},{5,1},{6,2},{7,3},{8,12},{9,13},{10,... | collective-permute-start | bytes 1032200 | tf_op jit(solution)/shard_map/ppermute | solution.py:39
  575.6 20.4 %collective-permute-start.118 = (bf16[2,48,1792]{2,1,0:T(8,128)(2,1)S(1)}, bf16[2,48,1792]{2,1,0:T(8,128)(2,1)S(1)}, u32[]{:S(2)}, u32[]{:S(2)}) collective-permute-start(bf16[2,48,1792]{2,1,0:T(8,128)(2,1)S(1)} %pad_maximum_fusion.6), channel_id=1, source_target_pairs={{0,2},{1,3},{2,0},{3,1},{4,6},{5,7},{6,4},{7,5},{8,10},{9,11},{10,... | collective-permute-start | bytes 1032200 | tf_op jit(solution)/shard_map/ppermute | solution.py:39
  (244 other events, 1649.1 us)
Sparse Core Ops, SparseCore 0:
  48.0 30.3 all-gather.8
  80.6 44.7 all-gather.10
  131.2 27.5 all-gather.12
  160.8 49.9 all-gather.14
  352.2 45.1 reduce-scatter.3
  418.7 27.0 reduce-scatter.5
  461.5 42.8 reduce-scatter.7

commit v3 on v2

--- a/solution.py
+++ b/solution.py
@@ -39,13 +39,13 @@
     return lax.ppermute(x, BOTH, [(d, d ^ mask) for d in range(size)])
 
 
-def turned(x):
+def turned(x, back=False):
     size = lax.axis_size("seq") * lax.axis_size("row")
-    rows = lax.axis_size("row")
     pairs = []
     for d in range(size):
-        o, i, r = d // PLANE, d % PLANE // rows, d % rows
-        pairs.append((d, r * PLANE + i * rows + o))
+        z, y, column, core = d // PLANE, d // 4 % 2, d // 2 % 2, d % 2
+        to = (2 * core + column) * PLANE + 4 * y + 2 * (column ^ (z // 2)) + z % 2
+        pairs.append((to, d) if back else (d, to))
     return lax.ppermute(x, BOTH, pairs)
 
 
@@ -62,7 +62,7 @@
         core, beside = tie(core, beside)
     parts = core_add(even, core)
     got = [across(parts[j], 2 * j) for j in (1, 2, 3)]
-    if beside is not None:
+    if beside is not None and not first:
         got, beside = tie(got, beside)
     return [parts[0]] + got, beside
 
@@ -74,11 +74,14 @@
     return core[0] + sum(across(sent[k - 1], 2 * k).astype(F32) for k in (1, 2, 3))
 
 
-def plane_exchange(x, relative):
+def plane_exchange(x, relative, before=None):
     x = pick(x, relative)
     core = across(x[1::2], 1)
+    if before is not None:
+        core, before = tie(core, before)
     got = tie(*[across(jnp.stack([x[2 * k], core[k]]), 2 * k) for k in (1, 2, 3)])
-    return pick(jnp.concatenate([x[:1], core[:1], *got]), relative)
+    x = pick(jnp.concatenate([x[:1], core[:1], *got]), relative)
+    return x if before is None else (x, before)
 
 
 def pick(x, index, axis=0):
@@ -640,6 +643,102 @@
     else:
         outs = [((far, rows + 16, 4 * wide), BF)]
     return call(kernel, ins, outs, scratch, 8 * N * D * wide)
+
+
+def plane_index():
+    return lax.axis_index("seq") % (PLANE // lax.axis_size("row")) * lax.axis_size("row") + lax.axis_index("row")
+
+
+def pack_shares(sums, others, ffn, lines, in_cols, hidden_cols):
+    rows, width = sums[0].shape[0] - 16, sums[0].shape[1]
+    part = rows // PLANE
+    L = len(ffn)
+    count = L * (in_cols + hidden_cols) + 128
+    bias_lines = in_cols // 128
+    first_line = part - L * bias_lines
+
+    def kernel(ins, outs, scratch):
+        even, odd, last = outs
+        attn = scratch[0]
+        n = len(sums)
+        total = ins[0][...].astype(F32)
+        for ref in ins[1:n]:
+            total = total + ref[...].astype(F32)
+        attn[0] = total.astype(BF)
+        for layer in range(1, L):
+            attn[layer] = ins[n + layer - 1][...]
+        last[...] = attn[0, :rows, in_cols:]
+        ups = ins[n + L - 1 : n + 2 * L - 1]
+        lines = ins[n + 2 * L - 1]
+        here = plane_index()
+        line = lax.broadcasted_iota(jnp.int32, (part, 128), 0)
+        for k in range(PLANE):
+            to = here ^ k
+            out = (odd if k % 2 else even).at[k // 2]
+            at = pl.ds(pl.multiple_of(to * part, 16), part)
+            half = pl.ds(pl.multiple_of(lax.rem(to, PLANE // 2) * part, 16), part)
+            for layer in range(L):
+                out[:, layer * in_cols : (layer + 1) * in_cols] = attn[layer, at, :in_cols]
+                folded = ups[layer][half, :]
+                own = jnp.where(to < PLANE // 2, folded[:, :hidden_cols], folded[:, hidden_cols:])
+                start = L * in_cols + layer * hidden_cols
+                out[:, start : start + hidden_cols] = own
+            block = lines[to]
+            for layer in range(L):
+                bias = attn[layer, rows : rows + 16, :in_cols].astype(F32)[:1]
+                for j in range(bias_lines):
+                    spot = line == first_line + layer * bias_lines + j
+                    block = jnp.where(spot, bias[:, j * 128 : (j + 1) * 128], block)
+            out[:, count - 128 :] = block.astype(BF)
+
+    half = PLANE // 2
+    outs = [((half, part, count), BF), ((half, part, count), BF), ((rows, width - in_cols), BF)]
+    ins = [near(item) for item in (*sums, *others, *ffn, lines)]
+    return call(kernel, ins, outs, [((L, rows + 16, width), BF)], rows * count, SMALL)
+
+
+def unpack_shares(even, core, got, L, in_cols, hidden_cols):
+    part, count = even.shape[1:]
+    wide = in_cols // 3
+    D, far = PLANE * wide, hidden_cols // 128
+    bias_lines = in_cols // 128
+    first_line = part - L * bias_lines
+
+    def natural(x):
+        q = wide // 4
+        return jnp.concatenate([x[:, :q], x[:, 2 * q : 3 * q], x[:, q : 2 * q], x[:, 3 * q :]], axis=1)
+
+    def kernel(ins, outs, scratch):
+        even, core, *got = ins
+        w_in, w_up, lines, bias = outs
+        here = plane_index()
+        blocks = [even.at[0], core.at[0]] + [ref.at[j] for ref in got for j in range(2)]
+        total = jnp.zeros((part, 128), F32)
+        for k in range(PLANE):
+            block = blocks[k][...].astype(F32)
+            of = here ^ k
+            own_lines = block[:, count - 128 :]
+            total = total + own_lines
+            for layer in range(L):
+                for t in range(3):
+                    at = pl.ds(pl.multiple_of(t * D + of * wide, 128), wide)
+                    start = layer * in_cols + t * wide
+                    columns = block[:, start : start + wide]
+                    row = first_line + layer * bias_lines + t
+                    line = own_lines[row : row + 1]
+                    if t < 2:
+                        columns, line = natural(columns), natural(line)
+                    w_in[layer, :, at] = columns
+                    bias[layer, :, at] = line
+                for o in range(far):
+                    at = pl.ds(pl.multiple_of(o * PLANE * 128 + of * 128, 128), 128)
+                    start = L * in_cols + layer * hidden_cols + o * 128
+                    w_up[layer, :, at] = block[:, start : start + 128]
+        lines[...] = total
+
+    outs = [((L, part, 3 * D), F32), ((L, part, far * PLANE * 128), F32), ((part, 128), F32), ((L, 1, 3 * D), F32)]
+    ins = [near(item) for item in (even, core, *got)]
+    return call(kernel, ins, outs, [], part * count * PLANE, SMALL)
 
 
 def body(
@@ -731,7 +830,6 @@
     lengths, kinds = table[:seg_count], table[seg_count : 2 * seg_count]
     pairs_of = table[2 * seg_count :]
     hidden_low = turned(tokens[0])
-    cot = turned(cotangent[0])
 
     def attn_block(layer, shard):
         out = shard_out[layer].reshape(in_rows, PLANE, wide).transpose(1, 0, 2).reshape(rows_in, wide)
@@ -784,7 +882,7 @@
     w_col = full_ffn[L - 1][:, rows_in // 2 + up_cols :].reshape(O, -1)[:, : col_plane.size]
     w_col = w_col.reshape(D, colbert.shape[1])
 
-    block_at = (relative % R) * (PLANE // R) + relative // R
+    block_at = 4 * ((relative // 2 % 2) ^ (far % 2)) + 2 * (relative % 2) + relative // 4
     positions = (block_at[:, None] * T + jnp.arange(T, dtype=jnp.int32)[None, :]).reshape(N)
     held_segment, held_offset = token_info(positions, lengths, kinds)[:2]
     cos, sin = rope_angles(held_offset, head_dim)
@@ -795,8 +893,6 @@
     records = []
     for layer in range(L):
         x_all = plane_gather(hidden_low)
-        if layer == 0:
-            x_all, cot = tie(x_all, cot)
         qkv, context, logs, even, odd = attn_forward(
             x_all, full_attn[layer], in_biases, layer * in_cols, table, seg_row, half, scale
         )
@@ -813,15 +909,18 @@
             [normed] + terms, params, at(layer, BIAS_DOWN), at(layer, GAIN_TWO), at(layer, SHIFT_TWO)
         )
         records.append((x_all, qkv, context, logs, first, normed_all, act, slope, second))
-    hidden_out = turned(hidden_low)
+    hidden_out = turned(hidden_low, True)
 
     full_width = w_col.shape[1]
     part_widths = (full_width, full_width * 3 // 4, full_width // 2)
     query_total = NQ * QLEN
     doc_total = NSD + 1
+    hidden_low, cot = tie(hidden_low, cotangent[0])
+    cot = turned(cot)
     col = dot(hidden_low, w_col)
     in_order = jnp.arange(PLANE, dtype=jnp.int32)
-    in_order = jnp.bitwise_xor((in_order % (PLANE // R)) * R + in_order // (PLANE // R), plane)
+    in_order = 4 * (in_order % 2) + 2 * ((in_order // 4) ^ (far % 2)) + in_order // 2 % 2
+    in_order = jnp.bitwise_xor(in_order, plane)
     col_row = pick(jnp.stack(plane_gather(col.astype(BF))), in_order, axis=0).reshape(N, full_width).astype(F32)
     own_at = block_at[0] * T
     row_positions = jnp.arange(N, dtype=jnp.int32)
@@ -861,7 +960,7 @@
         )
         pull_unit = jax.vjp(unit_rows, col[:, :width])[1]
         grad_col = grad_col + jnp.pad(pull_unit(grad_embed)[0], ((0, 0), (0, full_width - width)))
-    grad_col_low = grad_col.astype(BF)
+    grad_col_low, cot = tie(grad_col.astype(BF), cot)
     col_parts = dot_lt(hidden_low, grad_col_low).reshape(O, PLANE, in_rows, full_width).transpose(1, 0, 2, 3)
     col_parts = plane_sum(pick(col_parts.reshape(PLANE, O * in_rows, full_width), relative, axis=0))
     col_rows = jax.vmap(padded_rows)(col_parts.reshape(O, in_rows * full_width)).astype(BF)
@@ -873,23 +972,9 @@
 
     outs = [[None] * L for _ in range(6)]
 
-    def up_share(shares):
-        return unfold(shares[: rows_in // 2]).reshape(PLANE, in_rows, hidden_cols)
-
-    def in_share(shares):
-        return shares[:rows_in, :in_cols].reshape(PLANE, in_rows, in_cols)
-
-    def finish_out(layer, shares):
-        share_out = shares[:rows_in, in_cols:].astype(BF).reshape(PLANE, in_rows, wide)
-        share_out = share_out.transpose(1, 0, 2).reshape(in_rows, D)
+    def finish_out(layer, share_out):
+        share_out = share_out.reshape(PLANE, in_rows, wide).transpose(1, 0, 2).reshape(in_rows, D)
         outs[1][layer] = lax.ppermute(share_out, BOTH, from_group).astype(F32)
-
-    def bias_in_entries(rows):
-        natural = jnp.pad(unpack_columns(rows[:, None].astype(F32))[0], (0, O * PLANE * bias_part - 3 * D))
-        return pick(natural.reshape(O * PLANE, bias_part), place)
-
-    def as_rows(x, width):
-        return jax.vmap(lambda row: padded_rows(row, width))(x)
 
     shares_ffn, shares_attn = [None] * L, [None] * L
     vectors = [None] * L
@@ -927,40 +1012,31 @@
             grad_parts = [grad_first] + terms
 
     got = [across(blocks[step], PLANE * step) for step in range(1, O)]
-    entries = jnp.concatenate(vectors, axis=2).transpose(1, 0, 2).reshape(PLANE, O * L * part).astype(BF)
-    pieces = [in_share(shares_attn[layer]) for layer in range(1, L)] + [up_share(item) for item in shares_ffn]
-    pieces = jnp.concatenate(pieces, axis=2)
-    got, terms, entries, pieces = tie(got, terms, entries, pieces)
-    grad_tokens = turned((grad_first + sum(item.astype(F32) for item in terms)).astype(BF))
-    shares_attn[0] = (blocks[0].astype(F32) + sum(item.astype(F32) for item in got)).astype(BF)
-    pieces = jnp.concatenate([in_share(shares_attn[0]), pieces], axis=2)
-    bias_rows = [jnp.broadcast_to(item[None, rows_in, :in_cols], (PLANE, in_cols)) for item in shares_attn]
-    more = as_rows(jnp.concatenate([entries] + bias_rows, axis=1), pieces.shape[2])
-    back = plane_exchange(jnp.concatenate([pieces, more], axis=1), relative)
-    more = back[:, in_rows:].reshape(PLANE, -1)
-    entries = jnp.sum(more[:, : O * L * part].astype(F32), axis=0).reshape(O, L * part)
+    entries = jnp.concatenate(vectors, axis=2).transpose(1, 0, 2).reshape(PLANE, O * L * part)
+    lines = jnp.pad(entries, ((0, 0), (0, in_rows * 128 - O * L * part))).reshape(PLANE, in_rows, 128)
+    got, lines = tie(got, lines)
+    grad_tokens = turned((grad_first + sum(item.astype(F32) for item in terms)).astype(BF), True)
+    even, odd, last_out = pack_shares([blocks[0]] + got, shares_attn[1:], shares_ffn, lines, in_cols, hidden_cols)
+    core, grad_tokens = tie(across(odd, 1), grad_tokens)
+    got = tie(*[across(jnp.stack([even[k], core[k]]), 2 * k) for k in (1, 2, 3)])
+    w_in_grad, w_up_grad, lines, bias_in_grad = unpack_shares(even, core, got, L, in_cols, hidden_cols)
+    entries = lines.reshape(-1)[: O * L * part].reshape(O, L * part)
     entries = jnp.concatenate([entries, jnp.broadcast_to(loss_terms[None], (O, 2))], axis=1)
     mine = pick(entries, far)
     for step in range(1, O):
         mine = mine + across(pick(entries, far ^ step), PLANE * step)
-    start = 0
+    bias_in_grad = jnp.pad(bias_in_grad[:, 0], ((0, 0), (0, O * PLANE * bias_part - 3 * D)))
+    bias_in_grad = pick(bias_in_grad.reshape(L, O * PLANE, bias_part), place, axis=1)
     for layer in range(L):
-        outs[0][layer] = unpack_columns(back[:, :in_rows, start : start + in_cols])
-        start += in_cols
-    for layer in range(L):
-        outs[2][layer] = unpack_hidden(back[:, :in_rows, start : start + hidden_cols])
-        start += hidden_cols
-        at_row = rows_in // 2
-        outs[3][layer] = shares_ffn[layer][at_row : at_row + up_cols]
-        finish_out(layer, shares_attn[layer])
-        at_row = O * L * part + layer * in_cols
-        bias_in = bias_in_entries(more[:, at_row : at_row + in_cols])
+        outs[3][layer] = shares_ffn[layer][rows_in // 2 : rows_in // 2 + up_cols]
+        finish_out(layer, shares_attn[layer][:rows_in, in_cols:] if layer > 0 else last_out)
         outs[4][layer] = mine[layer * part : layer * part + gain_part]
-        outs[5][layer] = mine[layer * part + gain_part : (layer + 1) * part] + bias_in
+        outs[5][layer] = mine[layer * part + gain_part : (layer + 1) * part] + bias_in_grad[layer]
     col_share = shares_ffn[L - 1][rows_in // 2 + up_cols :].reshape(-1)[: in_rows * full_width]
     col_share = col_share.reshape(in_rows, full_width).astype(F32)
     loss_terms = mine[L * part :]
-    stacked = [jnp.stack(items).astype(F32) for items in outs]
+    outs[0], outs[2] = w_in_grad, w_up_grad
+    stacked = [jnp.stack(items).astype(F32) if isinstance(items, list) else items for items in outs]
     return (
         hidden_out[None],
         loss_terms[:1],

time: 626 us -> 594 us (0.949)
  waiting for transfers between devices: 245 us -> 208 us
  starting transfers between devices: 123 us -> 134 us
  local copies, waits for them, and re-layouts: 68.3 us -> 61.5 us
    ppermute x119, waiting for transfers between devices: 245 us -> 208 us  [across(): return lax.ppermute(x, BOTH, [(d, d ^ mask) for d in range(size)])]
    ppermute x119, starting transfers between devices: 112 us -> 123 us  [across(): return lax.ppermute(x, BOTH, [(d, d ^ mask) for d in range(size)])]
    pallas_call x28 -> x30, Pallas kernels: 130 us -> 133 us  [call(): pl.pallas_call(wrapped, in_specs=[IN_VMEM if kind == 'near' else IN_HBM f...]
    unnamed x311 -> x316, local copies, waits for them, and re-layouts: 32.3 us -> 35 us
  transfers between devices with their start and end apart: 134 -> 134, of which waited for: 65 -> 62; matrix products, arithmetic and copies ran while one was open for 9% -> 9% of each run, Pallas kernels for 18% -> 19%
where the time goes in v3:
time: 594 us; the launch traced here: 586 us
  waiting for transfers between devices  208 us (35%)
  starting transfers between devices  134 us (23%)
  Pallas kernels  133 us (22%)
  local copies, waits for them, and re-layouts  61.5 us (10%)
  other arithmetic  25.3 us (4%)
  between operations  18.4 us (3%)
  matrix products  6.19 us (1%)
    ppermute x119, waiting for transfers between devices, across(): return lax.ppermute(x, BOTH, [(d, d ^ mask) for d in range(size)])  208 us
    pallas_call x30, Pallas kernels, call(): pl.pallas_call(wrapped, in_specs=[IN_VMEM if kind == 'near' else IN_HBM f...  133 us
    ppermute x119, starting transfers between devices, across(): return lax.ppermute(x, BOTH, [(d, d ^ mask) for d in range(size)])  123 us
    unnamed x316, local copies, waits for them, and re-layouts  35 us
  transfers between devices with their start and end apart: 134, of which 62 were waited for; matrix products, arithmetic and copies ran while one was open for 9% of the time, Pallas kernels for 19%

profile of v3, /device:TPU:0, one launch (start us, length us, event | category | flops | bytes accessed | tf_op | source)
XLA Modules:
  0.0 586.4 jit_solution(12698155791717166485)
XLA Ops:
  26.4 9.6 %collective-permute-start.12 = (bf16[2,48,384]{2,1,0:T(8,128)(2,1)S(1)}, bf16[2,48,384]{2,1,0:T(8,128)(2,1)S(1)}, u32[]{:S(2)}, u32[]{:S(2)}) collective-permute-start(bf16[2,48,384]{2,1,0:T(8,128)(2,1)S(1)} %pad_maximum_fusion.15), channel_id=1, source_target_pairs={{0,6},{1,7},{2,4},{3,5},{4,2},{5,3},{6,0},{7,1},{8,14},{9,15},{10,... | collective-permute-start | bytes 221192 | tf_op jit(solution)/shard_map/ppermute | solution.py:39
  81.2 10.5 %shard_map.212 = (bf16[1152,384]{1,0:T(8,128)(2,1)}, bf16[1152,128]{1,0:T(8,128)(2,1)}, f32[2,1152]{1,0:T(2,128)}, bf16[4,144,1024]{2,1,0:T(8,128)(2,1)}, bf16[4,144,1024]{2,1,0:T(8,128)(2,1)}) custom-call(bf16[144,1024]{1,0:T(8,128)(2,1)} %copy-done.1, bf16[144,1024]{1,0:T(8,128)(2,1)} %copy-done.66, bf16[144,1024]{1,0:T(8,128)(2,1)} %copy-done.63, ...), custom_call_target="tpu_custom_call" | custom-call | flops 2566914048 | bytes 7553536 | tf_op jit(solution)/shard_map/pallas_call | solution.py:213
  131.2 8.1 %shard_map.215 = (bf16[1152,512]{1,0:T(8,128)(2,1)}, bf16[1152,512]{1,0:T(8,128)(2,1)}, bf16[4,144,1024]{2,1,0:T(8,128)(2,1)}, bf16[4,144,1024]{2,1,0:T(8,128)(2,1)}) custom-call(bf16[144,1024]{1,0:T(8,128)(2,1)} %copy-done.29, bf16[144,1024]{1,0:T(8,128)(2,1)} %copy-done.72, bf16[144,1024]{1,0:T(8,128)(2,1)} %copy-done.69, bf16[144,1024]{1,0:T(8,128)(2,1)} %copy-done.73, ...), custom_call_target="tpu_custom_call" | custom-call | flops 2415919104 | bytes 9179136 | tf_op jit(solution)/shard_map/pallas_call | solution.py:213
  152.9 7.0 %collective-permute-done.33.refs_3_ = bf16[144,1024]{1,0:T(8,128)(2,1)S(1)} collective-permute-done((bf16[144,1024]{1,0:T(8,128)(2,1)S(1)}, bf16[144,1024]{1,0:T(8,128)(2,1)S(1)}, u32[]{:S(2)}, u32[]{:S(2)}) %collective-permute-start.33) | collective-permute-done | bytes 294944 | tf_op jit(solution)/shard_map/ppermute | solution.py:39
  164.8 6.5 %collective-permute-done.36.refs_2_ = bf16[144,1024]{1,0:T(8,128)(2,1)S(1)} collective-permute-done((bf16[144,1024]{1,0:T(8,128)(2,1)S(1)}, bf16[144,1024]{1,0:T(8,128)(2,1)S(1)}, u32[]{:S(2)}, u32[]{:S(2)}) %collective-permute-start.36) | collective-permute-done | bytes 294944 | tf_op jit(solution)/shard_map/ppermute | solution.py:39
  179.3 10.3 %shard_map.218 = (bf16[1152,384]{1,0:T(8,128)(2,1)}, bf16[1152,128]{1,0:T(8,128)(2,1)}, f32[2,1152]{1,0:T(2,128)}, bf16[4,144,1024]{2,1,0:T(8,128)(2,1)}, bf16[4,144,1024]{2,1,0:T(8,128)(2,1)}) custom-call(bf16[144,1024]{1,0:T(8,128)(2,1)} %copy-done.30, bf16[144,1024]{1,0:T(8,128)(2,1)} %copy-done.79, bf16[144,1024]{1,0:T(8,128)(2,1)} %copy-done.76, ...), custom_call_target="tpu_custom_call" | custom-call | flops 2566914048 | bytes 7553536 | tf_op jit(solution)/shard_map/pallas_call | solution.py:213
  197.8 6.4 %collective-permute-done.43.refs_2_ = bf16[144,1024]{1,0:T(8,128)(2,1)S(1)} collective-permute-done((bf16[144,1024]{1,0:T(8,128)(2,1)S(1)}, bf16[144,1024]{1,0:T(8,128)(2,1)S(1)}, u32[]{:S(2)}, u32[]{:S(2)}) %collective-permute-start.43) | collective-permute-done | bytes 294944 | tf_op jit(solution)/shard_map/ppermute | solution.py:39
  204.2 6.4 %collective-permute-done.44.refs_3_ = bf16[144,1024]{1,0:T(8,128)(2,1)S(1)} collective-permute-done((bf16[144,1024]{1,0:T(8,128)(2,1)S(1)}, bf16[144,1024]{1,0:T(8,128)(2,1)S(1)}, u32[]{:S(2)}, u32[]{:S(2)}) %collective-permute-start.44) | collective-permute-done | bytes 294944 | tf_op jit(solution)/shard_map/ppermute | solution.py:39
  215.7 6.5 %collective-permute-done.47.refs_2_ = bf16[144,1024]{1,0:T(8,128)(2,1)S(1)} collective-permute-done((bf16[144,1024]{1,0:T(8,128)(2,1)S(1)}, bf16[144,1024]{1,0:T(8,128)(2,1)S(1)}, u32[]{:S(2)}, u32[]{:S(2)}) %collective-permute-start.47) | collective-permute-done | bytes 294944 | tf_op jit(solution)/shard_map/ppermute | solution.py:39
  229.3 8.1 %shard_map.221 = (bf16[1152,512]{1,0:T(8,128)(2,1)}, bf16[1152,512]{1,0:T(8,128)(2,1)}, bf16[4,144,1024]{2,1,0:T(8,128)(2,1)}, bf16[4,144,1024]{2,1,0:T(8,128)(2,1)}) custom-call(bf16[144,1024]{1,0:T(8,128)(2,1)} %copy-done.31, bf16[144,1024]{1,0:T(8,128)(2,1)} %copy-done.86, bf16[144,1024]{1,0:T(8,128)(2,1)} %copy-done.83, bf16[144,1024]{1,0:T(8,128)(2,1)} %copy-done.87, ...), custom_call_target="tpu_custom_call" | custom-call | flops 2415919104 | bytes 9441280 | tf_op jit(solution)/shard_map/pallas_call | solution.py:213
  252.0 7.3 %collective-permute-done.55.refs_3_ = bf16[144,1024]{1,0:T(8,128)(2,1)S(1)} collective-permute-done((bf16[144,1024]{1,0:T(8,128)(2,1)S(1)}, bf16[144,1024]{1,0:T(8,128)(2,1)S(1)}, u32[]{:S(2)}, u32[]{:S(2)}) %collective-permute-start.55) | collective-permute-done | bytes 294944 | tf_op jit(solution)/shard_map/ppermute | solution.py:39
  297.4 7.4 %collective-permute-done.68.refs_4_.refs_12_ = bf16[144,1024]{1,0:T(8,128)(2,1)S(1)} collective-permute-done((bf16[144,1024]{1,0:T(8,128)(2,1)S(1)}, bf16[144,1024]{1,0:T(8,128)(2,1)S(1)}, u32[]{:S(2)}, u32[]{:S(2)}) %collective-permute-start.68) | collective-permute-done | bytes 294944 | tf_op jit(solution)/shard_map/ppermute | solution.py:39
  307.9 7.2 %shard_map.225 = (bf16[1152,512]{1,0:T(8,128)(2,1)}, f32[1,512]{1,0:T(1,128)}, bf16[4,144,1024]{2,1,0:T(8,128)(2,1)}, bf16[4,144,1024]{2,1,0:T(8,128)(2,1)}) custom-call(bf16[144,1024]{1,0:T(8,128)(2,1)} %copy-done.32, bf16[144,1024]{1,0:T(8,128)(2,1)} %copy-done.93, bf16[144,1024]{1,0:T(8,128)(2,1)} %copy-done.90, bf16[144,1024]{1,0:T(8,128)(2,1)} %copy-done.94, ...), custom_call_target="tpu_custom_call" | custom-call | flops 2415919104 | bytes 9439232 | tf_op jit(solution)/shard_map/pallas_call | solution.py:213
  328.0 8.5 %shard_map.227 = bf16[4,272,1024]{2,1,0:T(8,128)(2,1)} custom-call(bf16[144,1024]{1,0:T(8,128)(2,1)} %copy-done.31, bf16[144,1024]{1,0:T(8,128)(2,1)} %copy-done.86, bf16[144,1024]{1,0:T(8,128)(2,1)} %copy-done.83, bf16[144,1024]{1,0:T(8,128)(2,1)} %copy-done.87, bf16[144,1024]{1,0:T(8,128)(2,1)} %copy-done.84, bf16[144,1024]{1,0:T(8,128)(2,1)} %copy-done.88, ...), custom_call_target="tpu_custom_call" | custom-call | flops 2415919104 | bytes 9437184 | tf_op jit(solution)/shard_map/pallas_call | solution.py:213
  345.7 6.5 %collective-permute-done.82.refs_2_.refs_10_ = bf16[144,1024]{1,0:T(8,128)(2,1)S(1)} collective-permute-done((bf16[144,1024]{1,0:T(8,128)(2,1)S(1)}, bf16[144,1024]{1,0:T(8,128)(2,1)S(1)}, u32[]{:S(2)}, u32[]{:S(2)}) %collective-permute-start.82) | collective-permute-done | bytes 294944 | tf_op jit(solution)/shard_map/ppermute | solution.py:39
  359.7 17.2 %shard_map.229 = (bf16[1152,384]{1,0:T(8,128)(2,1)}, f32[1,384]{1,0:T(1,128)}, bf16[4,144,1024]{2,1,0:T(8,128)(2,1)}, bf16[4,144,1024]{2,1,0:T(8,128)(2,1)}) custom-call(bf16[144,1024]{1,0:T(8,128)(2,1)} %copy-done.35, bf16[144,1024]{1,0:T(8,128)(2,1)} %copy-done.110, bf16[144,1024]{1,0:T(8,128)(2,1)} %copy-done.106, bf16[144,1024]{1,0:T(8,128)(2,1)} %copy-done.112, ...), custom_call_target="tpu_custom_call" | custom-call | flops 4605345792 | bytes 8436736 | tf_op jit(solution)/shard_map/pallas_call | solution.py:213
  386.6 6.8 %shard_map.231 = bf16[4,272,512]{2,1,0:T(8,128)(2,1)} custom-call(bf16[144,1024]{1,0:T(8,128)(2,1)} %copy-done.30, bf16[144,1024]{1,0:T(8,128)(2,1)} %copy-done.79, bf16[144,1024]{1,0:T(8,128)(2,1)} %copy-done.76, bf16[144,1024]{1,0:T(8,128)(2,1)} %copy-done.80, bf16[144,1024]{1,0:T(8,128)(2,1)} %copy-done.77, bf16[144,1024]{1,0:T(8,128)(2,1)} %copy-done.81, ...), custom_call_target="tpu_custom_call" | custom-call | flops 1207959552 | bytes 7013888 | tf_op jit(solution)/shard_map/pallas_call | solution.py:213
  422.4 7.2 %shard_map.233 = (bf16[1152,512]{1,0:T(8,128)(2,1)}, f32[1,512]{1,0:T(1,128)}, bf16[4,144,1024]{2,1,0:T(8,128)(2,1)}, bf16[4,144,1024]{2,1,0:T(8,128)(2,1)}) custom-call(bf16[144,1024]{1,0:T(8,128)(2,1)} %copy-done.34, bf16[144,1024]{1,0:T(8,128)(2,1)} %copy-done.111, bf16[144,1024]{1,0:T(8,128)(2,1)} %copy-done.102, bf16[144,1024]{1,0:T(8,128)(2,1)} %copy-done.113, ...), custom_call_target="tpu_custom_call" | custom-call | flops 2415919104 | bytes 9177088 | tf_op jit(solution)/shard_map/pallas_call | solution.py:213
  438.6 8.4 %shard_map.235 = bf16[4,256,1024]{2,1,0:T(8,128)(2,1)} custom-call(bf16[144,1024]{1,0:T(8,128)(2,1)} %copy-done.29, bf16[144,1024]{1,0:T(8,128)(2,1)} %copy-done.72, bf16[144,1024]{1,0:T(8,128)(2,1)} %copy-done.69, bf16[144,1024]{1,0:T(8,128)(2,1)} %copy-done.73, bf16[144,1024]{1,0:T(8,128)(2,1)} %copy-done.70, bf16[144,1024]{1,0:T(8,128)(2,1)} %copy-done.74, ...), custom_call_target="tpu_custom_call" | custom-call | flops 2415919104 | bytes 9175040 | tf_op jit(solution)/shard_map/pallas_call | solution.py:213
  476.2 17.1 %shard_map.237 = (bf16[1152,384]{1,0:T(8,128)(2,1)}, f32[1,384]{1,0:T(1,128)}, bf16[4,144,1024]{2,1,0:T(8,128)(2,1)}, bf16[4,144,1024]{2,1,0:T(8,128)(2,1)}) custom-call(bf16[144,1024]{1,0:T(8,128)(2,1)} %copy-done.33, bf16[144,1024]{1,0:T(8,128)(2,1)} %copy-done.100, bf16[144,1024]{1,0:T(8,128)(2,1)} %copy-done.96, bf16[144,1024]{1,0:T(8,128)(2,1)} %copy-done.101, ...), custom_call_target="tpu_custom_call" | custom-call | flops 4605345792 | bytes 8436736 | tf_op jit(solution)/shard_map/pallas_call | solution.py:213
  495.1 6.8 %shard_map.238 = (bf16[272,512]{1,0:T(8,128)(2,1)}, bf16[272,512]{1,0:T(8,128)(2,1)}, bf16[272,512]{1,0:T(8,128)(2,1)}, bf16[272,512]{1,0:T(8,128)(2,1)}) custom-call(bf16[144,1024]{1,0:T(8,128)(2,1)} %copy-done.1, bf16[144,1024]{1,0:T(8,128)(2,1)} %copy-done.66, bf16[144,1024]{1,0:T(8,128)(2,1)} %copy-done.63, bf16[144,1024]{1,0:T(8,128)(2,1)} %copy-done.67, ...), custom_call_target="tpu_custom_call" | custom-call | flops 1207959552 | bytes 7013888 | tf_op jit(solution)/shard_map/pallas_call | solution.py:213
  507.9 7.2 %collective-permute-start.112 = (bf16[272,512]{1,0:T(8,128)(2,1)}, bf16[272,512]{1,0:T(8,128)(2,1)S(1)}, u32[]{:S(2)}, u32[]{:S(2)}) collective-permute-start(bf16[272,512]{1,0:T(8,128)(2,1)} %get-tuple-element.300), channel_id=1, source_target_pairs={{0,16},{1,17},{2,18},{3,19},{4,20},{5,21},{6,22},{7,23},{8,24},{9,... | collective-permute-start | bytes 835592 | tf_op jit(solution)/shard_map/ppermute | solution.py:39
  520.6 14.2 %collective-permute-done.112.refs_2_ = bf16[272,512]{1,0:T(8,128)(2,1)S(1)} collective-permute-done((bf16[272,512]{1,0:T(8,128)(2,1)}, bf16[272,512]{1,0:T(8,128)(2,1)S(1)}, u32[]{:S(2)}, u32[]{:S(2)}) %collective-permute-start.112) | collective-permute-done | bytes 278560 | tf_op jit(solution)/shard_map/ppermute | solution.py:39
  545.6 9.0 %collective-permute-start.121 = (bf16[2,32,1920]{2,1,0:T(8,128)(2,1)S(1)}, bf16[2,32,1920]{2,1,0:T(8,128)(2,1)S(1)}, u32[]{:S(2)}, u32[]{:S(2)}) collective-permute-start(bf16[2,32,1920]{2,1,0:T(8,128)(2,1)S(1)} %pad_maximum_fusion.9), channel_id=1, source_target_pairs={{0,6},{1,7},{2,4},{3,5},{4,2},{5,3},{6,0},{7,1},{8,14},{9,15},{10,... | collective-permute-start | bytes 737288 | tf_op jit(solution)/shard_map/ppermute | solution.py:39
  (819 shorter events, 357.9 us)
Async XLA Ops:
  7.2 74.0 %all-gather.9.cloned.1.call-start = ((), (), s32[]{:S(2)}) async-start(), calls=%async_computation.6 | async-start | bytes 1310720 | tf_op jit(solution)/shard_map/all_gather | solution.py:839
  11.6 33.1 %collective-permute-start.27 = (bf16[4,32,1408]{2,1,0:T(8,128)(2,1)}, bf16[4,32,1408]{2,1,0:T(8,128)(2,1)}, u32[]{:S(2)}, u32[]{:S(2)}) collective-permute-start(bf16[4,32,1408]{2,1,0:T(8,128)(2,1)} %slice.359), channel_id=1, source_target_pairs={{0,1},{1,0},{2,3},{3,2},{4,5},{5,4},{6,7},{7,6},{8,9},{9,8},{10,11... | collective-permute-start | bytes 1081352 | tf_op jit(solution)/shard_map/ppermute | solution.py:39
  15.8 20.4 %collective-permute-start.13 = (bf16[2,32,1024]{2,1,0:T(8,128)(2,1)}, bf16[2,32,1024]{2,1,0:T(8,128)(2,1)}, u32[]{:S(2)}, u32[]{:S(2)}) collective-permute-start(bf16[2,32,1024]{2,1,0:T(8,128)(2,1)} %param.15), channel_id=1, source_target_pairs={{0,0},{1,8},{2,16},{3,24},{4,1},{5,9},{6,17},{7,25},{8,2},{9,10},{... | collective-permute-start | bytes 393224 | tf_op jit(solution)/shard_map/ppermute | solution.py:827
  17.9 46.9 %collective-permute-start.1 = (bf16[144,1024]{1,0:T(8,128)(2,1)}, bf16[144,1024]{1,0:T(8,128)(2,1)S(1)}, u32[]{:S(2)}, u32[]{:S(2)}) collective-permute-start(bf16[144,1024]{1,0:T(8,128)(2,1)} %bitcast.7), channel_id=1, source_target_pairs={{0,0},{1,16},{2,10},{3,26},{4,4},{5,20},{6,14},{7,30},{8,1},{9,17}... | collective-permute-start | bytes 884744 | tf_op jit(solution)/shard_map/ppermute | solution.py:49
  44.7 84.8 %all-gather.11.cloned.1.call-start = ((), (), s32[]{:S(2)}) async-start(), calls=%async_computation.7 | async-start | bytes 2621440 | tf_op jit(solution)/shard_map/all_gather | solution.py:839
  59.2 117.6 %all-gather.13.cloned.1.call-start = ((), (), s32[]{:S(2)}) async-start(), calls=%async_computation.8 | async-start | bytes 1310720 | tf_op jit(solution)/shard_map/all_gather | solution.py:839
  119.1 107.9 %all-gather.15.cloned.1.call-start = ((), (), s32[]{:S(2)}) async-start(), calls=%async_computation.9 | async-start | bytes 2949120 | tf_op jit(solution)/shard_map/all_gather | solution.py:839
  142.6 257.2 %reduce-scatter.4.cloned.1.call-start = ((), (), s32[]{:S(2)}) async-start(), calls=%async_computation.3 | async-start | bytes 2785280 | tf_op jit(solution)/shard_map/reduce_scatter | solution.py:971
  144.7 15.2 %collective-permute-start.33 = (bf16[144,1024]{1,0:T(8,128)(2,1)S(1)}, bf16[144,1024]{1,0:T(8,128)(2,1)S(1)}, u32[]{:S(2)}, u32[]{:S(2)}) collective-permute-start(bf16[144,1024]{1,0:T(8,128)(2,1)S(1)} %get-tuple-element.193), channel_id=1, source_target_pairs={{0,4},{1,5},{2,6},{3,7},{4,0},{5,1},{6,2},{7,3},{8,12},{9,13},{10,... | collective-permute-start | bytes 884744 | tf_op jit(solution)/shard_map/ppermute | solution.py:39
  195.4 15.1 %collective-permute-start.44 = (bf16[144,1024]{1,0:T(8,128)(2,1)S(1)}, bf16[144,1024]{1,0:T(8,128)(2,1)S(1)}, u32[]{:S(2)}, u32[]{:S(2)}) collective-permute-start(bf16[144,1024]{1,0:T(8,128)(2,1)S(1)} %get-tuple-element.201), channel_id=1, source_target_pairs={{0,4},{1,5},{2,6},{3,7},{4,0},{5,1},{6,2},{7,3},{8,12},{9,13},{10,... | collective-permute-start | bytes 884744 | tf_op jit(solution)/shard_map/ppermute | solution.py:39
  244.2 15.1 %collective-permute-start.55 = (bf16[144,1024]{1,0:T(8,128)(2,1)S(1)}, bf16[144,1024]{1,0:T(8,128)(2,1)S(1)}, u32[]{:S(2)}, u32[]{:S(2)}) collective-permute-start(bf16[144,1024]{1,0:T(8,128)(2,1)S(1)} %get-tuple-element.209), channel_id=1, source_target_pairs={{0,4},{1,5},{2,6},{3,7},{4,0},{5,1},{6,2},{7,3},{8,12},{9,13},{10,... | collective-permute-start | bytes 884744 | tf_op jit(solution)/shard_map/ppermute | solution.py:39
  265.7 19.4 %collective-permute-start.64 = (bf16[144,1024]{1,0:T(8,128)(2,1)}, bf16[144,1024]{1,0:T(8,128)(2,1)S(1)}, u32[]{:S(2)}, u32[]{:S(2)}) collective-permute-start(bf16[144,1024]{1,0:T(8,128)(2,1)} %bitcast.39), channel_id=1, source_target_pairs={{0,0},{1,16},{2,10},{3,26},{4,4},{5,20},{6,14},{7,30},{8,1},{9,17}... | collective-permute-start | bytes 884744 | tf_op jit(solution)/shard_map/ppermute | solution.py:49
  289.6 15.3 %collective-permute-start.68 = (bf16[144,1024]{1,0:T(8,128)(2,1)S(1)}, bf16[144,1024]{1,0:T(8,128)(2,1)S(1)}, u32[]{:S(2)}, u32[]{:S(2)}) collective-permute-start(bf16[144,1024]{1,0:T(8,128)(2,1)S(1)} %get-tuple-element.220.refs_0_.refs_8_), channel_id=1, source_target_pairs={{0,4},{1,5},{2,6},{3,7},{4,0},{5,1},{6,2},{7,3},{8,12},{9,13},{10,... | collective-permute-start | bytes 884744 | tf_op jit(solution)/shard_map/ppermute | solution.py:39
  338.6 135.3 %reduce-scatter.6.cloned.1.call-start = ((), (), s32[]{:S(2)}) async-start(), calls=%async_computation.4 | async-start | bytes 1392640 | tf_op jit(solution)/shard_map/reduce_scatter | solution.py:971
  383.8 15.3 %collective-permute-start.90 = (bf16[144,1024]{1,0:T(8,128)(2,1)}, bf16[144,1024]{1,0:T(8,128)(2,1)S(1)}, u32[]{:S(2)}, u32[]{:S(2)}) collective-permute-start(bf16[144,1024]{1,0:T(8,128)(2,1)} %get-tuple-element.250), channel_id=1, source_target_pairs={{0,4},{1,5},{2,6},{3,7},{4,0},{5,1},{6,2},{7,3},{8,12},{9,13},{10,... | collective-permute-start | bytes 884744 | tf_op jit(solution)/shard_map/ppermute | solution.py:39
  408.3 127.3 %reduce-scatter.8.cloned.1.call-start = ((), (), s32[]{:S(2)}) async-start(), calls=%async_computation.5 | async-start | bytes 2621440 | tf_op jit(solution)/shard_map/reduce_scatter | solution.py:971
  436.0 15.3 %collective-permute-start.101 = (bf16[144,1024]{1,0:T(8,128)(2,1)}, bf16[144,1024]{1,0:T(8,128)(2,1)S(1)}, u32[]{:S(2)}, u32[]{:S(2)}) collective-permute-start(bf16[144,1024]{1,0:T(8,128)(2,1)} %get-tuple-element.270), channel_id=1, source_target_pairs={{0,4},{1,5},{2,6},{3,7},{4,0},{5,1},{6,2},{7,3},{8,12},{9,13},{10,... | collective-permute-start | bytes 884744 | tf_op jit(solution)/shard_map/ppermute | solution.py:39
  504.4 31.1 %collective-permute-start.114 = (bf16[144,1024]{1,0:T(8,128)(2,1)}, bf16[144,1024]{1,0:T(8,128)(2,1)}, u32[]{:S(2)}, u32[]{:S(2)}) collective-permute-start(bf16[144,1024]{1,0:T(8,128)(2,1)} %get-tuple-element.315), channel_id=1, source_target_pairs={{0,2},{1,3},{2,0},{3,1},{4,6},{5,7},{6,4},{7,5},{8,10},{9,11},{10,... | collective-permute-start | bytes 884744 | tf_op jit(solution)/shard_map/ppermute | solution.py:39
  505.4 30.1 %collective-permute-start.115 = (bf16[144,1024]{1,0:T(8,128)(2,1)}, bf16[144,1024]{1,0:T(8,128)(2,1)}, u32[]{:S(2)}, u32[]{:S(2)}) collective-permute-start(bf16[144,1024]{1,0:T(8,128)(2,1)} %get-tuple-element.316), channel_id=1, source_target_pairs={{0,4},{1,5},{2,6},{3,7},{4,0},{5,1},{6,2},{7,3},{8,12},{9,13},{10,... | collective-permute-start | bytes 884744 | tf_op jit(solution)/shard_map/ppermute | solution.py:39
  506.3 29.2 %collective-permute-start.116 = (bf16[144,1024]{1,0:T(8,128)(2,1)}, bf16[144,1024]{1,0:T(8,128)(2,1)}, u32[]{:S(2)}, u32[]{:S(2)}) collective-permute-start(bf16[144,1024]{1,0:T(8,128)(2,1)} %get-tuple-element.317), channel_id=1, source_target_pairs={{0,6},{1,7},{2,4},{3,5},{4,2},{5,3},{6,0},{7,1},{8,14},{9,15},{10,... | collective-permute-start | bytes 884744 | tf_op jit(solution)/shard_map/ppermute | solution.py:39
  507.9 26.9 %collective-permute-start.112 = (bf16[272,512]{1,0:T(8,128)(2,1)}, bf16[272,512]{1,0:T(8,128)(2,1)S(1)}, u32[]{:S(2)}, u32[]{:S(2)}) collective-permute-start(bf16[272,512]{1,0:T(8,128)(2,1)} %get-tuple-element.300), channel_id=1, source_target_pairs={{0,16},{1,17},{2,18},{3,19},{4,20},{5,21},{6,22},{7,23},{8,24},{9,... | collective-permute-start | bytes 835592 | tf_op jit(solution)/shard_map/ppermute | solution.py:39
  515.1 20.4 %collective-permute-start.113 = (bf16[272,512]{1,0:T(8,128)(2,1)}, bf16[272,512]{1,0:T(8,128)(2,1)S(1)}, u32[]{:S(2)}, u32[]{:S(2)}) collective-permute-start(bf16[272,512]{1,0:T(8,128)(2,1)} %get-tuple-element.301), channel_id=1, source_target_pairs={{0,24},{1,25},{2,26},{3,27},{4,28},{5,29},{6,30},{7,31},{8,16},{9,... | collective-permute-start | bytes 835592 | tf_op jit(solution)/shard_map/ppermute | solution.py:39
  534.8 21.6 %collective-permute-start.126 = (bf16[32,1024]{1,0:T(8,128)(2,1)S(1)}, bf16[32,1024]{1,0:T(8,128)(2,1)S(1)}, u32[]{:S(2)}, u32[]{:S(2)}) collective-permute-start(bf16[32,1024]{1,0:T(8,128)(2,1)S(1)} %bitcast.340), channel_id=1, source_target_pairs={{0,0},{8,1},{16,2},{24,3},{1,4},{9,5},{17,6},{25,7},{2,8},{10,9},{... | collective-permute-start | bytes 196616 | tf_op jit(solution)/shard_map/ppermute | solution.py:977
  545.6 15.8 %collective-permute-start.121 = (bf16[2,32,1920]{2,1,0:T(8,128)(2,1)S(1)}, bf16[2,32,1920]{2,1,0:T(8,128)(2,1)S(1)}, u32[]{:S(2)}, u32[]{:S(2)}) collective-permute-start(bf16[2,32,1920]{2,1,0:T(8,128)(2,1)S(1)} %pad_maximum_fusion.9), channel_id=1, source_target_pairs={{0,6},{1,7},{2,4},{3,5},{4,2},{5,3},{6,0},{7,1},{8,14},{9,15},{10,... | collective-permute-start | bytes 737288 | tf_op jit(solution)/shard_map/ppermute | solution.py:39
  (248 other events, 1697.7 us)
Sparse Core Ops, SparseCore 0:
  44.8 30.3 all-gather.8
  77.4 44.7 all-gather.10
  124.3 26.6 all-gather.12
  153.0 49.9 all-gather.14
  338.7 49.8 reduce-scatter.3
  408.4 31.7 reduce-scatter.5
  451.4 47.3 reduce-scatter.7

commit v4 on v3

--- a/solution.py
+++ b/solution.py
@@ -647,6 +647,136 @@
 
 def plane_index():
     return lax.axis_index("seq") % (PLANE // lax.axis_size("row")) * lax.axis_size("row") + lax.axis_index("row")
+
+
+def head_kernel(blocks, own, codes, own_codes, positive, temp, w_col, loss_weight):
+    n = len(blocks)
+    T, C = own.shape
+    N = n * T
+    D = w_col.shape[0]
+    slots = NQ * QLEN
+
+    def kernel(ins, outs, scratch):
+        own, codes, own_codes, positive, temp, w_col = ins[n:]
+        grad, low, terms = outs
+        held, embeds = scratch
+        here = plane_index()
+        upper = lax.rem(lax.axis_index("seq") // (PLANE // lax.axis_size("row")), 2)
+
+        def place(c):
+            column = lax.rem(c // 2, 2) ^ upper
+            return pl.ds(pl.multiple_of((4 * column + 2 * lax.rem(c, 2) + c // 4) * T, 16), T)
+
+        for k in range(n):
+            held[place(here ^ k), :] = ins[k][...]
+        lane = lax.broadcasted_iota(jnp.int32, (1, C), 1)
+        slot = lax.broadcasted_iota(jnp.int32, (slots, 1), 0)
+        doc, own_doc = codes[0:1, :], own_codes[0:1, :]
+        select = jnp.where(codes[1:2, :] == slot, 1.0, 0.0).astype(BF)
+        own_select = jnp.where(own_codes[1:2, :] == slot, 1.0, 0.0).astype(BF)
+        rows = held[...].astype(F32)
+        mine = own[...]
+        heat = temp[...]
+        wanted = lane == positive[...]
+        valid = lane <= NSD
+        loss = jnp.zeros((1, 1), F32)
+        heat_grad = jnp.zeros((1, 1), F32)
+        total = jnp.zeros((T, C), F32)
+        for width in (C, C * 3 // 4, C // 2):
+            inside = lane < width
+            size = jnp.sum(jnp.where(inside, rows * rows, 0.0), axis=1, keepdims=True)
+            embed = jnp.where(inside, rows * lax.rsqrt(size + 1e-06), 0.0).astype(BF)
+            embeds[...] = embed
+            query = dot(select, embed).astype(BF)
+            powers = jnp.exp(SHARPNESS * dot_rt(query, embed))
+            soft = jnp.zeros((slots, C), F32)
+            sums = []
+            for d in range(NSD + 1):
+                sums.append(jnp.sum(jnp.where(doc == d, powers, 0.0), axis=1, keepdims=True))
+                soft = jnp.where(lane == d, jnp.log(sums[d]) / SHARPNESS, soft)
+            pair = jnp.sum(soft.reshape(NQ, QLEN, C), axis=1, keepdims=True)
+            pair = jnp.broadcast_to(pair, (NQ, QLEN, C)).reshape(slots, C)
+            logits = pair * heat / QLEN
+            masked = jnp.where(valid, logits, NEG_FILL)
+            top = jnp.max(masked, axis=1, keepdims=True)
+            shares = jnp.exp(masked - top)
+            share_sum = jnp.sum(shares, axis=1, keepdims=True)
+            chosen = jnp.sum(jnp.where(wanted, logits, 0.0), axis=1, keepdims=True)
+            losses = top + jnp.log(share_sum) - chosen
+            loss = loss + jnp.sum(losses, axis=0, keepdims=True) * (loss_weight / QLEN)
+            grad_logits = loss_weight * (shares / share_sum - jnp.where(wanted, 1.0, 0.0))
+            along = jnp.sum(jnp.where(valid, grad_logits * logits, 0.0), axis=1, keepdims=True)
+            heat_grad = heat_grad + jnp.sum(along, axis=0, keepdims=True) / QLEN
+            grad_soft = grad_logits * heat / QLEN
+            weight = jnp.zeros((slots, N), F32)
+            own_weight = jnp.zeros((slots, T), F32)
+            for d in range(NSD + 1):
+                ratio = grad_soft[:, d : d + 1] / sums[d]
+                weight = jnp.where(doc == d, ratio, weight)
+                own_weight = jnp.where(own_doc == d, ratio, own_weight)
+            grad_query = dot((powers * weight).astype(BF), embed)
+            own_embed = embeds[place(here), :]
+            own_powers = jnp.exp(SHARPNESS * dot_rt(query, own_embed))
+            grad_embed = dot_lt((own_powers * own_weight).astype(BF), query)
+            high = grad_query.astype(BF)
+            rest = (grad_query - high.astype(F32)).astype(BF)
+            grad_embed = grad_embed + dot_lt(own_select, high) + dot_lt(own_select, rest)
+            size = jnp.sum(jnp.where(inside, mine * mine, 0.0), axis=1, keepdims=True)
+            inverse = lax.rsqrt(size + 1e-06)
+            along = jnp.sum(jnp.where(inside, grad_embed * mine, 0.0), axis=1, keepdims=True)
+            part = inverse * grad_embed - mine * (inverse * inverse * inverse * along)
+            total = total + jnp.where(inside, part, 0.0)
+        low[...] = total.astype(BF)
+        grad[...] = dot_rt(total.astype(BF), w_col[...])
+        terms[...] = jnp.where(lane == 0, loss, jnp.where(lane == 1, heat_grad, 0.0))
+
+    outs = [((T, D), F32), ((T, C), BF), ((1, C), F32)]
+    ins = [near(item) for item in (*blocks, own, codes, own_codes, positive, temp, w_col)]
+    return call(kernel, ins, outs, [((N, C), BF), ((N, C), BF)], 24 * slots * N * C, 40)
+
+
+def swap_quarters(x):
+    q = x.shape[1] // 4
+    return jnp.concatenate([x[:, :q], x[:, 2 * q : 3 * q], x[:, q : 2 * q], x[:, 3 * q :]], axis=1)
+
+
+def pack_first(w, small):
+    rows, width = w.shape
+    D, wide = width // 3, width // 3 // PLANE
+    count = rows + small.shape[0]
+
+    def kernel(ins, outs, _):
+        w, small = ins
+        here = plane_index()
+        for k in range(PLANE):
+            out = outs[k % 2].at[k // 2]
+            for t in range(3):
+                columns = w[:, pl.ds(pl.multiple_of(t * D + (here ^ k) * wide, 128), wide)]
+                out[:rows, t * wide : (t + 1) * wide] = swap_quarters(columns) if t < 2 else columns
+            out[rows:] = small[...]
+
+    outs = [((PLANE // 2, count, 3 * wide), BF)] * 2
+    return call(kernel, [near(w), near(small)], outs, [], w.size, SMALL)
+
+
+def unpack_first(even, core, got, out_rows):
+    rows, D = out_rows.shape
+    count, cols = even.shape[1:]
+    wide = cols // 3
+
+    def kernel(ins, outs, _):
+        even, core, *got, out_rows = ins
+        block, below = outs
+        here = plane_index()
+        blocks = [even.at[0], core.at[0]] + [ref.at[j] for ref in got for j in range(2)]
+        for k in range(PLANE):
+            of = here ^ k
+            block[pl.ds(pl.multiple_of(of * rows, 16), rows), :cols] = blocks[k][:rows]
+            below[of] = blocks[k][rows:]
+            block[k * rows : (k + 1) * rows, cols:] = out_rows[:, k * wide : (k + 1) * wide]
+
+    outs = [((PLANE * rows, cols + wide), BF), ((PLANE, count - rows, cols), BF)]
+    return call(kernel, [near(item) for item in (even, core, *got, out_rows)], outs, [], even.size, SMALL)
 
 
 def pack_shares(sums, others, ffn, lines, in_cols, hidden_cols):
@@ -821,9 +951,9 @@
     to_group = [(b, (b % O) * PLANE + b // O) for b in range(O * PLANE)]
     from_group = [(d, b) for b, d in to_group]
     small = jnp.concatenate([norm_gains.reshape(-1), biases.reshape(-1), colbert.reshape(-1)])
-    small = jnp.broadcast_to(padded_rows(small, in_cols), (PLANE, *padded_rows(small, in_cols).shape))
-    first_in = plane_exchange(jnp.concatenate([pack_columns(attn_in[0]), small], axis=1), relative)
-    first_in, small = first_in[:, :in_rows].reshape(rows_in, in_cols), first_in[:, in_rows:].reshape(PLANE, -1)
+    even, odd = pack_first(attn_in[0], padded_rows(small, in_cols))
+    core = across(odd, 1)
+    got = tie(*[across(jnp.stack([even[k], core[k]]), 2 * k) for k in (1, 2, 3)])
     shard_out = lax.ppermute(attn_out, BOTH, to_group)
     table = turned(jnp.concatenate([seg_lengths[0], seg_kinds[0], pairing[0]]))
     seg_count = seg_lengths.shape[1]
@@ -838,9 +968,9 @@
     def gather_far(x):
         return lax.all_gather(x, "seq", axis=0, axis_index_groups=along_z)
 
-    own = attn_block(0, first_in)
+    own, small = unpack_first(even, core, got, shard_out[0])
+    small = small.reshape(PLANE, -1)
     full_attn = [gather_far(own)]
-
     count_small = L * part
     col_plane = small[:, count_small : count_small + colbert.size].reshape(-1)
     params = small[None, :, :count_small]
@@ -912,59 +1042,24 @@
     hidden_out = turned(hidden_low, True)
 
     full_width = w_col.shape[1]
-    part_widths = (full_width, full_width * 3 // 4, full_width // 2)
-    query_total = NQ * QLEN
-    doc_total = NSD + 1
+    row_positions = jnp.arange(N, dtype=jnp.int32)
+    segment, offset, is_query, query_slot, doc_num = token_info(row_positions, lengths, kinds)
+    codes = jnp.stack([jnp.where(is_query == 0, doc_num, -1), jnp.where(is_query == 1, query_slot, -1)])
+    own_codes = lax.dynamic_slice(codes, (0, block_at[0] * T), (2, T))
+    positive = jnp.repeat(pairs_of, QLEN)[:, None]
+    temp = jnp.exp(log_scale)[None]
     hidden_low, cot = tie(hidden_low, cotangent[0])
     cot = turned(cot)
     col = dot(hidden_low, w_col)
-    in_order = jnp.arange(PLANE, dtype=jnp.int32)
-    in_order = 4 * (in_order % 2) + 2 * ((in_order // 4) ^ (far % 2)) + in_order // 2 % 2
-    in_order = jnp.bitwise_xor(in_order, plane)
-    col_row = pick(jnp.stack(plane_gather(col.astype(BF))), in_order, axis=0).reshape(N, full_width).astype(F32)
-    own_at = block_at[0] * T
-    row_positions = jnp.arange(N, dtype=jnp.int32)
-    segment, offset, is_query, query_slot, doc_num = token_info(row_positions, lengths, kinds)
-    slots = jnp.arange(query_total, dtype=jnp.int32)[:, None]
-    selector = (is_query == 1)[None, :] & (query_slot[None, :] == slots)
-    selector_low = selector.astype(BF)
-    own_selector = lax.dynamic_slice(selector.astype(F32), (0, own_at), (query_total, T))
-    embeds = [unit_rows(col_row[:, :width]).astype(BF) for width in part_widths]
-    query_emb = [dot(selector_low, embed).astype(BF) for embed in embeds]
-    powers = jnp.exp(SHARPNESS * jnp.stack([dot_rt(query_emb[m], embeds[m]) for m in range(3)]))
-    doc_code = jnp.where(is_query == 0, doc_num, -1)[None, None, :]
-    totals = jnp.stack([jnp.sum(jnp.where(doc_code == d, powers, 0.0), axis=2) for d in range(doc_total)], axis=2)
-    soft = jnp.log(totals) / SHARPNESS
-    pair_sum = jnp.sum(soft.reshape(3, NQ, QLEN, doc_total), axis=2)
-    inverse_temp = jnp.exp(log_scale[0])
-    logits = pair_sum * inverse_temp / QLEN
-    positive = pairs_of[None, :, None] == jnp.arange(doc_total, dtype=jnp.int32)[None, None, :]
-    losses = jax.nn.logsumexp(logits, axis=-1) - jnp.sum(jnp.where(positive, logits, 0.0), axis=-1)
-    loss_weight = 1.0 / (3 * NQ * R)
-    grad_logits = loss_weight * (jax.nn.softmax(logits, axis=-1) - positive.astype(F32))
-    loss_terms = jnp.stack([jnp.sum(losses) * loss_weight, jnp.sum(grad_logits * logits)])
-    grad_pairs = grad_logits * inverse_temp / QLEN
-    grad_soft = jnp.broadcast_to(grad_pairs[:, :, None, :], (3, NQ, QLEN, doc_total)).reshape(
-        3, query_total, doc_total
+    col_blocks = plane_gather(col.astype(BF))
+    grad_out, grad_col_low, terms = head_kernel(
+        col_blocks, col, codes, own_codes, positive, temp, w_col, 1.0 / (3 * NQ * R)
     )
-    ratio = grad_soft / totals
-    weight = sum(jnp.where(doc_code == d, ratio[:, :, d : d + 1], 0.0) for d in range(doc_total))
-    grad_sims = (powers * weight).astype(BF)
-    own_sims = lax.dynamic_slice(grad_sims, (0, 0, own_at), (3, query_total, T))
-    grad_col = jnp.zeros((T, full_width), F32)
-    for m in range(3):
-        width = part_widths[m]
-        grad_query = dot(grad_sims[m], embeds[m])
-        grad_embed = dot_lt(own_sims[m], query_emb[m]) + lax.dot_general(
-            own_selector, grad_query, (((0,), (0,)), ((), ())), precision=HIGHEST, preferred_element_type=F32
-        )
-        pull_unit = jax.vjp(unit_rows, col[:, :width])[1]
-        grad_col = grad_col + jnp.pad(pull_unit(grad_embed)[0], ((0, 0), (0, full_width - width)))
-    grad_col_low, cot = tie(grad_col.astype(BF), cot)
+    loss_terms = terms[0, :2]
     col_parts = dot_lt(hidden_low, grad_col_low).reshape(O, PLANE, in_rows, full_width).transpose(1, 0, 2, 3)
     col_parts = plane_sum(pick(col_parts.reshape(PLANE, O * in_rows, full_width), relative, axis=0))
     col_rows = jax.vmap(padded_rows)(col_parts.reshape(O, in_rows * full_width)).astype(BF)
-    grad_parts = [cot, dot_rt(grad_col_low, w_col)]
+    grad_parts = [cot, grad_out]
 
     def scatter_far(whole):
         whole = whole.reshape(-1, whole.shape[-1])

time: 594 us -> 578 us (0.973)
  other arithmetic: 25.3 us -> 13.7 us
  local copies, waits for them, and re-layouts: 61.5 us -> 51.2 us
  Pallas kernels: 133 us -> 139 us
  waiting for transfers between devices: 208 us -> 214 us
    pallas_call x30 -> x33, Pallas kernels: 133 us -> 139 us  [call(): pl.pallas_call(wrapped, in_specs=[IN_VMEM if kind == 'near' else IN_HBM f...]
    unnamed x316 -> x279, local copies, waits for them, and re-layouts: 35 us -> 33.9 us
  transfers between devices with their start and end apart: 134 -> 134, of which waited for: 62 -> 59; matrix products, arithmetic and copies ran while one was open for 9% -> 5% of each run, Pallas kernels for 19% -> 21%
where the time goes in v4:
time: 578 us; the launch traced here: 571 us
  waiting for transfers between devices  214 us (37%)
  Pallas kernels  139 us (24%)
  starting transfers between devices  136 us (24%)
  local copies, waits for them, and re-layouts  51.2 us (9%)
  between operations  17.2 us (3%)
  other arithmetic  13.7 us (2%)
    ppermute x119, waiting for transfers between devices, across(): return lax.ppermute(x, BOTH, [(d, d ^ mask) for d in range(size)])  213 us
    pallas_call x33, Pallas kernels, call(): pl.pallas_call(wrapped, in_specs=[IN_VMEM if kind == 'near' else IN_HBM f...  139 us
    ppermute x119, starting transfers between devices, across(): return lax.ppermute(x, BOTH, [(d, d ^ mask) for d in range(size)])  125 us
    unnamed x279, local copies, waits for them, and re-layouts  33.9 us
  transfers between devices with their start and end apart: 134, of which 59 were waited for; matrix products, arithmetic and copies ran while one was open for 5% of the time, Pallas kernels for 21%

profile of v4, /device:TPU:0, one launch (start us, length us, event | category | flops | bytes accessed | tf_op | source)
XLA Modules:
  0.0 571.0 jit_solution(2548573123346863465)
XLA Ops:
  24.9 8.2 %collective-permute-start.11 = (bf16[2,48,384]{2,1,0:T(8,128)(2,1)S(1)}, bf16[2,48,384]{2,1,0:T(8,128)(2,1)S(1)}, u32[]{:S(2)}, u32[]{:S(2)}) collective-permute-start(bf16[2,48,384]{2,1,0:T(8,128)(2,1)S(1)} %pad_maximum_fusion.13), channel_id=1, source_target_pairs={{0,6},{1,7},{2,4},{3,5},{4,2},{5,3},{6,0},{7,1},{8,14},{9,15},{10,... | collective-permute-start | bytes 221192 | tf_op jit(solution)/shard_map/ppermute | solution.py:39
  78.9 10.4 %shard_map.214 = (bf16[1152,384]{1,0:T(8,128)(2,1)}, bf16[1152,128]{1,0:T(8,128)(2,1)}, f32[2,1152]{1,0:T(2,128)}, bf16[4,144,1024]{2,1,0:T(8,128)(2,1)}, bf16[4,144,1024]{2,1,0:T(8,128)(2,1)}) custom-call(bf16[144,1024]{1,0:T(8,128)(2,1)} %copy-done.1, bf16[144,1024]{1,0:T(8,128)(2,1)} %copy-done.64, bf16[144,1024]{1,0:T(8,128)(2,1)} %copy-done.61, ...), custom_call_target="tpu_custom_call" | custom-call | flops 2566914048 | bytes 7553536 | tf_op jit(solution)/shard_map/pallas_call | solution.py:213
  97.6 6.3 %collective-permute-done.17.refs_2_ = bf16[144,1024]{1,0:T(8,128)(2,1)S(1)} collective-permute-done((bf16[144,1024]{1,0:T(8,128)(2,1)S(1)}, bf16[144,1024]{1,0:T(8,128)(2,1)S(1)}, u32[]{:S(2)}, u32[]{:S(2)}) %collective-permute-start.17) | collective-permute-done | bytes 294944 | tf_op jit(solution)/shard_map/ppermute | solution.py:39
  128.9 8.0 %shard_map.217 = (bf16[1152,512]{1,0:T(8,128)(2,1)}, bf16[1152,512]{1,0:T(8,128)(2,1)}, bf16[4,144,1024]{2,1,0:T(8,128)(2,1)}, bf16[4,144,1024]{2,1,0:T(8,128)(2,1)}) custom-call(bf16[144,1024]{1,0:T(8,128)(2,1)} %copy-done.31, bf16[144,1024]{1,0:T(8,128)(2,1)} %copy-done.70, bf16[144,1024]{1,0:T(8,128)(2,1)} %copy-done.67, bf16[144,1024]{1,0:T(8,128)(2,1)} %copy-done.71, ...), custom_call_target="tpu_custom_call" | custom-call | flops 2415919104 | bytes 9179136 | tf_op jit(solution)/shard_map/pallas_call | solution.py:213
  144.1 6.3 %collective-permute-done.32.refs_2_ = bf16[144,1024]{1,0:T(8,128)(2,1)S(1)} collective-permute-done((bf16[144,1024]{1,0:T(8,128)(2,1)S(1)}, bf16[144,1024]{1,0:T(8,128)(2,1)S(1)}, u32[]{:S(2)}, u32[]{:S(2)}) %collective-permute-start.32) | collective-permute-done | bytes 294944 | tf_op jit(solution)/shard_map/ppermute | solution.py:39
  161.9 6.5 %collective-permute-done.36.refs_2_ = bf16[144,1024]{1,0:T(8,128)(2,1)S(1)} collective-permute-done((bf16[144,1024]{1,0:T(8,128)(2,1)S(1)}, bf16[144,1024]{1,0:T(8,128)(2,1)S(1)}, u32[]{:S(2)}, u32[]{:S(2)}) %collective-permute-start.36) | collective-permute-done | bytes 294944 | tf_op jit(solution)/shard_map/ppermute | solution.py:39
  168.4 5.8 %collective-permute-done.38.refs_4_ = bf16[144,1024]{1,0:T(8,128)(2,1)S(1)} collective-permute-done((bf16[144,1024]{1,0:T(8,128)(2,1)S(1)}, bf16[144,1024]{1,0:T(8,128)(2,1)S(1)}, u32[]{:S(2)}, u32[]{:S(2)}) %collective-permute-start.38) | collective-permute-done | bytes 294944 | tf_op jit(solution)/shard_map/ppermute | solution.py:39
  177.3 10.4 %shard_map.220 = (bf16[1152,384]{1,0:T(8,128)(2,1)}, bf16[1152,128]{1,0:T(8,128)(2,1)}, f32[2,1152]{1,0:T(2,128)}, bf16[4,144,1024]{2,1,0:T(8,128)(2,1)}, bf16[4,144,1024]{2,1,0:T(8,128)(2,1)}) custom-call(bf16[144,1024]{1,0:T(8,128)(2,1)} %copy-done.32, bf16[144,1024]{1,0:T(8,128)(2,1)} %copy-done.76, bf16[144,1024]{1,0:T(8,128)(2,1)} %copy-done.73, ...), custom_call_target="tpu_custom_call" | custom-call | flops 2566914048 | bytes 7553536 | tf_op jit(solution)/shard_map/pallas_call | solution.py:213
  195.9 6.4 %collective-permute-done.43.refs_2_ = bf16[144,1024]{1,0:T(8,128)(2,1)S(1)} collective-permute-done((bf16[144,1024]{1,0:T(8,128)(2,1)S(1)}, bf16[144,1024]{1,0:T(8,128)(2,1)S(1)}, u32[]{:S(2)}, u32[]{:S(2)}) %collective-permute-start.43) | collective-permute-done | bytes 294944 | tf_op jit(solution)/shard_map/ppermute | solution.py:39
  213.0 6.5 %collective-permute-done.47.refs_2_ = bf16[144,1024]{1,0:T(8,128)(2,1)S(1)} collective-permute-done((bf16[144,1024]{1,0:T(8,128)(2,1)S(1)}, bf16[144,1024]{1,0:T(8,128)(2,1)S(1)}, u32[]{:S(2)}, u32[]{:S(2)}) %collective-permute-start.47) | collective-permute-done | bytes 294944 | tf_op jit(solution)/shard_map/ppermute | solution.py:39
  228.1 8.0 %shard_map.223 = (bf16[1152,512]{1,0:T(8,128)(2,1)}, bf16[1152,512]{1,0:T(8,128)(2,1)}, bf16[4,144,1024]{2,1,0:T(8,128)(2,1)}, bf16[4,144,1024]{2,1,0:T(8,128)(2,1)}) custom-call(bf16[144,1024]{1,0:T(8,128)(2,1)} %copy-done.33, bf16[144,1024]{1,0:T(8,128)(2,1)} %copy-done.83, bf16[144,1024]{1,0:T(8,128)(2,1)} %copy-done.80, bf16[144,1024]{1,0:T(8,128)(2,1)} %copy-done.84, ...), custom_call_target="tpu_custom_call" | custom-call | flops 2415919104 | bytes 9441280 | tf_op jit(solution)/shard_map/pallas_call | solution.py:213
  295.3 7.2 %shard_map.228 = (bf16[1152,512]{1,0:T(8,128)(2,1)}, f32[1,512]{1,0:T(1,128)}, bf16[4,144,1024]{2,1,0:T(8,128)(2,1)}, bf16[4,144,1024]{2,1,0:T(8,128)(2,1)}) custom-call(bf16[144,1024]{1,0:T(8,128)(2,1)} %copy-done.34, bf16[144,1024]{1,0:T(8,128)(2,1)} %copy-done.90, bf16[144,1024]{1,0:T(8,128)(2,1)} %copy-done.87, bf16[144,1024]{1,0:T(8,128)(2,1)} %copy-done.91, ...), custom_call_target="tpu_custom_call" | custom-call | flops 2415919104 | bytes 9439232 | tf_op jit(solution)/shard_map/pallas_call | solution.py:213
  316.3 8.5 %shard_map.230 = bf16[4,272,1024]{2,1,0:T(8,128)(2,1)} custom-call(bf16[144,1024]{1,0:T(8,128)(2,1)} %copy-done.33, bf16[144,1024]{1,0:T(8,128)(2,1)} %copy-done.83, bf16[144,1024]{1,0:T(8,128)(2,1)} %copy-done.80, bf16[144,1024]{1,0:T(8,128)(2,1)} %copy-done.84, bf16[144,1024]{1,0:T(8,128)(2,1)} %copy-done.81, bf16[144,1024]{1,0:T(8,128)(2,1)} %copy-done.85, ...), custom_call_target="tpu_custom_call" | custom-call | flops 2415919104 | bytes 9437184 | tf_op jit(solution)/shard_map/pallas_call | solution.py:213
  348.6 17.2 %shard_map.232 = (bf16[1152,384]{1,0:T(8,128)(2,1)}, f32[1,384]{1,0:T(1,128)}, bf16[4,144,1024]{2,1,0:T(8,128)(2,1)}, bf16[4,144,1024]{2,1,0:T(8,128)(2,1)}) custom-call(bf16[144,1024]{1,0:T(8,128)(2,1)} %copy-done.37, bf16[144,1024]{1,0:T(8,128)(2,1)} %copy-done.107, bf16[144,1024]{1,0:T(8,128)(2,1)} %copy-done.103, bf16[144,1024]{1,0:T(8,128)(2,1)} %copy-done.109, ...), custom_call_target="tpu_custom_call" | custom-call | flops 4605345792 | bytes 8436736 | tf_op jit(solution)/shard_map/pallas_call | solution.py:213
  375.6 6.8 %shard_map.234 = bf16[4,272,512]{2,1,0:T(8,128)(2,1)} custom-call(bf16[144,1024]{1,0:T(8,128)(2,1)} %copy-done.32, bf16[144,1024]{1,0:T(8,128)(2,1)} %copy-done.76, bf16[144,1024]{1,0:T(8,128)(2,1)} %copy-done.73, bf16[144,1024]{1,0:T(8,128)(2,1)} %copy-done.77, bf16[144,1024]{1,0:T(8,128)(2,1)} %copy-done.74, bf16[144,1024]{1,0:T(8,128)(2,1)} %copy-done.78, ...), custom_call_target="tpu_custom_call" | custom-call | flops 1207959552 | bytes 7013888 | tf_op jit(solution)/shard_map/pallas_call | solution.py:213
  398.2 6.1 %collective-permute-done.93.refs_2_.refs_10_ = bf16[144,1024]{1,0:T(8,128)(2,1)S(1)} collective-permute-done((bf16[144,1024]{1,0:T(8,128)(2,1)S(1)}, bf16[144,1024]{1,0:T(8,128)(2,1)S(1)}, u32[]{:S(2)}, u32[]{:S(2)}) %collective-permute-start.93) | collective-permute-done | bytes 294944 | tf_op jit(solution)/shard_map/ppermute | solution.py:39
  411.5 7.2 %shard_map.236 = (bf16[1152,512]{1,0:T(8,128)(2,1)}, f32[1,512]{1,0:T(1,128)}, bf16[4,144,1024]{2,1,0:T(8,128)(2,1)}, bf16[4,144,1024]{2,1,0:T(8,128)(2,1)}) custom-call(bf16[144,1024]{1,0:T(8,128)(2,1)} %copy-done.36, bf16[144,1024]{1,0:T(8,128)(2,1)} %copy-done.108, bf16[144,1024]{1,0:T(8,128)(2,1)} %copy-done.99, bf16[144,1024]{1,0:T(8,128)(2,1)} %copy-done.110, ...), custom_call_target="tpu_custom_call" | custom-call | flops 2415919104 | bytes 9177088 | tf_op jit(solution)/shard_map/pallas_call | solution.py:213
  427.6 8.5 %shard_map.238 = bf16[4,256,1024]{2,1,0:T(8,128)(2,1)} custom-call(bf16[144,1024]{1,0:T(8,128)(2,1)} %copy-done.31, bf16[144,1024]{1,0:T(8,128)(2,1)} %copy-done.70, bf16[144,1024]{1,0:T(8,128)(2,1)} %copy-done.67, bf16[144,1024]{1,0:T(8,128)(2,1)} %copy-done.71, bf16[144,1024]{1,0:T(8,128)(2,1)} %copy-done.68, bf16[144,1024]{1,0:T(8,128)(2,1)} %copy-done.72, ...), custom_call_target="tpu_custom_call" | custom-call | flops 2415919104 | bytes 9175040 | tf_op jit(solution)/shard_map/pallas_call | solution.py:213
  449.9 6.2 %collective-permute-done.104.refs_2_.refs_10_ = bf16[144,1024]{1,0:T(8,128)(2,1)S(1)} collective-permute-done((bf16[144,1024]{1,0:T(8,128)(2,1)S(1)}, bf16[144,1024]{1,0:T(8,128)(2,1)S(1)}, u32[]{:S(2)}, u32[]{:S(2)}) %collective-permute-start.104) | collective-permute-done | bytes 294944 | tf_op jit(solution)/shard_map/ppermute | solution.py:39
  463.3 17.1 %shard_map.240 = (bf16[1152,384]{1,0:T(8,128)(2,1)}, f32[1,384]{1,0:T(1,128)}, bf16[4,144,1024]{2,1,0:T(8,128)(2,1)}, bf16[4,144,1024]{2,1,0:T(8,128)(2,1)}) custom-call(bf16[144,1024]{1,0:T(8,128)(2,1)} %copy-done.35, bf16[144,1024]{1,0:T(8,128)(2,1)} %copy-done.97, bf16[144,1024]{1,0:T(8,128)(2,1)} %copy-done.93, bf16[144,1024]{1,0:T(8,128)(2,1)} %copy-done.98, ...), custom_call_target="tpu_custom_call" | custom-call | flops 4605345792 | bytes 8436736 | tf_op jit(solution)/shard_map/pallas_call | solution.py:213
  482.3 6.9 %shard_map.241 = (bf16[272,512]{1,0:T(8,128)(2,1)}, bf16[272,512]{1,0:T(8,128)(2,1)}, bf16[272,512]{1,0:T(8,128)(2,1)}, bf16[272,512]{1,0:T(8,128)(2,1)}) custom-call(bf16[144,1024]{1,0:T(8,128)(2,1)} %copy-done.1, bf16[144,1024]{1,0:T(8,128)(2,1)} %copy-done.64, bf16[144,1024]{1,0:T(8,128)(2,1)} %copy-done.61, bf16[144,1024]{1,0:T(8,128)(2,1)} %copy-done.65, ...), custom_call_target="tpu_custom_call" | custom-call | flops 1207959552 | bytes 7013888 | tf_op jit(solution)/shard_map/pallas_call | solution.py:213
  503.1 16.0 %collective-permute-done.112.refs_2_ = bf16[272,512]{1,0:T(8,128)(2,1)S(1)} collective-permute-done((bf16[272,512]{1,0:T(8,128)(2,1)}, bf16[272,512]{1,0:T(8,128)(2,1)S(1)}, u32[]{:S(2)}, u32[]{:S(2)}) %collective-permute-start.112) | collective-permute-done | bytes 278560 | tf_op jit(solution)/shard_map/ppermute | solution.py:39
  522.3 6.3 %collective-permute-start.117 = (bf16[4,32,1920]{2,1,0:T(8,128)(2,1)S(1)}, bf16[4,32,1920]{2,1,0:T(8,128)(2,1)S(1)}, u32[]{:S(2)}, u32[]{:S(2)}) collective-permute-start(bf16[4,32,1920]{2,1,0:T(8,128)(2,1)S(1)} %get-tuple-element.332), channel_id=1, source_target_pairs={{0,1},{1,0},{2,3},{3,2},{4,5},{5,4},{6,7},{7,6},{8,9},{9,8},{10,11... | collective-permute-start | bytes 1474568 | tf_op jit(solution)/shard_map/ppermute | solution.py:39
  530.2 9.0 %collective-permute-start.121 = (bf16[2,32,1920]{2,1,0:T(8,128)(2,1)S(1)}, bf16[2,32,1920]{2,1,0:T(8,128)(2,1)S(1)}, u32[]{:S(2)}, u32[]{:S(2)}) collective-permute-start(bf16[2,32,1920]{2,1,0:T(8,128)(2,1)S(1)} %pad_maximum_fusion.7), channel_id=1, source_target_pairs={{0,6},{1,7},{2,4},{3,5},{4,2},{5,3},{6,0},{7,1},{8,14},{9,15},{10,... | collective-permute-start | bytes 737288 | tf_op jit(solution)/shard_map/ppermute | solution.py:39
  (717 shorter events, 348.1 us)
Async XLA Ops:
  7.2 71.7 %all-gather.9.cloned.1.call-start = ((), (), s32[]{:S(2)}) async-start(), calls=%async_computation.6 | async-start | bytes 1310720 | tf_op jit(solution)/shard_map/all_gather | solution.py:969
  11.7 27.3 %collective-permute-start.27 = (bf16[4,32,1408]{2,1,0:T(8,128)(2,1)}, bf16[4,32,1408]{2,1,0:T(8,128)(2,1)}, u32[]{:S(2)}, u32[]{:S(2)}) collective-permute-start(bf16[4,32,1408]{2,1,0:T(8,128)(2,1)} %slice.291), channel_id=1, source_target_pairs={{0,1},{1,0},{2,3},{3,2},{4,5},{5,4},{6,7},{7,6},{8,9},{9,8},{10,11... | collective-permute-start | bytes 1081352 | tf_op jit(solution)/shard_map/ppermute | solution.py:39
  12.7 20.3 %collective-permute-start.12 = (bf16[2,32,1024]{2,1,0:T(8,128)(2,1)}, bf16[2,32,1024]{2,1,0:T(8,128)(2,1)}, u32[]{:S(2)}, u32[]{:S(2)}) collective-permute-start(bf16[2,32,1024]{2,1,0:T(8,128)(2,1)} %param.15), channel_id=1, source_target_pairs={{0,0},{1,8},{2,16},{3,24},{4,1},{5,9},{6,17},{7,25},{8,2},{9,10},{... | collective-permute-start | bytes 393224 | tf_op jit(solution)/shard_map/ppermute | solution.py:957
  15.6 45.3 %collective-permute-start = (bf16[144,1024]{1,0:T(8,128)(2,1)}, bf16[144,1024]{1,0:T(8,128)(2,1)S(1)}, u32[]{:S(2)}, u32[]{:S(2)}) collective-permute-start(bf16[144,1024]{1,0:T(8,128)(2,1)} %bitcast), channel_id=1, source_target_pairs={{0,0},{1,16},{2,10},{3,26},{4,4},{5,20},{6,14},{7,30},{8,1},{9,17}... | collective-permute-start | bytes 884744 | tf_op jit(solution)/shard_map/ppermute | solution.py:49
  39.0 88.8 %all-gather.11.cloned.1.call-start = ((), (), s32[]{:S(2)}) async-start(), calls=%async_computation.7 | async-start | bytes 2621440 | tf_op jit(solution)/shard_map/all_gather | solution.py:969
  55.2 119.5 %all-gather.13.cloned.1.call-start = ((), (), s32[]{:S(2)}) async-start(), calls=%async_computation.8 | async-start | bytes 1310720 | tf_op jit(solution)/shard_map/all_gather | solution.py:969
  94.4 15.1 %collective-permute-start.18 = (bf16[144,1024]{1,0:T(8,128)(2,1)S(1)}, bf16[144,1024]{1,0:T(8,128)(2,1)S(1)}, u32[]{:S(2)}, u32[]{:S(2)}) collective-permute-start(bf16[144,1024]{1,0:T(8,128)(2,1)S(1)} %get-tuple-element.191), channel_id=1, source_target_pairs={{0,4},{1,5},{2,6},{3,7},{4,0},{5,1},{6,2},{7,3},{8,12},{9,13},{10,... | collective-permute-start | bytes 884744 | tf_op jit(solution)/shard_map/ppermute | solution.py:39
  116.2 109.5 %all-gather.15.cloned.1.call-start = ((), (), s32[]{:S(2)}) async-start(), calls=%async_computation.9 | async-start | bytes 2949120 | tf_op jit(solution)/shard_map/all_gather | solution.py:969
  140.2 249.3 %reduce-scatter.4.cloned.1.call-start = ((), (), s32[]{:S(2)}) async-start(), calls=%async_computation.3 | async-start | bytes 2785280 | tf_op jit(solution)/shard_map/reduce_scatter | solution.py:1066
  141.1 15.2 %collective-permute-start.33 = (bf16[144,1024]{1,0:T(8,128)(2,1)S(1)}, bf16[144,1024]{1,0:T(8,128)(2,1)S(1)}, u32[]{:S(2)}, u32[]{:S(2)}) collective-permute-start(bf16[144,1024]{1,0:T(8,128)(2,1)S(1)} %get-tuple-element.202), channel_id=1, source_target_pairs={{0,4},{1,5},{2,6},{3,7},{4,0},{5,1},{6,2},{7,3},{8,12},{9,13},{10,... | collective-permute-start | bytes 884744 | tf_op jit(solution)/shard_map/ppermute | solution.py:39
  192.8 15.1 %collective-permute-start.44 = (bf16[144,1024]{1,0:T(8,128)(2,1)S(1)}, bf16[144,1024]{1,0:T(8,128)(2,1)S(1)}, u32[]{:S(2)}, u32[]{:S(2)}) collective-permute-start(bf16[144,1024]{1,0:T(8,128)(2,1)S(1)} %get-tuple-element.210), channel_id=1, source_target_pairs={{0,4},{1,5},{2,6},{3,7},{4,0},{5,1},{6,2},{7,3},{8,12},{9,13},{10,... | collective-permute-start | bytes 884744 | tf_op jit(solution)/shard_map/ppermute | solution.py:39
  242.7 15.3 %collective-permute-start.55 = (bf16[144,1024]{1,0:T(8,128)(2,1)}, bf16[144,1024]{1,0:T(8,128)(2,1)S(1)}, u32[]{:S(2)}, u32[]{:S(2)}) collective-permute-start(bf16[144,1024]{1,0:T(8,128)(2,1)} %get-tuple-element.218), channel_id=1, source_target_pairs={{0,4},{1,5},{2,6},{3,7},{4,0},{5,1},{6,2},{7,3},{8,12},{9,13},{10,... | collective-permute-start | bytes 884744 | tf_op jit(solution)/shard_map/ppermute | solution.py:39
  328.5 132.7 %reduce-scatter.6.cloned.1.call-start = ((), (), s32[]{:S(2)}) async-start(), calls=%async_computation.4 | async-start | bytes 1392640 | tf_op jit(solution)/shard_map/reduce_scatter | solution.py:1066
  373.4 15.3 %collective-permute-start.90 = (bf16[144,1024]{1,0:T(8,128)(2,1)}, bf16[144,1024]{1,0:T(8,128)(2,1)S(1)}, u32[]{:S(2)}, u32[]{:S(2)}) collective-permute-start(bf16[144,1024]{1,0:T(8,128)(2,1)} %get-tuple-element.259), channel_id=1, source_target_pairs={{0,4},{1,5},{2,6},{3,7},{4,0},{5,1},{6,2},{7,3},{8,12},{9,13},{10,... | collective-permute-start | bytes 884744 | tf_op jit(solution)/shard_map/ppermute | solution.py:39
  374.0 15.4 %collective-permute-start.91 = (bf16[144,1024]{1,0:T(8,128)(2,1)}, bf16[144,1024]{1,0:T(8,128)(2,1)}, u32[]{:S(2)}, u32[]{:S(2)}) collective-permute-start(bf16[144,1024]{1,0:T(8,128)(2,1)} %get-tuple-element.260), channel_id=1, source_target_pairs={{0,6},{1,7},{2,4},{3,5},{4,2},{5,3},{6,0},{7,1},{8,14},{9,15},{10,... | collective-permute-start | bytes 884744 | tf_op jit(solution)/shard_map/ppermute | solution.py:39
  397.9 121.9 %reduce-scatter.8.cloned.1.call-start = ((), (), s32[]{:S(2)}) async-start(), calls=%async_computation.5 | async-start | bytes 2621440 | tf_op jit(solution)/shard_map/reduce_scatter | solution.py:1066
  425.5 15.3 %collective-permute-start.101 = (bf16[144,1024]{1,0:T(8,128)(2,1)}, bf16[144,1024]{1,0:T(8,128)(2,1)S(1)}, u32[]{:S(2)}, u32[]{:S(2)}) collective-permute-start(bf16[144,1024]{1,0:T(8,128)(2,1)} %get-tuple-element.279), channel_id=1, source_target_pairs={{0,4},{1,5},{2,6},{3,7},{4,0},{5,1},{6,2},{7,3},{8,12},{9,13},{10,... | collective-permute-start | bytes 884744 | tf_op jit(solution)/shard_map/ppermute | solution.py:39
  491.5 28.2 %collective-permute-start.114 = (bf16[144,1024]{1,0:T(8,128)(2,1)}, bf16[144,1024]{1,0:T(8,128)(2,1)S(1)}, u32[]{:S(2)}, u32[]{:S(2)}) collective-permute-start(bf16[144,1024]{1,0:T(8,128)(2,1)} %get-tuple-element.324), channel_id=1, source_target_pairs={{0,2},{1,3},{2,0},{3,1},{4,6},{5,7},{6,4},{7,5},{8,10},{9,11},{10,... | collective-permute-start | bytes 884744 | tf_op jit(solution)/shard_map/ppermute | solution.py:39
  492.8 27.0 %collective-permute-start.115 = (bf16[144,1024]{1,0:T(8,128)(2,1)}, bf16[144,1024]{1,0:T(8,128)(2,1)}, u32[]{:S(2)}, u32[]{:S(2)}) collective-permute-start(bf16[144,1024]{1,0:T(8,128)(2,1)} %get-tuple-element.325), channel_id=1, source_target_pairs={{0,4},{1,5},{2,6},{3,7},{4,0},{5,1},{6,2},{7,3},{8,12},{9,13},{10,... | collective-permute-start | bytes 884744 | tf_op jit(solution)/shard_map/ppermute | solution.py:39
  492.9 26.9 %collective-permute-start.116 = (bf16[144,1024]{1,0:T(8,128)(2,1)}, bf16[144,1024]{1,0:T(8,128)(2,1)}, u32[]{:S(2)}, u32[]{:S(2)}) collective-permute-start(bf16[144,1024]{1,0:T(8,128)(2,1)} %get-tuple-element.326), channel_id=1, source_target_pairs={{0,6},{1,7},{2,4},{3,5},{4,2},{5,3},{6,0},{7,1},{8,14},{9,15},{10,... | collective-permute-start | bytes 884744 | tf_op jit(solution)/shard_map/ppermute | solution.py:39
  495.0 24.1 %collective-permute-start.112 = (bf16[272,512]{1,0:T(8,128)(2,1)}, bf16[272,512]{1,0:T(8,128)(2,1)S(1)}, u32[]{:S(2)}, u32[]{:S(2)}) collective-permute-start(bf16[272,512]{1,0:T(8,128)(2,1)} %get-tuple-element.309), channel_id=1, source_target_pairs={{0,16},{1,17},{2,18},{3,19},{4,20},{5,21},{6,22},{7,23},{8,24},{9,... | collective-permute-start | bytes 835592 | tf_op jit(solution)/shard_map/ppermute | solution.py:39
  499.4 20.3 %collective-permute-start.113 = (bf16[272,512]{1,0:T(8,128)(2,1)}, bf16[272,512]{1,0:T(8,128)(2,1)S(1)}, u32[]{:S(2)}, u32[]{:S(2)}) collective-permute-start(bf16[272,512]{1,0:T(8,128)(2,1)} %get-tuple-element.310), channel_id=1, source_target_pairs={{0,24},{1,25},{2,26},{3,27},{4,28},{5,29},{6,30},{7,31},{8,16},{9,... | collective-permute-start | bytes 835592 | tf_op jit(solution)/shard_map/ppermute | solution.py:39
  519.1 21.9 %collective-permute-start.126 = (bf16[32,1024]{1,0:T(8,128)(2,1)S(1)}, bf16[32,1024]{1,0:T(8,128)(2,1)S(1)}, u32[]{:S(2)}, u32[]{:S(2)}) collective-permute-start(bf16[32,1024]{1,0:T(8,128)(2,1)S(1)} %bitcast.234), channel_id=1, source_target_pairs={{0,0},{8,1},{16,2},{24,3},{1,4},{9,5},{17,6},{25,7},{2,8},{10,9},{... | collective-permute-start | bytes 196616 | tf_op jit(solution)/shard_map/ppermute | solution.py:1072
  530.2 15.8 %collective-permute-start.121 = (bf16[2,32,1920]{2,1,0:T(8,128)(2,1)S(1)}, bf16[2,32,1920]{2,1,0:T(8,128)(2,1)S(1)}, u32[]{:S(2)}, u32[]{:S(2)}) collective-permute-start(bf16[2,32,1920]{2,1,0:T(8,128)(2,1)S(1)} %pad_maximum_fusion.7), channel_id=1, source_target_pairs={{0,6},{1,7},{2,4},{3,5},{4,2},{5,3},{6,0},{7,1},{8,14},{9,15},{10,... | collective-permute-start | bytes 737288 | tf_op jit(solution)/shard_map/ppermute | solution.py:39
  (237 other events, 1553.7 us)
Sparse Core Ops, SparseCore 0:
  39.1 31.3 all-gather.8
  72.6 44.7 all-gather.10
  119.6 26.6 all-gather.12
  147.7 49.9 all-gather.14
  328.6 46.4 reduce-scatter.3
  398.0 28.5 reduce-scatter.5
  440.9 44.4 reduce-scatter.7

commit v5 on v4

--- a/solution.py
+++ b/solution.py
@@ -154,7 +154,7 @@
     return (x, "raw")
 
 
-def call(kernel, ins, outs, scratch, flops, limit=BIG):
+def call(kernel, ins, outs, scratch, flops, limit=BIG, light=True):
     arrays = [a for a, _ in ins]
     kept = [i for i, (_, kind) in enumerate(ins) if kind == "held"]
     left = [i for i, out in enumerate(outs) if len(out) == 3]
@@ -217,7 +217,7 @@
         out_shape=tuple(jax.ShapeDtypeStruct(out[0], out[1]) for out in outs),
         scratch_shapes=buffers,
         compiler_params=pltpu.CompilerParams(vmem_limit_bytes=limit * 1024 * 1024),
-        cost_estimate=pl.CostEstimate(flops=flops, bytes_accessed=moved, transcendentals=0),
+        cost_estimate=pl.CostEstimate(flops=1 if light else flops, bytes_accessed=1 if light else moved, transcendentals=0),
     )(*arrays)
 
 
@@ -523,7 +523,7 @@
     sems = pltpu.SemaphoreType.DMA
     scratch = [((N, D), BF), ((N, D), BF), sems((n,)), sems((n,))]
     ins = [raw(item) for item in (*normed, *grads)] + [held(act), near(grad_pre)] + more
-    return call(kernel, ins, [((far, count, D), BF)], scratch, 4 * N * D * H)[0]
+    return call(kernel, ins, [((far, count, D), BF)], scratch, 4 * N * D * H, light=False)[0]
 
 
 def attn_back(blocks, full, qkv, context, logs, table, seg_row, half, scale):
@@ -642,7 +642,7 @@
         outs = [((rows + 16, 4 * wide), BF)] * far
     else:
         outs = [((far, rows + 16, 4 * wide), BF)]
-    return call(kernel, ins, outs, scratch, 8 * N * D * wide)
+    return call(kernel, ins, outs, scratch, 8 * N * D * wide, light=False)
 
 
 def plane_index():
@@ -1109,10 +1109,10 @@
     got = [across(blocks[step], PLANE * step) for step in range(1, O)]
     entries = jnp.concatenate(vectors, axis=2).transpose(1, 0, 2).reshape(PLANE, O * L * part)
     lines = jnp.pad(entries, ((0, 0), (0, in_rows * 128 - O * L * part))).reshape(PLANE, in_rows, 128)
-    got, lines = tie(got, lines)
     grad_tokens = turned((grad_first + sum(item.astype(F32) for item in terms)).astype(BF), True)
+    got, lines, grad_tokens = tie(got, lines, grad_tokens)
     even, odd, last_out = pack_shares([blocks[0]] + got, shares_attn[1:], shares_ffn, lines, in_cols, hidden_cols)
-    core, grad_tokens = tie(across(odd, 1), grad_tokens)
+    core = across(odd, 1)
     got = tie(*[across(jnp.stack([even[k], core[k]]), 2 * k) for k in (1, 2, 3)])
     w_in_grad, w_up_grad, lines, bias_in_grad = unpack_shares(even, core, got, L, in_cols, hidden_cols)
     entries = lines.reshape(-1)[: O * L * part].reshape(O, L * part)

time: 578 us -> 570 us (0.986)
  local copies, waits for them, and re-layouts: 51.2 us -> 43.8 us
    unnamed x279 -> x271, local copies, waits for them, and re-layouts: 33.9 us -> 26.2 us
  transfers between devices with their start and end apart: 134 -> 134, of which waited for: 59 -> 66; matrix products, arithmetic and copies ran while one was open for 5% -> 5% of each run, Pallas kernels for 21% -> 21%
where the time goes in v5:
time: 570 us; the launch traced here: 564 us
  waiting for transfers between devices  213 us (37%)
  Pallas kernels  138 us (24%)
  starting transfers between devices  136 us (24%)
  local copies, waits for them, and re-layouts  43.8 us (8%)
  between operations  17.2 us (3%)
  other arithmetic  16 us (3%)
    ppermute x119, waiting for transfers between devices, across(): return lax.ppermute(x, BOTH, [(d, d ^ mask) for d in range(size)])  213 us
    pallas_call x33, Pallas kernels, call(): pl.pallas_call(wrapped, in_specs=[IN_VMEM if kind == 'near' else IN_HBM f...  138 us
    ppermute x119, starting transfers between devices, across(): return lax.ppermute(x, BOTH, [(d, d ^ mask) for d in range(size)])  126 us
    unnamed x271, local copies, waits for them, and re-layouts  26.2 us
  transfers between devices with their start and end apart: 134, of which 66 were waited for; matrix products, arithmetic and copies ran while one was open for 5% of the time, Pallas kernels for 21%

profile of v5, /device:TPU:0, one launch (start us, length us, event | category | flops | bytes accessed | tf_op | source)
XLA Modules:
  0.0 564.2 jit_solution(4522095627301185258)
XLA Ops:
  23.7 7.7 %collective-permute-start.11 = (bf16[2,48,384]{2,1,0:T(8,128)(2,1)S(1)}, bf16[2,48,384]{2,1,0:T(8,128)(2,1)S(1)}, u32[]{:S(2)}, u32[]{:S(2)}) collective-permute-start(bf16[2,48,384]{2,1,0:T(8,128)(2,1)S(1)} %pad_maximum_fusion.13), channel_id=1, source_target_pairs={{0,6},{1,7},{2,4},{3,5},{4,2},{5,3},{6,0},{7,1},{8,14},{9,15},{10,... | collective-permute-start | bytes 221192 | tf_op jit(solution)/shard_map/ppermute | solution.py:39
  77.2 10.4 %shard_map.214 = (bf16[1152,384]{1,0:T(8,128)(2,1)}, bf16[1152,128]{1,0:T(8,128)(2,1)}, f32[2,1152]{1,0:T(2,128)}, bf16[4,144,1024]{2,1,0:T(8,128)(2,1)}, bf16[4,144,1024]{2,1,0:T(8,128)(2,1)}) custom-call(bf16[144,1024]{1,0:T(8,128)(2,1)} %copy-done, bf16[144,1024]{1,0:T(8,128)(2,1)} %copy-done.45, bf16[144,1024]{1,0:T(8,128)(2,1)} %copy-done.42, ...), custom_call_target="tpu_custom_call" | custom-call | flops 1 | bytes 1 | tf_op jit(solution)/shard_map/pallas_call | solution.py:213
  111.6 6.5 %collective-permute-done.21.refs_2_ = bf16[144,1024]{1,0:T(8,128)(2,1)S(1)} collective-permute-done((bf16[144,1024]{1,0:T(8,128)(2,1)S(1)}, bf16[144,1024]{1,0:T(8,128)(2,1)S(1)}, u32[]{:S(2)}, u32[]{:S(2)}) %collective-permute-start.21) | collective-permute-done | bytes 294944 | tf_op jit(solution)/shard_map/ppermute | solution.py:39
  126.4 8.0 %shard_map.217 = (bf16[1152,512]{1,0:T(8,128)(2,1)}, bf16[1152,512]{1,0:T(8,128)(2,1)}, bf16[4,144,1024]{2,1,0:T(8,128)(2,1)}, bf16[4,144,1024]{2,1,0:T(8,128)(2,1)}) custom-call(bf16[144,1024]{1,0:T(8,128)(2,1)} %copy-done.3, bf16[144,1024]{1,0:T(8,128)(2,1)} %copy-done.51, bf16[144,1024]{1,0:T(8,128)(2,1)} %copy-done.48, bf16[144,1024]{1,0:T(8,128)(2,1)} %copy-done.52, ...), custom_call_target="tpu_custom_call" | custom-call | flops 1 | bytes 1 | tf_op jit(solution)/shard_map/pallas_call | solution.py:213
  141.6 6.3 %collective-permute-done.32.refs_2_ = bf16[144,1024]{1,0:T(8,128)(2,1)S(1)} collective-permute-done((bf16[144,1024]{1,0:T(8,128)(2,1)S(1)}, bf16[144,1024]{1,0:T(8,128)(2,1)S(1)}, u32[]{:S(2)}, u32[]{:S(2)}) %collective-permute-start.32) | collective-permute-done | bytes 294944 | tf_op jit(solution)/shard_map/ppermute | solution.py:39
  159.1 6.5 %collective-permute-done.36.refs_2_ = bf16[144,1024]{1,0:T(8,128)(2,1)S(1)} collective-permute-done((bf16[144,1024]{1,0:T(8,128)(2,1)S(1)}, bf16[144,1024]{1,0:T(8,128)(2,1)S(1)}, u32[]{:S(2)}, u32[]{:S(2)}) %collective-permute-start.36) | collective-permute-done | bytes 294944 | tf_op jit(solution)/shard_map/ppermute | solution.py:39
  174.1 10.4 %shard_map.220 = (bf16[1152,384]{1,0:T(8,128)(2,1)}, bf16[1152,128]{1,0:T(8,128)(2,1)}, f32[2,1152]{1,0:T(2,128)}, bf16[4,144,1024]{2,1,0:T(8,128)(2,1)}, bf16[4,144,1024]{2,1,0:T(8,128)(2,1)}) custom-call(bf16[144,1024]{1,0:T(8,128)(2,1)} %copy-done.4, bf16[144,1024]{1,0:T(8,128)(2,1)} %copy-done.58, bf16[144,1024]{1,0:T(8,128)(2,1)} %copy-done.55, ...), custom_call_target="tpu_custom_call" | custom-call | flops 1 | bytes 1 | tf_op jit(solution)/shard_map/pallas_call | solution.py:213
  192.8 6.4 %collective-permute-done.43.refs_2_ = bf16[144,1024]{1,0:T(8,128)(2,1)S(1)} collective-permute-done((bf16[144,1024]{1,0:T(8,128)(2,1)S(1)}, bf16[144,1024]{1,0:T(8,128)(2,1)S(1)}, u32[]{:S(2)}, u32[]{:S(2)}) %collective-permute-start.43) | collective-permute-done | bytes 294944 | tf_op jit(solution)/shard_map/ppermute | solution.py:39
  210.2 6.5 %collective-permute-done.47.refs_2_ = bf16[144,1024]{1,0:T(8,128)(2,1)S(1)} collective-permute-done((bf16[144,1024]{1,0:T(8,128)(2,1)S(1)}, bf16[144,1024]{1,0:T(8,128)(2,1)S(1)}, u32[]{:S(2)}, u32[]{:S(2)}) %collective-permute-start.47) | collective-permute-done | bytes 294944 | tf_op jit(solution)/shard_map/ppermute | solution.py:39
  225.2 8.0 %shard_map.223 = (bf16[1152,512]{1,0:T(8,128)(2,1)}, bf16[1152,512]{1,0:T(8,128)(2,1)}, bf16[4,144,1024]{2,1,0:T(8,128)(2,1)}, bf16[4,144,1024]{2,1,0:T(8,128)(2,1)}) custom-call(bf16[144,1024]{1,0:T(8,128)(2,1)} %copy-done.18, bf16[144,1024]{1,0:T(8,128)(2,1)} %copy-done.93, bf16[144,1024]{1,0:T(8,128)(2,1)} %copy-done.90, bf16[144,1024]{1,0:T(8,128)(2,1)} %copy-done.94, ...), custom_call_target="tpu_custom_call" | custom-call | flops 1 | bytes 1 | tf_op jit(solution)/shard_map/pallas_call | solution.py:213
  293.3 7.3 %shard_map.228 = (bf16[1152,512]{1,0:T(8,128)(2,1)}, f32[1,512]{1,0:T(1,128)}, bf16[4,144,1024]{2,1,0:T(8,128)(2,1)}, bf16[4,144,1024]{2,1,0:T(8,128)(2,1)}) custom-call(bf16[144,1024]{1,0:T(8,128)(2,1)} %copy-done.5, bf16[144,1024]{1,0:T(8,128)(2,1)} %copy-done.65, bf16[144,1024]{1,0:T(8,128)(2,1)} %copy-done.62, bf16[144,1024]{1,0:T(8,128)(2,1)} %copy-done.66, ...), custom_call_target="tpu_custom_call" | custom-call | flops 1 | bytes 1 | tf_op jit(solution)/shard_map/pallas_call | solution.py:213
  312.7 8.5 %shard_map.230 = bf16[4,272,1024]{2,1,0:T(8,128)(2,1)} custom-call(bf16[144,1024]{1,0:T(8,128)(2,1)} %copy-done.18, bf16[144,1024]{1,0:T(8,128)(2,1)} %copy-done.93, bf16[144,1024]{1,0:T(8,128)(2,1)} %copy-done.90, bf16[144,1024]{1,0:T(8,128)(2,1)} %copy-done.94, bf16[144,1024]{1,0:T(8,128)(2,1)} %copy-done.91, bf16[144,1024]{1,0:T(8,128)(2,1)} %copy-done.95, ...), custom_call_target="tpu_custom_call" | custom-call | flops 2415919104 | bytes 9437184 | tf_op jit(solution)/shard_map/pallas_call | solution.py:213
  329.9 6.5 %collective-permute-done.82.refs_2_.refs_10_ = bf16[144,1024]{1,0:T(8,128)(2,1)S(1)} collective-permute-done((bf16[144,1024]{1,0:T(8,128)(2,1)S(1)}, bf16[144,1024]{1,0:T(8,128)(2,1)S(1)}, u32[]{:S(2)}, u32[]{:S(2)}) %collective-permute-start.82) | collective-permute-done | bytes 294944 | tf_op jit(solution)/shard_map/ppermute | solution.py:39
  342.6 17.2 %shard_map.232 = (bf16[1152,384]{1,0:T(8,128)(2,1)}, f32[1,384]{1,0:T(1,128)}, bf16[4,144,1024]{2,1,0:T(8,128)(2,1)}, bf16[4,144,1024]{2,1,0:T(8,128)(2,1)}) custom-call(bf16[144,1024]{1,0:T(8,128)(2,1)} %copy-done.7, bf16[144,1024]{1,0:T(8,128)(2,1)} %copy-done.82, bf16[144,1024]{1,0:T(8,128)(2,1)} %copy-done.76, bf16[144,1024]{1,0:T(8,128)(2,1)} %copy-done.84, ...), custom_call_target="tpu_custom_call" | custom-call | flops 1 | bytes 1 | tf_op jit(solution)/shard_map/pallas_call | solution.py:213
  369.4 6.8 %shard_map.234 = bf16[4,272,512]{2,1,0:T(8,128)(2,1)} custom-call(bf16[144,1024]{1,0:T(8,128)(2,1)} %copy-done.4, bf16[144,1024]{1,0:T(8,128)(2,1)} %copy-done.58, bf16[144,1024]{1,0:T(8,128)(2,1)} %copy-done.55, bf16[144,1024]{1,0:T(8,128)(2,1)} %copy-done.59, bf16[144,1024]{1,0:T(8,128)(2,1)} %copy-done.56, bf16[144,1024]{1,0:T(8,128)(2,1)} %copy-done.60, ...), custom_call_target="tpu_custom_call" | custom-call | flops 1207959552 | bytes 7013888 | tf_op jit(solution)/shard_map/pallas_call | solution.py:213
  391.3 6.5 %collective-permute-done.93.refs_2_.refs_10_ = bf16[144,1024]{1,0:T(8,128)(2,1)S(1)} collective-permute-done((bf16[144,1024]{1,0:T(8,128)(2,1)S(1)}, bf16[144,1024]{1,0:T(8,128)(2,1)S(1)}, u32[]{:S(2)}, u32[]{:S(2)}) %collective-permute-start.93) | collective-permute-done | bytes 294944 | tf_op jit(solution)/shard_map/ppermute | solution.py:39
  406.0 7.2 %shard_map.236 = (bf16[1152,512]{1,0:T(8,128)(2,1)}, f32[1,512]{1,0:T(1,128)}, bf16[4,144,1024]{2,1,0:T(8,128)(2,1)}, bf16[4,144,1024]{2,1,0:T(8,128)(2,1)}) custom-call(bf16[144,1024]{1,0:T(8,128)(2,1)} %copy-done.8, bf16[144,1024]{1,0:T(8,128)(2,1)} %copy-done.83, bf16[144,1024]{1,0:T(8,128)(2,1)} %copy-done.77, bf16[144,1024]{1,0:T(8,128)(2,1)} %copy-done.85, ...), custom_call_target="tpu_custom_call" | custom-call | flops 1 | bytes 1 | tf_op jit(solution)/shard_map/pallas_call | solution.py:213
  422.1 8.4 %shard_map.238 = bf16[4,256,1024]{2,1,0:T(8,128)(2,1)} custom-call(bf16[144,1024]{1,0:T(8,128)(2,1)} %copy-done.3, bf16[144,1024]{1,0:T(8,128)(2,1)} %copy-done.51, bf16[144,1024]{1,0:T(8,128)(2,1)} %copy-done.48, bf16[144,1024]{1,0:T(8,128)(2,1)} %copy-done.52, bf16[144,1024]{1,0:T(8,128)(2,1)} %copy-done.49, bf16[144,1024]{1,0:T(8,128)(2,1)} %copy-done.53, ...), custom_call_target="tpu_custom_call" | custom-call | flops 2415919104 | bytes 9175040 | tf_op jit(solution)/shard_map/pallas_call | solution.py:213
  441.8 6.3 %collective-permute-done.104.refs_2_.refs_10_ = bf16[144,1024]{1,0:T(8,128)(2,1)S(1)} collective-permute-done((bf16[144,1024]{1,0:T(8,128)(2,1)S(1)}, bf16[144,1024]{1,0:T(8,128)(2,1)S(1)}, u32[]{:S(2)}, u32[]{:S(2)}) %collective-permute-start.104) | collective-permute-done | bytes 294944 | tf_op jit(solution)/shard_map/ppermute | solution.py:39
  455.2 17.3 %shard_map.240 = (bf16[1152,384]{1,0:T(8,128)(2,1)}, f32[1,384]{1,0:T(1,128)}, bf16[4,144,1024]{2,1,0:T(8,128)(2,1)}, bf16[4,144,1024]{2,1,0:T(8,128)(2,1)}) custom-call(bf16[144,1024]{1,0:T(8,128)(2,1)} %copy-done.6, bf16[144,1024]{1,0:T(8,128)(2,1)} %copy-done.72, bf16[144,1024]{1,0:T(8,128)(2,1)} %copy-done.68, bf16[144,1024]{1,0:T(8,128)(2,1)} %copy-done.73, ...), custom_call_target="tpu_custom_call" | custom-call | flops 1 | bytes 1 | tf_op jit(solution)/shard_map/pallas_call | solution.py:213
  473.9 6.9 %shard_map.241 = (bf16[272,512]{1,0:T(8,128)(2,1)}, bf16[272,512]{1,0:T(8,128)(2,1)}, bf16[272,512]{1,0:T(8,128)(2,1)}, bf16[272,512]{1,0:T(8,128)(2,1)}) custom-call(bf16[144,1024]{1,0:T(8,128)(2,1)} %copy-done, bf16[144,1024]{1,0:T(8,128)(2,1)} %copy-done.45, bf16[144,1024]{1,0:T(8,128)(2,1)} %copy-done.42, bf16[144,1024]{1,0:T(8,128)(2,1)} %copy-done.46, ...), custom_call_target="tpu_custom_call" | custom-call | flops 1207959552 | bytes 7013888 | tf_op jit(solution)/shard_map/pallas_call | solution.py:213
  487.0 6.3 %collective-permute-start.112 = (bf16[272,512]{1,0:T(8,128)(2,1)}, bf16[272,512]{1,0:T(8,128)(2,1)S(1)}, u32[]{:S(2)}, u32[]{:S(2)}) collective-permute-start(bf16[272,512]{1,0:T(8,128)(2,1)} %get-tuple-element.308), channel_id=1, source_target_pairs={{0,16},{1,17},{2,18},{3,19},{4,20},{5,21},{6,22},{7,23},{8,24},{9,... | collective-permute-start | bytes 835592 | tf_op jit(solution)/shard_map/ppermute | solution.py:39
  503.2 9.9 %collective-permute-done.113.refs_3_ = bf16[272,512]{1,0:T(8,128)(2,1)S(1)} collective-permute-done((bf16[272,512]{1,0:T(8,128)(2,1)}, bf16[272,512]{1,0:T(8,128)(2,1)S(1)}, u32[]{:S(2)}, u32[]{:S(2)}) %collective-permute-start.113) | collective-permute-done | bytes 278560 | tf_op jit(solution)/shard_map/ppermute | solution.py:39
  513.5 12.7 %collective-permute-start.118 = (bf16[4,32,1920]{2,1,0:T(8,128)(2,1)S(1)}, bf16[4,32,1920]{2,1,0:T(8,128)(2,1)S(1)}, u32[]{:S(2)}, u32[]{:S(2)}) collective-permute-start(bf16[4,32,1920]{2,1,0:T(8,128)(2,1)S(1)} %get-tuple-element.336), channel_id=1, source_target_pairs={{0,1},{1,0},{2,3},{3,2},{4,5},{5,4},{6,7},{7,6},{8,9},{9,8},{10,11... | collective-permute-start | bytes 1474568 | tf_op jit(solution)/shard_map/ppermute | solution.py:39
  (710 shorter events, 342.6 us)
Async XLA Ops:
  7.2 70.0 %all-gather.9.cloned.1.call-start = ((), (), s32[]{:S(2)}) async-start(), calls=%async_computation.6 | async-start | bytes 1310720 | tf_op jit(solution)/shard_map/all_gather | solution.py:969
  11.7 26.6 %collective-permute-start.27 = (bf16[4,32,1408]{2,1,0:T(8,128)(2,1)}, bf16[4,32,1408]{2,1,0:T(8,128)(2,1)S(1)}, u32[]{:S(2)}, u32[]{:S(2)}) collective-permute-start(bf16[4,32,1408]{2,1,0:T(8,128)(2,1)} %slice.291), channel_id=1, source_target_pairs={{0,1},{1,0},{2,3},{3,2},{4,5},{5,4},{6,7},{7,6},{8,9},{9,8},{10,11... | collective-permute-start | bytes 1081352 | tf_op jit(solution)/shard_map/ppermute | solution.py:39
  12.7 18.7 %collective-permute-start.12 = (bf16[2,32,1024]{2,1,0:T(8,128)(2,1)}, bf16[2,32,1024]{2,1,0:T(8,128)(2,1)}, u32[]{:S(2)}, u32[]{:S(2)}) collective-permute-start(bf16[2,32,1024]{2,1,0:T(8,128)(2,1)} %param.15), channel_id=1, source_target_pairs={{0,0},{1,8},{2,16},{3,24},{4,1},{5,9},{6,17},{7,25},{8,2},{9,10},{... | collective-permute-start | bytes 393224 | tf_op jit(solution)/shard_map/ppermute | solution.py:957
  15.6 44.5 %collective-permute-start = (bf16[144,1024]{1,0:T(8,128)(2,1)}, bf16[144,1024]{1,0:T(8,128)(2,1)S(1)}, u32[]{:S(2)}, u32[]{:S(2)}) collective-permute-start(bf16[144,1024]{1,0:T(8,128)(2,1)} %bitcast), channel_id=1, source_target_pairs={{0,0},{1,16},{2,10},{3,26},{4,4},{5,20},{6,14},{7,30},{8,1},{9,17}... | collective-permute-start | bytes 884744 | tf_op jit(solution)/shard_map/ppermute | solution.py:49
  38.2 86.7 %all-gather.11.cloned.1.call-start = ((), (), s32[]{:S(2)}) async-start(), calls=%async_computation.7 | async-start | bytes 2621440 | tf_op jit(solution)/shard_map/all_gather | solution.py:969
  53.3 118.3 %all-gather.13.cloned.1.call-start = ((), (), s32[]{:S(2)}) async-start(), calls=%async_computation.8 | async-start | bytes 1310720 | tf_op jit(solution)/shard_map/all_gather | solution.py:969
  89.8 132.8 %all-gather.15.cloned.1.call-start = ((), (), s32[]{:S(2)}) async-start(), calls=%async_computation.9 | async-start | bytes 2949120 | tf_op jit(solution)/shard_map/all_gather | solution.py:969
  137.7 245.7 %reduce-scatter.4.cloned.1.call-start = ((), (), s32[]{:S(2)}) async-start(), calls=%async_computation.3 | async-start | bytes 2785280 | tf_op jit(solution)/shard_map/reduce_scatter | solution.py:1066
  139.0 15.2 %collective-permute-start.33 = (bf16[144,1024]{1,0:T(8,128)(2,1)S(1)}, bf16[144,1024]{1,0:T(8,128)(2,1)S(1)}, u32[]{:S(2)}, u32[]{:S(2)}) collective-permute-start(bf16[144,1024]{1,0:T(8,128)(2,1)S(1)} %get-tuple-element.201), channel_id=1, source_target_pairs={{0,4},{1,5},{2,6},{3,7},{4,0},{5,1},{6,2},{7,3},{8,12},{9,13},{10,... | collective-permute-start | bytes 884744 | tf_op jit(solution)/shard_map/ppermute | solution.py:39
  189.8 15.1 %collective-permute-start.44 = (bf16[144,1024]{1,0:T(8,128)(2,1)S(1)}, bf16[144,1024]{1,0:T(8,128)(2,1)S(1)}, u32[]{:S(2)}, u32[]{:S(2)}) collective-permute-start(bf16[144,1024]{1,0:T(8,128)(2,1)S(1)} %get-tuple-element.209), channel_id=1, source_target_pairs={{0,4},{1,5},{2,6},{3,7},{4,0},{5,1},{6,2},{7,3},{8,12},{9,13},{10,... | collective-permute-start | bytes 884744 | tf_op jit(solution)/shard_map/ppermute | solution.py:39
  239.4 15.1 %collective-permute-start.55 = (bf16[144,1024]{1,0:T(8,128)(2,1)S(1)}, bf16[144,1024]{1,0:T(8,128)(2,1)S(1)}, u32[]{:S(2)}, u32[]{:S(2)}) collective-permute-start(bf16[144,1024]{1,0:T(8,128)(2,1)S(1)} %get-tuple-element.217), channel_id=1, source_target_pairs={{0,4},{1,5},{2,6},{3,7},{4,0},{5,1},{6,2},{7,3},{8,12},{9,13},{10,... | collective-permute-start | bytes 884744 | tf_op jit(solution)/shard_map/ppermute | solution.py:39
  275.7 14.6 %collective-permute-start.68 = (bf16[144,1024]{1,0:T(8,128)(2,1)S(1)}, bf16[144,1024]{1,0:T(8,128)(2,1)S(1)}, u32[]{:S(2)}, u32[]{:S(2)}) collective-permute-start(bf16[144,1024]{1,0:T(8,128)(2,1)S(1)} %get-tuple-element.227.refs_0_.refs_8_), channel_id=1, source_target_pairs={{0,4},{1,5},{2,6},{3,7},{4,0},{5,1},{6,2},{7,3},{8,12},{9,13},{10,... | collective-permute-start | bytes 884744 | tf_op jit(solution)/shard_map/ppermute | solution.py:39
  324.4 129.2 %reduce-scatter.6.cloned.1.call-start = ((), (), s32[]{:S(2)}) async-start(), calls=%async_computation.4 | async-start | bytes 1392640 | tf_op jit(solution)/shard_map/reduce_scatter | solution.py:1066
  383.0 117.2 %reduce-scatter.8.cloned.1.call-start = ((), (), s32[]{:S(2)}) async-start(), calls=%async_computation.5 | async-start | bytes 2621440 | tf_op jit(solution)/shard_map/reduce_scatter | solution.py:1066
  419.7 15.4 %collective-permute-start.101 = (bf16[144,1024]{1,0:T(8,128)(2,1)}, bf16[144,1024]{1,0:T(8,128)(2,1)}, u32[]{:S(2)}, u32[]{:S(2)}) collective-permute-start(bf16[144,1024]{1,0:T(8,128)(2,1)} %get-tuple-element.278), channel_id=1, source_target_pairs={{0,4},{1,5},{2,6},{3,7},{4,0},{5,1},{6,2},{7,3},{8,12},{9,13},{10,... | collective-permute-start | bytes 884744 | tf_op jit(solution)/shard_map/ppermute | solution.py:39
  419.7 15.4 %collective-permute-start.102 = (bf16[144,1024]{1,0:T(8,128)(2,1)}, bf16[144,1024]{1,0:T(8,128)(2,1)}, u32[]{:S(2)}, u32[]{:S(2)}) collective-permute-start(bf16[144,1024]{1,0:T(8,128)(2,1)} %get-tuple-element.279), channel_id=1, source_target_pairs={{0,6},{1,7},{2,4},{3,5},{4,2},{5,3},{6,0},{7,1},{8,14},{9,15},{10,... | collective-permute-start | bytes 884744 | tf_op jit(solution)/shard_map/ppermute | solution.py:39
  484.6 15.6 %collective-permute-start.115 = (bf16[144,1024]{1,0:T(8,128)(2,1)}, bf16[144,1024]{1,0:T(8,128)(2,1)}, u32[]{:S(2)}, u32[]{:S(2)}) collective-permute-start(bf16[144,1024]{1,0:T(8,128)(2,1)} %get-tuple-element.321), channel_id=1, source_target_pairs={{0,4},{1,5},{2,6},{3,7},{4,0},{5,1},{6,2},{7,3},{8,12},{9,13},{10,... | collective-permute-start | bytes 884744 | tf_op jit(solution)/shard_map/ppermute | solution.py:39
  485.5 14.7 %collective-permute-start.116 = (bf16[144,1024]{1,0:T(8,128)(2,1)S(1)}, bf16[144,1024]{1,0:T(8,128)(2,1)}, u32[]{:S(2)}, u32[]{:S(2)}) collective-permute-start(bf16[144,1024]{1,0:T(8,128)(2,1)S(1)} %get-tuple-element.322), channel_id=1, source_target_pairs={{0,6},{1,7},{2,4},{3,5},{4,2},{5,3},{6,0},{7,1},{8,14},{9,15},{10,... | collective-permute-start | bytes 884744 | tf_op jit(solution)/shard_map/ppermute | solution.py:39
  486.9 16.3 %collective-permute-start.111 = (bf16[272,512]{1,0:T(8,128)(2,1)}, bf16[272,512]{1,0:T(8,128)(2,1)S(1)}, u32[]{:S(2)}, u32[]{:S(2)}) collective-permute-start(bf16[272,512]{1,0:T(8,128)(2,1)} %get-tuple-element.307), channel_id=1, source_target_pairs={{0,8},{1,9},{2,10},{3,11},{4,12},{5,13},{6,14},{7,15},{8,0},{9,1},... | collective-permute-start | bytes 835592 | tf_op jit(solution)/shard_map/ppermute | solution.py:39
  487.0 16.2 %collective-permute-start.112 = (bf16[272,512]{1,0:T(8,128)(2,1)}, bf16[272,512]{1,0:T(8,128)(2,1)S(1)}, u32[]{:S(2)}, u32[]{:S(2)}) collective-permute-start(bf16[272,512]{1,0:T(8,128)(2,1)} %get-tuple-element.308), channel_id=1, source_target_pairs={{0,16},{1,17},{2,18},{3,19},{4,20},{5,21},{6,22},{7,23},{8,24},{9,... | collective-permute-start | bytes 835592 | tf_op jit(solution)/shard_map/ppermute | solution.py:39
  493.4 19.8 %collective-permute-start.113 = (bf16[272,512]{1,0:T(8,128)(2,1)}, bf16[272,512]{1,0:T(8,128)(2,1)S(1)}, u32[]{:S(2)}, u32[]{:S(2)}) collective-permute-start(bf16[272,512]{1,0:T(8,128)(2,1)} %get-tuple-element.309), channel_id=1, source_target_pairs={{0,24},{1,25},{2,26},{3,27},{4,28},{5,29},{6,30},{7,31},{8,16},{9,... | collective-permute-start | bytes 835592 | tf_op jit(solution)/shard_map/ppermute | solution.py:39
  502.5 48.0 %collective-permute-start.126 = (bf16[32,1024]{1,0:T(8,128)(2,1)S(1)}, bf16[32,1024]{1,0:T(8,128)(2,1)S(1)}, u32[]{:S(2)}, u32[]{:S(2)}) collective-permute-start(bf16[32,1024]{1,0:T(8,128)(2,1)S(1)} %bitcast.243), channel_id=1, source_target_pairs={{0,0},{8,1},{16,2},{24,3},{1,4},{9,5},{17,6},{25,7},{2,8},{10,9},{... | collective-permute-start | bytes 196616 | tf_op jit(solution)/shard_map/ppermute | solution.py:1072
  527.3 23.2 %collective-permute-start.125 = (bf16[32,1024]{1,0:T(8,128)(2,1)S(1)}, bf16[32,1024]{1,0:T(8,128)(2,1)S(1)}, u32[]{:S(2)}, u32[]{:S(2)}) collective-permute-start(bf16[32,1024]{1,0:T(8,128)(2,1)S(1)} %bitcast.244), channel_id=1, source_target_pairs={{0,0},{8,1},{16,2},{24,3},{1,4},{9,5},{17,6},{25,7},{2,8},{10,9},{... | collective-permute-start | bytes 196616 | tf_op jit(solution)/shard_map/ppermute | solution.py:1072
  528.2 15.0 %collective-permute-start.120 = (bf16[2,32,1920]{2,1,0:T(8,128)(2,1)S(1)}, bf16[2,32,1920]{2,1,0:T(8,128)(2,1)S(1)}, u32[]{:S(2)}, u32[]{:S(2)}) collective-permute-start(bf16[2,32,1920]{2,1,0:T(8,128)(2,1)S(1)} %pad_maximum_fusion.6), channel_id=1, source_target_pairs={{0,4},{1,5},{2,6},{3,7},{4,0},{5,1},{6,2},{7,3},{8,12},{9,13},{10,... | collective-permute-start | bytes 737288 | tf_op jit(solution)/shard_map/ppermute | solution.py:39
  (234 other events, 1605.0 us)
Sparse Core Ops, SparseCore 0:
  38.3 30.4 all-gather.8
  71.0 44.7 all-gather.10
  118.0 26.6 all-gather.12
  146.6 49.9 all-gather.14
  324.5 47.8 reduce-scatter.3
  383.1 30.8 reduce-scatter.5
  435.2 46.5 reduce-scatter.7

commit v6 on v5

--- a/solution.py
+++ b/solution.py
@@ -1107,19 +1107,19 @@
             grad_parts = [grad_first] + terms
 
     got = [across(blocks[step], PLANE * step) for step in range(1, O)]
-    entries = jnp.concatenate(vectors, axis=2).transpose(1, 0, 2).reshape(PLANE, O * L * part)
-    lines = jnp.pad(entries, ((0, 0), (0, in_rows * 128 - O * L * part))).reshape(PLANE, in_rows, 128)
+    entries = jnp.concatenate(vectors + [jnp.broadcast_to(loss_terms, (O, PLANE, 2))], axis=2)
+    lines = pick(entries, far)
+    for step in range(1, O):
+        lines = lines + across(pick(entries, far ^ step), PLANE * step)
+    loss_terms = lines[0, L * part :]
+    lines = jnp.pad(lines[:, : L * part], ((0, 0), (0, in_rows * 128 - L * part))).reshape(PLANE, in_rows, 128)
     grad_tokens = turned((grad_first + sum(item.astype(F32) for item in terms)).astype(BF), True)
     got, lines, grad_tokens = tie(got, lines, grad_tokens)
     even, odd, last_out = pack_shares([blocks[0]] + got, shares_attn[1:], shares_ffn, lines, in_cols, hidden_cols)
     core = across(odd, 1)
     got = tie(*[across(jnp.stack([even[k], core[k]]), 2 * k) for k in (1, 2, 3)])
     w_in_grad, w_up_grad, lines, bias_in_grad = unpack_shares(even, core, got, L, in_cols, hidden_cols)
-    entries = lines.reshape(-1)[: O * L * part].reshape(O, L * part)
-    entries = jnp.concatenate([entries, jnp.broadcast_to(loss_terms[None], (O, 2))], axis=1)
-    mine = pick(entries, far)
-    for step in range(1, O):
-        mine = mine + across(pick(entries, far ^ step), PLANE * step)
+    mine = lines.reshape(-1)
     bias_in_grad = jnp.pad(bias_in_grad[:, 0], ((0, 0), (0, O * PLANE * bias_part - 3 * D)))
     bias_in_grad = pick(bias_in_grad.reshape(L, O * PLANE, bias_part), place, axis=1)
     for layer in range(L):
@@ -1129,7 +1129,6 @@
         outs[5][layer] = mine[layer * part + gain_part : (layer + 1) * part] + bias_in_grad[layer]
     col_share = shares_ffn[L - 1][rows_in // 2 + up_cols :].reshape(-1)[: in_rows * full_width]
     col_share = col_share.reshape(in_rows, full_width).astype(F32)
-    loss_terms = mine[L * part :]
     outs[0], outs[2] = w_in_grad, w_up_grad
     stacked = [jnp.stack(items).astype(F32) if isinstance(items, list) else items for items in outs]
     return (

time: 570 us -> 565 us (level)
    unnamed x271 -> x279, local copies, waits for them, and re-layouts: 26.2 us -> 28.8 us
  transfers between devices with their start and end apart: 134 -> 134, of which waited for: 66 -> 63; matrix products, arithmetic and copies ran while one was open for 5% -> 6% of each run, Pallas kernels for 21% -> 21%
where the time goes in v6:
time: 565 us; the launch traced here: 560 us
  waiting for transfers between devices  209 us (37%)
  Pallas kernels  137 us (24%)
  starting transfers between devices  133 us (24%)
  local copies, waits for them, and re-layouts  46.7 us (8%)
  between operations  17.2 us (3%)
  other arithmetic  16 us (3%)
    ppermute x119, waiting for transfers between devices, across(): return lax.ppermute(x, BOTH, [(d, d ^ mask) for d in range(size)])  209 us
    pallas_call x33, Pallas kernels, call(): pl.pallas_call(wrapped, in_specs=[IN_VMEM if kind == 'near' else IN_HBM f...  137 us
    ppermute x119, starting transfers between devices, across(): return lax.ppermute(x, BOTH, [(d, d ^ mask) for d in range(size)])  123 us
    unnamed x279, local copies, waits for them, and re-layouts  28.8 us
  transfers between devices with their start and end apart: 134, of which 63 were waited for; matrix products, arithmetic and copies ran while one was open for 6% of the time, Pallas kernels for 21%

profile of v6, /device:TPU:0, one launch (start us, length us, event | category | flops | bytes accessed | tf_op | source)
XLA Modules:
  0.0 559.6 jit_solution(15190754576933858146)
XLA Ops:
  23.8 7.7 %collective-permute-start.11 = (bf16[2,48,384]{2,1,0:T(8,128)(2,1)S(1)}, bf16[2,48,384]{2,1,0:T(8,128)(2,1)S(1)}, u32[]{:S(2)}, u32[]{:S(2)}) collective-permute-start(bf16[2,48,384]{2,1,0:T(8,128)(2,1)S(1)} %pad_maximum_fusion.13), channel_id=1, source_target_pairs={{0,6},{1,7},{2,4},{3,5},{4,2},{5,3},{6,0},{7,1},{8,14},{9,15},{10,... | collective-permute-start | bytes 221192 | tf_op jit(solution)/shard_map/ppermute | solution.py:39
  77.2 10.4 %shard_map.214 = (bf16[1152,384]{1,0:T(8,128)(2,1)}, bf16[1152,128]{1,0:T(8,128)(2,1)}, f32[2,1152]{1,0:T(2,128)}, bf16[4,144,1024]{2,1,0:T(8,128)(2,1)}, bf16[4,144,1024]{2,1,0:T(8,128)(2,1)}) custom-call(bf16[144,1024]{1,0:T(8,128)(2,1)} %copy-done, bf16[144,1024]{1,0:T(8,128)(2,1)} %copy-done.47, bf16[144,1024]{1,0:T(8,128)(2,1)} %copy-done.44, ...), custom_call_target="tpu_custom_call" | custom-call | flops 1 | bytes 1 | tf_op jit(solution)/shard_map/pallas_call | solution.py:213
  111.7 6.5 %collective-permute-done.21.refs_2_ = bf16[144,1024]{1,0:T(8,128)(2,1)S(1)} collective-permute-done((bf16[144,1024]{1,0:T(8,128)(2,1)S(1)}, bf16[144,1024]{1,0:T(8,128)(2,1)S(1)}, u32[]{:S(2)}, u32[]{:S(2)}) %collective-permute-start.21) | collective-permute-done | bytes 294944 | tf_op jit(solution)/shard_map/ppermute | solution.py:39
  126.0 8.0 %shard_map.217 = (bf16[1152,512]{1,0:T(8,128)(2,1)}, bf16[1152,512]{1,0:T(8,128)(2,1)}, bf16[4,144,1024]{2,1,0:T(8,128)(2,1)}, bf16[4,144,1024]{2,1,0:T(8,128)(2,1)}) custom-call(bf16[144,1024]{1,0:T(8,128)(2,1)} %copy-done.3, bf16[144,1024]{1,0:T(8,128)(2,1)} %copy-done.53, bf16[144,1024]{1,0:T(8,128)(2,1)} %copy-done.50, bf16[144,1024]{1,0:T(8,128)(2,1)} %copy-done.54, ...), custom_call_target="tpu_custom_call" | custom-call | flops 1 | bytes 1 | tf_op jit(solution)/shard_map/pallas_call | solution.py:213
  141.3 6.3 %collective-permute-done.32.refs_2_ = bf16[144,1024]{1,0:T(8,128)(2,1)S(1)} collective-permute-done((bf16[144,1024]{1,0:T(8,128)(2,1)S(1)}, bf16[144,1024]{1,0:T(8,128)(2,1)S(1)}, u32[]{:S(2)}, u32[]{:S(2)}) %collective-permute-start.32) | collective-permute-done | bytes 294944 | tf_op jit(solution)/shard_map/ppermute | solution.py:39
  147.7 6.5 %collective-permute-done.33.refs_3_ = bf16[144,1024]{1,0:T(8,128)(2,1)S(1)} collective-permute-done((bf16[144,1024]{1,0:T(8,128)(2,1)S(1)}, bf16[144,1024]{1,0:T(8,128)(2,1)S(1)}, u32[]{:S(2)}, u32[]{:S(2)}) %collective-permute-start.33) | collective-permute-done | bytes 294944 | tf_op jit(solution)/shard_map/ppermute | solution.py:39
  159.1 6.5 %collective-permute-done.36.refs_2_ = bf16[144,1024]{1,0:T(8,128)(2,1)S(1)} collective-permute-done((bf16[144,1024]{1,0:T(8,128)(2,1)S(1)}, bf16[144,1024]{1,0:T(8,128)(2,1)S(1)}, u32[]{:S(2)}, u32[]{:S(2)}) %collective-permute-start.36) | collective-permute-done | bytes 294944 | tf_op jit(solution)/shard_map/ppermute | solution.py:39
  174.1 10.3 %shard_map.220 = (bf16[1152,384]{1,0:T(8,128)(2,1)}, bf16[1152,128]{1,0:T(8,128)(2,1)}, f32[2,1152]{1,0:T(2,128)}, bf16[4,144,1024]{2,1,0:T(8,128)(2,1)}, bf16[4,144,1024]{2,1,0:T(8,128)(2,1)}) custom-call(bf16[144,1024]{1,0:T(8,128)(2,1)} %copy-done.4, bf16[144,1024]{1,0:T(8,128)(2,1)} %copy-done.60, bf16[144,1024]{1,0:T(8,128)(2,1)} %copy-done.57, ...), custom_call_target="tpu_custom_call" | custom-call | flops 1 | bytes 1 | tf_op jit(solution)/shard_map/pallas_call | solution.py:213
  192.6 6.4 %collective-permute-done.43.refs_2_ = bf16[144,1024]{1,0:T(8,128)(2,1)S(1)} collective-permute-done((bf16[144,1024]{1,0:T(8,128)(2,1)S(1)}, bf16[144,1024]{1,0:T(8,128)(2,1)S(1)}, u32[]{:S(2)}, u32[]{:S(2)}) %collective-permute-start.43) | collective-permute-done | bytes 294944 | tf_op jit(solution)/shard_map/ppermute | solution.py:39
  210.1 6.5 %collective-permute-done.47.refs_2_ = bf16[144,1024]{1,0:T(8,128)(2,1)S(1)} collective-permute-done((bf16[144,1024]{1,0:T(8,128)(2,1)S(1)}, bf16[144,1024]{1,0:T(8,128)(2,1)S(1)}, u32[]{:S(2)}, u32[]{:S(2)}) %collective-permute-start.47) | collective-permute-done | bytes 294944 | tf_op jit(solution)/shard_map/ppermute | solution.py:39
  225.0 8.0 %shard_map.223 = (bf16[1152,512]{1,0:T(8,128)(2,1)}, bf16[1152,512]{1,0:T(8,128)(2,1)}, bf16[4,144,1024]{2,1,0:T(8,128)(2,1)}, bf16[4,144,1024]{2,1,0:T(8,128)(2,1)}) custom-call(bf16[144,1024]{1,0:T(8,128)(2,1)} %copy-done.18, bf16[144,1024]{1,0:T(8,128)(2,1)} %copy-done.95, bf16[144,1024]{1,0:T(8,128)(2,1)} %copy-done.92, bf16[144,1024]{1,0:T(8,128)(2,1)} %copy-done.96, ...), custom_call_target="tpu_custom_call" | custom-call | flops 1 | bytes 1 | tf_op jit(solution)/shard_map/pallas_call | solution.py:213
  292.0 7.2 %shard_map.228 = (bf16[1152,512]{1,0:T(8,128)(2,1)}, f32[1,512]{1,0:T(1,128)}, bf16[4,144,1024]{2,1,0:T(8,128)(2,1)}, bf16[4,144,1024]{2,1,0:T(8,128)(2,1)}) custom-call(bf16[144,1024]{1,0:T(8,128)(2,1)} %copy-done.6, bf16[144,1024]{1,0:T(8,128)(2,1)} %copy-done.70, bf16[144,1024]{1,0:T(8,128)(2,1)} %copy-done.66, bf16[144,1024]{1,0:T(8,128)(2,1)} %copy-done.72, ...), custom_call_target="tpu_custom_call" | custom-call | flops 1 | bytes 1 | tf_op jit(solution)/shard_map/pallas_call | solution.py:213
  312.0 8.5 %shard_map.230 = bf16[4,272,1024]{2,1,0:T(8,128)(2,1)} custom-call(bf16[144,1024]{1,0:T(8,128)(2,1)} %copy-done.18, bf16[144,1024]{1,0:T(8,128)(2,1)} %copy-done.95, bf16[144,1024]{1,0:T(8,128)(2,1)} %copy-done.92, bf16[144,1024]{1,0:T(8,128)(2,1)} %copy-done.96, bf16[144,1024]{1,0:T(8,128)(2,1)} %copy-done.93, bf16[144,1024]{1,0:T(8,128)(2,1)} %copy-done.97, ...), custom_call_target="tpu_custom_call" | custom-call | flops 2415919104 | bytes 9437184 | tf_op jit(solution)/shard_map/pallas_call | solution.py:213
  329.7 6.5 %collective-permute-done.82.refs_2_.refs_10_ = bf16[144,1024]{1,0:T(8,128)(2,1)S(1)} collective-permute-done((bf16[144,1024]{1,0:T(8,128)(2,1)S(1)}, bf16[144,1024]{1,0:T(8,128)(2,1)S(1)}, u32[]{:S(2)}, u32[]{:S(2)}) %collective-permute-start.82) | collective-permute-done | bytes 294944 | tf_op jit(solution)/shard_map/ppermute | solution.py:39
  342.7 17.2 %shard_map.232 = (bf16[1152,384]{1,0:T(8,128)(2,1)}, f32[1,384]{1,0:T(1,128)}, bf16[4,144,1024]{2,1,0:T(8,128)(2,1)}, bf16[4,144,1024]{2,1,0:T(8,128)(2,1)}) custom-call(bf16[144,1024]{1,0:T(8,128)(2,1)} %copy-done.7, bf16[144,1024]{1,0:T(8,128)(2,1)} %copy-done.84, bf16[144,1024]{1,0:T(8,128)(2,1)} %copy-done.78, bf16[144,1024]{1,0:T(8,128)(2,1)} %copy-done.86, ...), custom_call_target="tpu_custom_call" | custom-call | flops 1 | bytes 1 | tf_op jit(solution)/shard_map/pallas_call | solution.py:213
  369.5 6.8 %shard_map.234 = bf16[4,272,512]{2,1,0:T(8,128)(2,1)} custom-call(bf16[144,1024]{1,0:T(8,128)(2,1)} %copy-done.4, bf16[144,1024]{1,0:T(8,128)(2,1)} %copy-done.60, bf16[144,1024]{1,0:T(8,128)(2,1)} %copy-done.57, bf16[144,1024]{1,0:T(8,128)(2,1)} %copy-done.61, bf16[144,1024]{1,0:T(8,128)(2,1)} %copy-done.58, bf16[144,1024]{1,0:T(8,128)(2,1)} %copy-done.62, ...), custom_call_target="tpu_custom_call" | custom-call | flops 1207959552 | bytes 7013888 | tf_op jit(solution)/shard_map/pallas_call | solution.py:213
  376.3 6.6 %collective-permute-done.90.refs_3_ = bf16[144,1024]{1,0:T(8,128)(2,1)S(1)} collective-permute-done((bf16[144,1024]{1,0:T(8,128)(2,1)S(1)}, bf16[144,1024]{1,0:T(8,128)(2,1)S(1)}, u32[]{:S(2)}, u32[]{:S(2)}) %collective-permute-start.90) | collective-permute-done | bytes 294944 | tf_op jit(solution)/shard_map/ppermute | solution.py:39
  391.2 6.5 %collective-permute-done.93.refs_2_.refs_10_ = bf16[144,1024]{1,0:T(8,128)(2,1)S(1)} collective-permute-done((bf16[144,1024]{1,0:T(8,128)(2,1)S(1)}, bf16[144,1024]{1,0:T(8,128)(2,1)S(1)}, u32[]{:S(2)}, u32[]{:S(2)}) %collective-permute-start.93) | collective-permute-done | bytes 294944 | tf_op jit(solution)/shard_map/ppermute | solution.py:39
  406.2 7.2 %shard_map.236 = (bf16[1152,512]{1,0:T(8,128)(2,1)}, f32[1,512]{1,0:T(1,128)}, bf16[4,144,1024]{2,1,0:T(8,128)(2,1)}, bf16[4,144,1024]{2,1,0:T(8,128)(2,1)}) custom-call(bf16[144,1024]{1,0:T(8,128)(2,1)} %copy-done.8, bf16[144,1024]{1,0:T(8,128)(2,1)} %copy-done.85, bf16[144,1024]{1,0:T(8,128)(2,1)} %copy-done.79, bf16[144,1024]{1,0:T(8,128)(2,1)} %copy-done.87, ...), custom_call_target="tpu_custom_call" | custom-call | flops 1 | bytes 1 | tf_op jit(solution)/shard_map/pallas_call | solution.py:213
  423.2 8.5 %shard_map.238 = bf16[4,256,1024]{2,1,0:T(8,128)(2,1)} custom-call(bf16[144,1024]{1,0:T(8,128)(2,1)} %copy-done.3, bf16[144,1024]{1,0:T(8,128)(2,1)} %copy-done.53, bf16[144,1024]{1,0:T(8,128)(2,1)} %copy-done.50, bf16[144,1024]{1,0:T(8,128)(2,1)} %copy-done.54, bf16[144,1024]{1,0:T(8,128)(2,1)} %copy-done.51, bf16[144,1024]{1,0:T(8,128)(2,1)} %copy-done.55, ...), custom_call_target="tpu_custom_call" | custom-call | flops 2415919104 | bytes 9175040 | tf_op jit(solution)/shard_map/pallas_call | solution.py:213
  458.1 17.3 %shard_map.240 = (bf16[1152,384]{1,0:T(8,128)(2,1)}, f32[1,384]{1,0:T(1,128)}, bf16[4,144,1024]{2,1,0:T(8,128)(2,1)}, bf16[4,144,1024]{2,1,0:T(8,128)(2,1)}) custom-call(bf16[144,1024]{1,0:T(8,128)(2,1)} %copy-done.5, bf16[144,1024]{1,0:T(8,128)(2,1)} %copy-done.71, bf16[144,1024]{1,0:T(8,128)(2,1)} %copy-done.64, bf16[144,1024]{1,0:T(8,128)(2,1)} %copy-done.73, ...), custom_call_target="tpu_custom_call" | custom-call | flops 1 | bytes 1 | tf_op jit(solution)/shard_map/pallas_call | solution.py:213
  483.5 6.8 %shard_map.241 = (bf16[272,512]{1,0:T(8,128)(2,1)}, bf16[272,512]{1,0:T(8,128)(2,1)}, bf16[272,512]{1,0:T(8,128)(2,1)}, bf16[272,512]{1,0:T(8,128)(2,1)}) custom-call(bf16[144,1024]{1,0:T(8,128)(2,1)} %copy-done, bf16[144,1024]{1,0:T(8,128)(2,1)} %copy-done.47, bf16[144,1024]{1,0:T(8,128)(2,1)} %copy-done.44, bf16[144,1024]{1,0:T(8,128)(2,1)} %copy-done.48, ...), custom_call_target="tpu_custom_call" | custom-call | flops 1207959552 | bytes 7013888 | tf_op jit(solution)/shard_map/pallas_call | solution.py:213
  511.7 6.9 %collective-permute-done.115.refs_2_ = bf16[272,512]{1,0:T(8,128)(2,1)S(1)} collective-permute-done((bf16[272,512]{1,0:T(8,128)(2,1)}, bf16[272,512]{1,0:T(8,128)(2,1)S(1)}, u32[]{:S(2)}, u32[]{:S(2)}) %collective-permute-start.115) | collective-permute-done | bytes 278560 | tf_op jit(solution)/shard_map/ppermute | solution.py:39
  519.0 12.1 %collective-permute-start.121 = (bf16[4,32,1920]{2,1,0:T(8,128)(2,1)S(1)}, bf16[4,32,1920]{2,1,0:T(8,128)(2,1)S(1)}, u32[]{:S(2)}, u32[]{:S(2)}) collective-permute-start(bf16[4,32,1920]{2,1,0:T(8,128)(2,1)S(1)} %get-tuple-element.338), channel_id=1, source_target_pairs={{0,1},{1,0},{2,3},{3,2},{4,5},{5,4},{6,7},{7,6},{8,9},{9,8},{10,11... | collective-permute-start | bytes 1474568 | tf_op jit(solution)/shard_map/ppermute | solution.py:39
  (716 shorter events, 341.2 us)
Async XLA Ops:
  7.2 70.0 %all-gather.9.cloned.1.call-start = ((), (), s32[]{:S(2)}) async-start(), calls=%async_computation.6 | async-start | bytes 1310720 | tf_op jit(solution)/shard_map/all_gather | solution.py:969
  11.7 26.5 %collective-permute-start.27 = (bf16[4,32,1408]{2,1,0:T(8,128)(2,1)}, bf16[4,32,1408]{2,1,0:T(8,128)(2,1)S(1)}, u32[]{:S(2)}, u32[]{:S(2)}) collective-permute-start(bf16[4,32,1408]{2,1,0:T(8,128)(2,1)} %slice.296), channel_id=1, source_target_pairs={{0,1},{1,0},{2,3},{3,2},{4,5},{5,4},{6,7},{7,6},{8,9},{9,8},{10,11... | collective-permute-start | bytes 1081352 | tf_op jit(solution)/shard_map/ppermute | solution.py:39
  12.7 18.7 %collective-permute-start.12 = (bf16[2,32,1024]{2,1,0:T(8,128)(2,1)}, bf16[2,32,1024]{2,1,0:T(8,128)(2,1)}, u32[]{:S(2)}, u32[]{:S(2)}) collective-permute-start(bf16[2,32,1024]{2,1,0:T(8,128)(2,1)} %param.15), channel_id=1, source_target_pairs={{0,0},{1,8},{2,16},{3,24},{4,1},{5,9},{6,17},{7,25},{8,2},{9,10},{... | collective-permute-start | bytes 393224 | tf_op jit(solution)/shard_map/ppermute | solution.py:957
  15.6 44.5 %collective-permute-start = (bf16[144,1024]{1,0:T(8,128)(2,1)}, bf16[144,1024]{1,0:T(8,128)(2,1)S(1)}, u32[]{:S(2)}, u32[]{:S(2)}) collective-permute-start(bf16[144,1024]{1,0:T(8,128)(2,1)} %bitcast), channel_id=1, source_target_pairs={{0,0},{1,16},{2,10},{3,26},{4,4},{5,20},{6,14},{7,30},{8,1},{9,17}... | collective-permute-start | bytes 884744 | tf_op jit(solution)/shard_map/ppermute | solution.py:49
  38.2 86.3 %all-gather.11.cloned.1.call-start = ((), (), s32[]{:S(2)}) async-start(), calls=%async_computation.7 | async-start | bytes 2621440 | tf_op jit(solution)/shard_map/all_gather | solution.py:969
  53.4 118.2 %all-gather.13.cloned.1.call-start = ((), (), s32[]{:S(2)}) async-start(), calls=%async_computation.8 | async-start | bytes 1310720 | tf_op jit(solution)/shard_map/all_gather | solution.py:969
  89.9 132.7 %all-gather.15.cloned.1.call-start = ((), (), s32[]{:S(2)}) async-start(), calls=%async_computation.9 | async-start | bytes 2949120 | tf_op jit(solution)/shard_map/all_gather | solution.py:969
  137.4 246.0 %reduce-scatter.4.cloned.1.call-start = ((), (), s32[]{:S(2)}) async-start(), calls=%async_computation.3 | async-start | bytes 2785280 | tf_op jit(solution)/shard_map/reduce_scatter | solution.py:1066
  139.0 15.2 %collective-permute-start.33 = (bf16[144,1024]{1,0:T(8,128)(2,1)S(1)}, bf16[144,1024]{1,0:T(8,128)(2,1)S(1)}, u32[]{:S(2)}, u32[]{:S(2)}) collective-permute-start(bf16[144,1024]{1,0:T(8,128)(2,1)S(1)} %get-tuple-element.201), channel_id=1, source_target_pairs={{0,4},{1,5},{2,6},{3,7},{4,0},{5,1},{6,2},{7,3},{8,12},{9,13},{10,... | collective-permute-start | bytes 884744 | tf_op jit(solution)/shard_map/ppermute | solution.py:39
  189.7 15.1 %collective-permute-start.44 = (bf16[144,1024]{1,0:T(8,128)(2,1)S(1)}, bf16[144,1024]{1,0:T(8,128)(2,1)S(1)}, u32[]{:S(2)}, u32[]{:S(2)}) collective-permute-start(bf16[144,1024]{1,0:T(8,128)(2,1)S(1)} %get-tuple-element.209), channel_id=1, source_target_pairs={{0,4},{1,5},{2,6},{3,7},{4,0},{5,1},{6,2},{7,3},{8,12},{9,13},{10,... | collective-permute-start | bytes 884744 | tf_op jit(solution)/shard_map/ppermute | solution.py:39
  239.3 15.1 %collective-permute-start.55 = (bf16[144,1024]{1,0:T(8,128)(2,1)S(1)}, bf16[144,1024]{1,0:T(8,128)(2,1)S(1)}, u32[]{:S(2)}, u32[]{:S(2)}) collective-permute-start(bf16[144,1024]{1,0:T(8,128)(2,1)S(1)} %get-tuple-element.217), channel_id=1, source_target_pairs={{0,4},{1,5},{2,6},{3,7},{4,0},{5,1},{6,2},{7,3},{8,12},{9,13},{10,... | collective-permute-start | bytes 884744 | tf_op jit(solution)/shard_map/ppermute | solution.py:39
  324.2 131.7 %reduce-scatter.6.cloned.1.call-start = ((), (), s32[]{:S(2)}) async-start(), calls=%async_computation.4 | async-start | bytes 1392640 | tf_op jit(solution)/shard_map/reduce_scatter | solution.py:1066
  367.8 15.1 %collective-permute-start.90 = (bf16[144,1024]{1,0:T(8,128)(2,1)S(1)}, bf16[144,1024]{1,0:T(8,128)(2,1)S(1)}, u32[]{:S(2)}, u32[]{:S(2)}) collective-permute-start(bf16[144,1024]{1,0:T(8,128)(2,1)S(1)} %get-tuple-element.258), channel_id=1, source_target_pairs={{0,4},{1,5},{2,6},{3,7},{4,0},{5,1},{6,2},{7,3},{8,12},{9,13},{10,... | collective-permute-start | bytes 884744 | tf_op jit(solution)/shard_map/ppermute | solution.py:39
  382.9 125.2 %reduce-scatter.8.cloned.1.call-start = ((), (), s32[]{:S(2)}) async-start(), calls=%async_computation.5 | async-start | bytes 2621440 | tf_op jit(solution)/shard_map/reduce_scatter | solution.py:1066
  420.4 15.3 %collective-permute-start.101 = (bf16[144,1024]{1,0:T(8,128)(2,1)}, bf16[144,1024]{1,0:T(8,128)(2,1)S(1)}, u32[]{:S(2)}, u32[]{:S(2)}) collective-permute-start(bf16[144,1024]{1,0:T(8,128)(2,1)} %get-tuple-element.278), channel_id=1, source_target_pairs={{0,4},{1,5},{2,6},{3,7},{4,0},{5,1},{6,2},{7,3},{8,12},{9,13},{10,... | collective-permute-start | bytes 884744 | tf_op jit(solution)/shard_map/ppermute | solution.py:39
  420.7 14.9 %collective-permute-start.102 = (bf16[144,1024]{1,0:T(8,128)(2,1)}, bf16[144,1024]{1,0:T(8,128)(2,1)}, u32[]{:S(2)}, u32[]{:S(2)}) collective-permute-start(bf16[144,1024]{1,0:T(8,128)(2,1)} %get-tuple-element.279), channel_id=1, source_target_pairs={{0,6},{1,7},{2,4},{3,5},{4,2},{5,3},{6,0},{7,1},{8,14},{9,15},{10,... | collective-permute-start | bytes 884744 | tf_op jit(solution)/shard_map/ppermute | solution.py:39
  475.4 14.8 %collective-permute-start.113 = (bf16[4,144,1024]{2,1,0:T(8,128)(2,1)}, bf16[4,144,1024]{2,1,0:T(8,128)(2,1)}, u32[]{:S(2)}, u32[]{:S(2)}) collective-permute-start(bf16[4,144,1024]{2,1,0:T(8,128)(2,1)} %get-tuple-element.306), channel_id=1, source_target_pairs={{0,1},{1,0},{2,3},{3,2},{4,5},{5,4},{6,7},{7,6},{8,9},{9,8},{10,11... | collective-permute-start | bytes 3538952 | tf_op jit(solution)/shard_map/ppermute | solution.py:39
  476.7 17.3 %collective-permute-start.103 = (f32[8,834]{1,0:T(8,128)}, f32[8,834]{1,0:T(8,128)S(1)}, u32[]{:S(2)}, u32[]{:S(2)}) collective-permute-start(f32[8,834]{1,0:T(8,128)} %get-tuple-element.395), channel_id=1, source_target_pairs={{0,8},{1,9},{2,10},{3,11},{4,12},{5,13},{6,14},{7,15},{8,0},{9,1},... | collective-permute-start | bytes 80072 | tf_op jit(solution)/shard_map/ppermute | solution.py:39
  476.8 18.7 %collective-permute-start.104 = (f32[8,834]{1,0:T(8,128)S(1)}, f32[8,834]{1,0:T(8,128)S(1)}, u32[]{:S(2)}, u32[]{:S(2)}) collective-permute-start(f32[8,834]{1,0:T(8,128)S(1)} %get-tuple-element.397), channel_id=1, source_target_pairs={{0,16},{1,17},{2,18},{3,19},{4,20},{5,21},{6,22},{7,23},{8,24},{9,... | collective-permute-start | bytes 80072 | tf_op jit(solution)/shard_map/ppermute | solution.py:39
  495.5 16.2 %collective-permute-start.114 = (bf16[272,512]{1,0:T(8,128)(2,1)}, bf16[272,512]{1,0:T(8,128)(2,1)S(1)}, u32[]{:S(2)}, u32[]{:S(2)}) collective-permute-start(bf16[272,512]{1,0:T(8,128)(2,1)} %get-tuple-element.313), channel_id=1, source_target_pairs={{0,8},{1,9},{2,10},{3,11},{4,12},{5,13},{6,14},{7,15},{8,0},{9,1},... | collective-permute-start | bytes 835592 | tf_op jit(solution)/shard_map/ppermute | solution.py:39
  496.1 22.5 %collective-permute-start.115 = (bf16[272,512]{1,0:T(8,128)(2,1)}, bf16[272,512]{1,0:T(8,128)(2,1)S(1)}, u32[]{:S(2)}, u32[]{:S(2)}) collective-permute-start(bf16[272,512]{1,0:T(8,128)(2,1)} %get-tuple-element.314), channel_id=1, source_target_pairs={{0,16},{1,17},{2,18},{3,19},{4,20},{5,21},{6,22},{7,23},{8,24},{9,... | collective-permute-start | bytes 835592 | tf_op jit(solution)/shard_map/ppermute | solution.py:39
  501.9 16.8 %collective-permute-start.116 = (bf16[272,512]{1,0:T(8,128)(2,1)}, bf16[272,512]{1,0:T(8,128)(2,1)S(1)}, u32[]{:S(2)}, u32[]{:S(2)}) collective-permute-start(bf16[272,512]{1,0:T(8,128)(2,1)} %get-tuple-element.315), channel_id=1, source_target_pairs={{0,24},{1,25},{2,26},{3,27},{4,28},{5,29},{6,30},{7,31},{8,16},{9,... | collective-permute-start | bytes 835592 | tf_op jit(solution)/shard_map/ppermute | solution.py:39
  511.0 27.6 %collective-permute-start.126 = (bf16[32,1024]{1,0:T(8,128)(2,1)S(1)}, bf16[32,1024]{1,0:T(8,128)(2,1)S(1)}, u32[]{:S(2)}, u32[]{:S(2)}) collective-permute-start(bf16[32,1024]{1,0:T(8,128)(2,1)S(1)} %bitcast.258), channel_id=1, source_target_pairs={{0,0},{8,1},{16,2},{24,3},{1,4},{9,5},{17,6},{25,7},{2,8},{10,9},{... | collective-permute-start | bytes 196616 | tf_op jit(solution)/shard_map/ppermute | solution.py:1072
  533.1 14.8 %collective-permute-start.123 = (bf16[2,32,1920]{2,1,0:T(8,128)(2,1)S(1)}, bf16[2,32,1920]{2,1,0:T(8,128)(2,1)S(1)}, u32[]{:S(2)}, u32[]{:S(2)}) collective-permute-start(bf16[2,32,1920]{2,1,0:T(8,128)(2,1)S(1)} %pad_maximum_fusion.6), channel_id=1, source_target_pairs={{0,4},{1,5},{2,6},{3,7},{4,0},{5,1},{6,2},{7,3},{8,12},{9,13},{10,... | collective-permute-start | bytes 737288 | tf_op jit(solution)/shard_map/ppermute | solution.py:39
  (238 other events, 1598.0 us)
Sparse Core Ops, SparseCore 0:
  38.3 30.4 all-gather.8
  71.0 44.7 all-gather.10
  118.0 26.6 all-gather.12
  146.6 49.9 all-gather.14
  324.3 48.0 reduce-scatter.3
  383.1 30.8 reduce-scatter.5
  435.8 46.7 reduce-scatter.7

commit v7 on v6

--- a/solution.py
+++ b/solution.py
@@ -1108,6 +1108,7 @@
 
     got = [across(blocks[step], PLANE * step) for step in range(1, O)]
     entries = jnp.concatenate(vectors + [jnp.broadcast_to(loss_terms, (O, PLANE, 2))], axis=2)
+    entries, terms = tie(entries, terms)
     lines = pick(entries, far)
     for step in range(1, O):
         lines = lines + across(pick(entries, far ^ step), PLANE * step)

time: 565 us -> 578 us (1.023)
  waiting for transfers between devices: 209 us -> 221 us
    ppermute x119, waiting for transfers between devices: 209 us -> 221 us  [across(): return lax.ppermute(x, BOTH, [(d, d ^ mask) for d in range(size)])]
    unnamed x279 -> x275, local copies, waits for them, and re-layouts: 28.8 us -> 26.8 us
  transfers between devices with their start and end apart: 134 -> 134, of which waited for: 63 -> 65; matrix products, arithmetic and copies ran while one was open for 6% -> 5% of each run, Pallas kernels for 21% -> 21%
where the time goes in v7:
time: 578 us; the launch traced here: 572 us
  waiting for transfers between devices  221 us (38%)
  Pallas kernels  138 us (24%)
  starting transfers between devices  134 us (23%)
  local copies, waits for them, and re-layouts  45.2 us (8%)
  between operations  17.2 us (3%)
  other arithmetic  14.7 us (3%)
    ppermute x119, waiting for transfers between devices, across(): return lax.ppermute(x, BOTH, [(d, d ^ mask) for d in range(size)])  221 us
    pallas_call x33, Pallas kernels, call(): pl.pallas_call(wrapped, in_specs=[IN_VMEM if kind == 'near' else IN_HBM f...  138 us
    ppermute x119, starting transfers between devices, across(): return lax.ppermute(x, BOTH, [(d, d ^ mask) for d in range(size)])  124 us
    unnamed x275, local copies, waits for them, and re-layouts  26.8 us
  transfers between devices with their start and end apart: 134, of which 65 were waited for; matrix products, arithmetic and copies ran while one was open for 5% of the time, Pallas kernels for 21%

profile of v7, /device:TPU:0, one launch (start us, length us, event | category | flops | bytes accessed | tf_op | source)
XLA Modules:
  0.0 571.7 jit_solution(15713391732311382133)
XLA Ops:
  23.7 7.7 %collective-permute-start.11 = (bf16[2,48,384]{2,1,0:T(8,128)(2,1)S(1)}, bf16[2,48,384]{2,1,0:T(8,128)(2,1)S(1)}, u32[]{:S(2)}, u32[]{:S(2)}) collective-permute-start(bf16[2,48,384]{2,1,0:T(8,128)(2,1)S(1)} %pad_maximum_fusion.13), channel_id=1, source_target_pairs={{0,6},{1,7},{2,4},{3,5},{4,2},{5,3},{6,0},{7,1},{8,14},{9,15},{10,... | collective-permute-start | bytes 221192 | tf_op jit(solution)/shard_map/ppermute | solution.py:39
  77.2 10.4 %shard_map.214 = (bf16[1152,384]{1,0:T(8,128)(2,1)}, bf16[1152,128]{1,0:T(8,128)(2,1)}, f32[2,1152]{1,0:T(2,128)}, bf16[4,144,1024]{2,1,0:T(8,128)(2,1)}, bf16[4,144,1024]{2,1,0:T(8,128)(2,1)}) custom-call(bf16[144,1024]{1,0:T(8,128)(2,1)} %copy-done, bf16[144,1024]{1,0:T(8,128)(2,1)} %copy-done.45, bf16[144,1024]{1,0:T(8,128)(2,1)} %copy-done.42, ...), custom_call_target="tpu_custom_call" | custom-call | flops 1 | bytes 1 | tf_op jit(solution)/shard_map/pallas_call | solution.py:213
  111.6 6.5 %collective-permute-done.21.refs_2_ = bf16[144,1024]{1,0:T(8,128)(2,1)S(1)} collective-permute-done((bf16[144,1024]{1,0:T(8,128)(2,1)S(1)}, bf16[144,1024]{1,0:T(8,128)(2,1)S(1)}, u32[]{:S(2)}, u32[]{:S(2)}) %collective-permute-start.21) | collective-permute-done | bytes 294944 | tf_op jit(solution)/shard_map/ppermute | solution.py:39
  126.4 8.0 %shard_map.217 = (bf16[1152,512]{1,0:T(8,128)(2,1)}, bf16[1152,512]{1,0:T(8,128)(2,1)}, bf16[4,144,1024]{2,1,0:T(8,128)(2,1)}, bf16[4,144,1024]{2,1,0:T(8,128)(2,1)}) custom-call(bf16[144,1024]{1,0:T(8,128)(2,1)} %copy-done.3, bf16[144,1024]{1,0:T(8,128)(2,1)} %copy-done.51, bf16[144,1024]{1,0:T(8,128)(2,1)} %copy-done.48, bf16[144,1024]{1,0:T(8,128)(2,1)} %copy-done.52, ...), custom_call_target="tpu_custom_call" | custom-call | flops 1 | bytes 1 | tf_op jit(solution)/shard_map/pallas_call | solution.py:213
  159.1 6.5 %collective-permute-done.36.refs_2_ = bf16[144,1024]{1,0:T(8,128)(2,1)S(1)} collective-permute-done((bf16[144,1024]{1,0:T(8,128)(2,1)S(1)}, bf16[144,1024]{1,0:T(8,128)(2,1)S(1)}, u32[]{:S(2)}, u32[]{:S(2)}) %collective-permute-start.36) | collective-permute-done | bytes 294944 | tf_op jit(solution)/shard_map/ppermute | solution.py:39
  174.1 10.5 %shard_map.220 = (bf16[1152,384]{1,0:T(8,128)(2,1)}, bf16[1152,128]{1,0:T(8,128)(2,1)}, f32[2,1152]{1,0:T(2,128)}, bf16[4,144,1024]{2,1,0:T(8,128)(2,1)}, bf16[4,144,1024]{2,1,0:T(8,128)(2,1)}) custom-call(bf16[144,1024]{1,0:T(8,128)(2,1)} %copy-done.4, bf16[144,1024]{1,0:T(8,128)(2,1)} %copy-done.58, bf16[144,1024]{1,0:T(8,128)(2,1)} %copy-done.55, ...), custom_call_target="tpu_custom_call" | custom-call | flops 1 | bytes 1 | tf_op jit(solution)/shard_map/pallas_call | solution.py:213
  192.8 6.4 %collective-permute-done.43.refs_2_ = bf16[144,1024]{1,0:T(8,128)(2,1)S(1)} collective-permute-done((bf16[144,1024]{1,0:T(8,128)(2,1)S(1)}, bf16[144,1024]{1,0:T(8,128)(2,1)S(1)}, u32[]{:S(2)}, u32[]{:S(2)}) %collective-permute-start.43) | collective-permute-done | bytes 294944 | tf_op jit(solution)/shard_map/ppermute | solution.py:39
  210.2 6.5 %collective-permute-done.47.refs_2_ = bf16[144,1024]{1,0:T(8,128)(2,1)S(1)} collective-permute-done((bf16[144,1024]{1,0:T(8,128)(2,1)S(1)}, bf16[144,1024]{1,0:T(8,128)(2,1)S(1)}, u32[]{:S(2)}, u32[]{:S(2)}) %collective-permute-start.47) | collective-permute-done | bytes 294944 | tf_op jit(solution)/shard_map/ppermute | solution.py:39
  224.3 8.0 %shard_map.223 = (bf16[1152,512]{1,0:T(8,128)(2,1)}, bf16[1152,512]{1,0:T(8,128)(2,1)}, bf16[4,144,1024]{2,1,0:T(8,128)(2,1)}, bf16[4,144,1024]{2,1,0:T(8,128)(2,1)}) custom-call(bf16[144,1024]{1,0:T(8,128)(2,1)} %copy-done.18, bf16[144,1024]{1,0:T(8,128)(2,1)} %copy-done.93, bf16[144,1024]{1,0:T(8,128)(2,1)} %copy-done.90, bf16[144,1024]{1,0:T(8,128)(2,1)} %copy-done.94, ...), custom_call_target="tpu_custom_call" | custom-call | flops 1 | bytes 1 | tf_op jit(solution)/shard_map/pallas_call | solution.py:213
  247.6 6.9 %collective-permute-done.55.refs_3_ = bf16[144,1024]{1,0:T(8,128)(2,1)S(1)} collective-permute-done((bf16[144,1024]{1,0:T(8,128)(2,1)S(1)}, bf16[144,1024]{1,0:T(8,128)(2,1)S(1)}, u32[]{:S(2)}, u32[]{:S(2)}) %collective-permute-start.55) | collective-permute-done | bytes 294944 | tf_op jit(solution)/shard_map/ppermute | solution.py:39
  293.4 7.2 %shard_map.228 = (bf16[1152,512]{1,0:T(8,128)(2,1)}, f32[1,512]{1,0:T(1,128)}, bf16[4,144,1024]{2,1,0:T(8,128)(2,1)}, bf16[4,144,1024]{2,1,0:T(8,128)(2,1)}) custom-call(bf16[144,1024]{1,0:T(8,128)(2,1)} %copy-done.5, bf16[144,1024]{1,0:T(8,128)(2,1)} %copy-done.65, bf16[144,1024]{1,0:T(8,128)(2,1)} %copy-done.62, bf16[144,1024]{1,0:T(8,128)(2,1)} %copy-done.66, ...), custom_call_target="tpu_custom_call" | custom-call | flops 1 | bytes 1 | tf_op jit(solution)/shard_map/pallas_call | solution.py:213
  312.7 8.5 %shard_map.230 = bf16[4,272,1024]{2,1,0:T(8,128)(2,1)} custom-call(bf16[144,1024]{1,0:T(8,128)(2,1)} %copy-done.18, bf16[144,1024]{1,0:T(8,128)(2,1)} %copy-done.93, bf16[144,1024]{1,0:T(8,128)(2,1)} %copy-done.90, bf16[144,1024]{1,0:T(8,128)(2,1)} %copy-done.94, bf16[144,1024]{1,0:T(8,128)(2,1)} %copy-done.91, bf16[144,1024]{1,0:T(8,128)(2,1)} %copy-done.95, ...), custom_call_target="tpu_custom_call" | custom-call | flops 2415919104 | bytes 9437184 | tf_op jit(solution)/shard_map/pallas_call | solution.py:213
  329.6 6.5 %collective-permute-done.82.refs_2_.refs_10_ = bf16[144,1024]{1,0:T(8,128)(2,1)S(1)} collective-permute-done((bf16[144,1024]{1,0:T(8,128)(2,1)S(1)}, bf16[144,1024]{1,0:T(8,128)(2,1)S(1)}, u32[]{:S(2)}, u32[]{:S(2)}) %collective-permute-start.82) | collective-permute-done | bytes 294944 | tf_op jit(solution)/shard_map/ppermute | solution.py:39
  343.3 17.2 %shard_map.232 = (bf16[1152,384]{1,0:T(8,128)(2,1)}, f32[1,384]{1,0:T(1,128)}, bf16[4,144,1024]{2,1,0:T(8,128)(2,1)}, bf16[4,144,1024]{2,1,0:T(8,128)(2,1)}) custom-call(bf16[144,1024]{1,0:T(8,128)(2,1)} %copy-done.7, bf16[144,1024]{1,0:T(8,128)(2,1)} %copy-done.82, bf16[144,1024]{1,0:T(8,128)(2,1)} %copy-done.76, bf16[144,1024]{1,0:T(8,128)(2,1)} %copy-done.84, ...), custom_call_target="tpu_custom_call" | custom-call | flops 1 | bytes 1 | tf_op jit(solution)/shard_map/pallas_call | solution.py:213
  370.0 6.8 %shard_map.234 = bf16[4,272,512]{2,1,0:T(8,128)(2,1)} custom-call(bf16[144,1024]{1,0:T(8,128)(2,1)} %copy-done.4, bf16[144,1024]{1,0:T(8,128)(2,1)} %copy-done.58, bf16[144,1024]{1,0:T(8,128)(2,1)} %copy-done.55, bf16[144,1024]{1,0:T(8,128)(2,1)} %copy-done.59, bf16[144,1024]{1,0:T(8,128)(2,1)} %copy-done.56, bf16[144,1024]{1,0:T(8,128)(2,1)} %copy-done.60, ...), custom_call_target="tpu_custom_call" | custom-call | flops 1207959552 | bytes 7013888 | tf_op jit(solution)/shard_map/pallas_call | solution.py:213
  390.9 6.5 %collective-permute-done.93.refs_2_.refs_10_ = bf16[144,1024]{1,0:T(8,128)(2,1)S(1)} collective-permute-done((bf16[144,1024]{1,0:T(8,128)(2,1)S(1)}, bf16[144,1024]{1,0:T(8,128)(2,1)S(1)}, u32[]{:S(2)}, u32[]{:S(2)}) %collective-permute-start.93) | collective-permute-done | bytes 294944 | tf_op jit(solution)/shard_map/ppermute | solution.py:39
  405.7 7.2 %shard_map.236 = (bf16[1152,512]{1,0:T(8,128)(2,1)}, f32[1,512]{1,0:T(1,128)}, bf16[4,144,1024]{2,1,0:T(8,128)(2,1)}, bf16[4,144,1024]{2,1,0:T(8,128)(2,1)}) custom-call(bf16[144,1024]{1,0:T(8,128)(2,1)} %copy-done.8, bf16[144,1024]{1,0:T(8,128)(2,1)} %copy-done.83, bf16[144,1024]{1,0:T(8,128)(2,1)} %copy-done.77, bf16[144,1024]{1,0:T(8,128)(2,1)} %copy-done.85, ...), custom_call_target="tpu_custom_call" | custom-call | flops 1 | bytes 1 | tf_op jit(solution)/shard_map/pallas_call | solution.py:213
  421.9 8.5 %shard_map.238 = bf16[4,256,1024]{2,1,0:T(8,128)(2,1)} custom-call(bf16[144,1024]{1,0:T(8,128)(2,1)} %copy-done.3, bf16[144,1024]{1,0:T(8,128)(2,1)} %copy-done.51, bf16[144,1024]{1,0:T(8,128)(2,1)} %copy-done.48, bf16[144,1024]{1,0:T(8,128)(2,1)} %copy-done.52, bf16[144,1024]{1,0:T(8,128)(2,1)} %copy-done.49, bf16[144,1024]{1,0:T(8,128)(2,1)} %copy-done.53, ...), custom_call_target="tpu_custom_call" | custom-call | flops 2415919104 | bytes 9175040 | tf_op jit(solution)/shard_map/pallas_call | solution.py:213
  455.6 17.3 %shard_map.240 = (bf16[1152,384]{1,0:T(8,128)(2,1)}, f32[1,384]{1,0:T(1,128)}, bf16[4,144,1024]{2,1,0:T(8,128)(2,1)}, bf16[4,144,1024]{2,1,0:T(8,128)(2,1)}) custom-call(bf16[144,1024]{1,0:T(8,128)(2,1)} %copy-done.6, bf16[144,1024]{1,0:T(8,128)(2,1)} %copy-done.72, bf16[144,1024]{1,0:T(8,128)(2,1)} %copy-done.67, bf16[144,1024]{1,0:T(8,128)(2,1)} %copy-done.73, ...), custom_call_target="tpu_custom_call" | custom-call | flops 1 | bytes 1 | tf_op jit(solution)/shard_map/pallas_call | solution.py:213
  474.1 6.9 %shard_map.241 = (bf16[272,512]{1,0:T(8,128)(2,1)}, bf16[272,512]{1,0:T(8,128)(2,1)}, bf16[272,512]{1,0:T(8,128)(2,1)}, bf16[272,512]{1,0:T(8,128)(2,1)}) custom-call(bf16[144,1024]{1,0:T(8,128)(2,1)} %copy-done, bf16[144,1024]{1,0:T(8,128)(2,1)} %copy-done.45, bf16[144,1024]{1,0:T(8,128)(2,1)} %copy-done.42, bf16[144,1024]{1,0:T(8,128)(2,1)} %copy-done.46, ...), custom_call_target="tpu_custom_call" | custom-call | flops 1207959552 | bytes 7013888 | tf_op jit(solution)/shard_map/pallas_call | solution.py:213
  493.3 6.6 %collective-permute-done.112 = bf16[144,1024]{1,0:T(8,128)(2,1)S(1)} collective-permute-done((bf16[144,1024]{1,0:T(8,128)(2,1)}, bf16[144,1024]{1,0:T(8,128)(2,1)S(1)}, u32[]{:S(2)}, u32[]{:S(2)}) %collective-permute-start.112) | collective-permute-done | bytes 294944 | tf_op jit(solution)/shard_map/ppermute | solution.py:39
  500.7 7.1 %collective-permute-start.115 = (f32[8,834]{1,0:T(8,128)S(1)}, f32[8,834]{1,0:T(8,128)S(1)}, u32[]{:S(2)}, u32[]{:S(2)}) collective-permute-start(f32[8,834]{1,0:T(8,128)S(1)} %get-tuple-element.407), channel_id=1, source_target_pairs={{0,16},{1,17},{2,18},{3,19},{4,20},{5,21},{6,22},{7,23},{8,24},{9,... | collective-permute-start | bytes 80072 | tf_op jit(solution)/shard_map/ppermute | solution.py:39
  515.8 16.5 %collective-permute-done.118.refs_2_ = bf16[272,512]{1,0:T(8,128)(2,1)S(1)} collective-permute-done((bf16[272,512]{1,0:T(8,128)(2,1)S(1)}, bf16[272,512]{1,0:T(8,128)(2,1)S(1)}, u32[]{:S(2)}, u32[]{:S(2)}) %collective-permute-start.118) | collective-permute-done | bytes 278560 | tf_op jit(solution)/shard_map/ppermute | solution.py:39
  532.7 12.1 %collective-permute-start.121 = (bf16[4,32,1920]{2,1,0:T(8,128)(2,1)S(1)}, bf16[4,32,1920]{2,1,0:T(8,128)(2,1)S(1)}, u32[]{:S(2)}, u32[]{:S(2)}) collective-permute-start(bf16[4,32,1920]{2,1,0:T(8,128)(2,1)S(1)} %get-tuple-element.348), channel_id=1, source_target_pairs={{0,1},{1,0},{2,3},{3,2},{4,5},{5,4},{6,7},{7,6},{8,9},{9,8},{10,11... | collective-permute-start | bytes 1474568 | tf_op jit(solution)/shard_map/ppermute | solution.py:39
  (712 shorter events, 342.6 us)
Async XLA Ops:
  7.2 70.0 %all-gather.9.cloned.1.call-start = ((), (), s32[]{:S(2)}) async-start(), calls=%async_computation.6 | async-start | bytes 1310720 | tf_op jit(solution)/shard_map/all_gather | solution.py:969
  11.7 26.5 %collective-permute-start.27 = (bf16[4,32,1408]{2,1,0:T(8,128)(2,1)}, bf16[4,32,1408]{2,1,0:T(8,128)(2,1)S(1)}, u32[]{:S(2)}, u32[]{:S(2)}) collective-permute-start(bf16[4,32,1408]{2,1,0:T(8,128)(2,1)} %slice.296), channel_id=1, source_target_pairs={{0,1},{1,0},{2,3},{3,2},{4,5},{5,4},{6,7},{7,6},{8,9},{9,8},{10,11... | collective-permute-start | bytes 1081352 | tf_op jit(solution)/shard_map/ppermute | solution.py:39
  12.7 18.7 %collective-permute-start.12 = (bf16[2,32,1024]{2,1,0:T(8,128)(2,1)}, bf16[2,32,1024]{2,1,0:T(8,128)(2,1)}, u32[]{:S(2)}, u32[]{:S(2)}) collective-permute-start(bf16[2,32,1024]{2,1,0:T(8,128)(2,1)} %param.15), channel_id=1, source_target_pairs={{0,0},{1,8},{2,16},{3,24},{4,1},{5,9},{6,17},{7,25},{8,2},{9,10},{... | collective-permute-start | bytes 393224 | tf_op jit(solution)/shard_map/ppermute | solution.py:957
  15.6 44.5 %collective-permute-start = (bf16[144,1024]{1,0:T(8,128)(2,1)}, bf16[144,1024]{1,0:T(8,128)(2,1)S(1)}, u32[]{:S(2)}, u32[]{:S(2)}) collective-permute-start(bf16[144,1024]{1,0:T(8,128)(2,1)} %bitcast), channel_id=1, source_target_pairs={{0,0},{1,16},{2,10},{3,26},{4,4},{5,20},{6,14},{7,30},{8,1},{9,17}... | collective-permute-start | bytes 884744 | tf_op jit(solution)/shard_map/ppermute | solution.py:49
  38.2 86.7 %all-gather.11.cloned.1.call-start = ((), (), s32[]{:S(2)}) async-start(), calls=%async_computation.7 | async-start | bytes 2621440 | tf_op jit(solution)/shard_map/all_gather | solution.py:969
  53.4 118.3 %all-gather.13.cloned.1.call-start = ((), (), s32[]{:S(2)}) async-start(), calls=%async_computation.8 | async-start | bytes 1310720 | tf_op jit(solution)/shard_map/all_gather | solution.py:969
  89.8 132.1 %all-gather.15.cloned.1.call-start = ((), (), s32[]{:S(2)}) async-start(), calls=%async_computation.9 | async-start | bytes 2949120 | tf_op jit(solution)/shard_map/all_gather | solution.py:969
  137.7 245.4 %reduce-scatter.4.cloned.1.call-start = ((), (), s32[]{:S(2)}) async-start(), calls=%async_computation.3 | async-start | bytes 2785280 | tf_op jit(solution)/shard_map/reduce_scatter | solution.py:1066
  139.0 15.2 %collective-permute-start.33 = (bf16[144,1024]{1,0:T(8,128)(2,1)S(1)}, bf16[144,1024]{1,0:T(8,128)(2,1)S(1)}, u32[]{:S(2)}, u32[]{:S(2)}) collective-permute-start(bf16[144,1024]{1,0:T(8,128)(2,1)S(1)} %get-tuple-element.206), channel_id=1, source_target_pairs={{0,4},{1,5},{2,6},{3,7},{4,0},{5,1},{6,2},{7,3},{8,12},{9,13},{10,... | collective-permute-start | bytes 884744 | tf_op jit(solution)/shard_map/ppermute | solution.py:39
  189.8 15.1 %collective-permute-start.44 = (bf16[144,1024]{1,0:T(8,128)(2,1)S(1)}, bf16[144,1024]{1,0:T(8,128)(2,1)S(1)}, u32[]{:S(2)}, u32[]{:S(2)}) collective-permute-start(bf16[144,1024]{1,0:T(8,128)(2,1)S(1)} %get-tuple-element.214), channel_id=1, source_target_pairs={{0,4},{1,5},{2,6},{3,7},{4,0},{5,1},{6,2},{7,3},{8,12},{9,13},{10,... | collective-permute-start | bytes 884744 | tf_op jit(solution)/shard_map/ppermute | solution.py:39
  190.4 14.5 %collective-permute-start.45 = (bf16[144,1024]{1,0:T(8,128)(2,1)S(1)}, bf16[144,1024]{1,0:T(8,128)(2,1)S(1)}, u32[]{:S(2)}, u32[]{:S(2)}) collective-permute-start(bf16[144,1024]{1,0:T(8,128)(2,1)S(1)} %get-tuple-element.215), channel_id=1, source_target_pairs={{0,6},{1,7},{2,4},{3,5},{4,2},{5,3},{6,0},{7,1},{8,14},{9,15},{10,... | collective-permute-start | bytes 884744 | tf_op jit(solution)/shard_map/ppermute | solution.py:39
  239.5 15.1 %collective-permute-start.55 = (bf16[144,1024]{1,0:T(8,128)(2,1)S(1)}, bf16[144,1024]{1,0:T(8,128)(2,1)S(1)}, u32[]{:S(2)}, u32[]{:S(2)}) collective-permute-start(bf16[144,1024]{1,0:T(8,128)(2,1)S(1)} %get-tuple-element.222), channel_id=1, source_target_pairs={{0,4},{1,5},{2,6},{3,7},{4,0},{5,1},{6,2},{7,3},{8,12},{9,13},{10,... | collective-permute-start | bytes 884744 | tf_op jit(solution)/shard_map/ppermute | solution.py:39
  275.6 14.8 %collective-permute-start.68 = (bf16[144,1024]{1,0:T(8,128)(2,1)S(1)}, bf16[144,1024]{1,0:T(8,128)(2,1)S(1)}, u32[]{:S(2)}, u32[]{:S(2)}) collective-permute-start(bf16[144,1024]{1,0:T(8,128)(2,1)S(1)} %get-tuple-element.232.refs_0_.refs_8_), channel_id=1, source_target_pairs={{0,4},{1,5},{2,6},{3,7},{4,0},{5,1},{6,2},{7,3},{8,12},{9,13},{10,... | collective-permute-start | bytes 884744 | tf_op jit(solution)/shard_map/ppermute | solution.py:39
  324.1 130.0 %reduce-scatter.6.cloned.1.call-start = ((), (), s32[]{:S(2)}) async-start(), calls=%async_computation.4 | async-start | bytes 1392640 | tf_op jit(solution)/shard_map/reduce_scatter | solution.py:1066
  382.7 117.9 %reduce-scatter.8.cloned.1.call-start = ((), (), s32[]{:S(2)}) async-start(), calls=%async_computation.5 | async-start | bytes 2621440 | tf_op jit(solution)/shard_map/reduce_scatter | solution.py:1066
  419.5 15.4 %collective-permute-start.101 = (bf16[144,1024]{1,0:T(8,128)(2,1)}, bf16[144,1024]{1,0:T(8,128)(2,1)}, u32[]{:S(2)}, u32[]{:S(2)}) collective-permute-start(bf16[144,1024]{1,0:T(8,128)(2,1)} %get-tuple-element.283), channel_id=1, source_target_pairs={{0,4},{1,5},{2,6},{3,7},{4,0},{5,1},{6,2},{7,3},{8,12},{9,13},{10,... | collective-permute-start | bytes 884744 | tf_op jit(solution)/shard_map/ppermute | solution.py:39
  484.3 15.6 %collective-permute-start.112 = (bf16[144,1024]{1,0:T(8,128)(2,1)}, bf16[144,1024]{1,0:T(8,128)(2,1)S(1)}, u32[]{:S(2)}, u32[]{:S(2)}) collective-permute-start(bf16[144,1024]{1,0:T(8,128)(2,1)} %get-tuple-element.322), channel_id=1, source_target_pairs={{0,4},{1,5},{2,6},{3,7},{4,0},{5,1},{6,2},{7,3},{8,12},{9,13},{10,... | collective-permute-start | bytes 884744 | tf_op jit(solution)/shard_map/ppermute | solution.py:39
  485.3 15.3 %collective-permute-start.113 = (bf16[144,1024]{1,0:T(8,128)(2,1)}, bf16[144,1024]{1,0:T(8,128)(2,1)S(1)}, u32[]{:S(2)}, u32[]{:S(2)}) collective-permute-start(bf16[144,1024]{1,0:T(8,128)(2,1)} %get-tuple-element.323), channel_id=1, source_target_pairs={{0,6},{1,7},{2,4},{3,5},{4,2},{5,3},{6,0},{7,1},{8,14},{9,15},{10,... | collective-permute-start | bytes 884744 | tf_op jit(solution)/shard_map/ppermute | solution.py:39
  487.1 64.9 %collective-permute-start.126 = (bf16[32,1024]{1,0:T(8,128)(2,1)S(1)}, bf16[32,1024]{1,0:T(8,128)(2,1)S(1)}, u32[]{:S(2)}, u32[]{:S(2)}) collective-permute-start(bf16[32,1024]{1,0:T(8,128)(2,1)S(1)} %bitcast.258), channel_id=1, source_target_pairs={{0,0},{8,1},{16,2},{24,3},{1,4},{9,5},{17,6},{25,7},{2,8},{10,9},{... | collective-permute-start | bytes 196616 | tf_op jit(solution)/shard_map/ppermute | solution.py:1072
  487.8 28.1 %collective-permute-start.117 = (bf16[272,512]{1,0:T(8,128)(2,1)}, bf16[272,512]{1,0:T(8,128)(2,1)S(1)}, u32[]{:S(2)}, u32[]{:S(2)}) collective-permute-start(bf16[272,512]{1,0:T(8,128)(2,1)} %get-tuple-element.330), channel_id=1, source_target_pairs={{0,8},{1,9},{2,10},{3,11},{4,12},{5,13},{6,14},{7,15},{8,0},{9,1},... | collective-permute-start | bytes 835592 | tf_op jit(solution)/shard_map/ppermute | solution.py:39
  512.1 20.2 %collective-permute-start.118 = (bf16[272,512]{1,0:T(8,128)(2,1)S(1)}, bf16[272,512]{1,0:T(8,128)(2,1)S(1)}, u32[]{:S(2)}, u32[]{:S(2)}) collective-permute-start(bf16[272,512]{1,0:T(8,128)(2,1)S(1)} %copy-done.122), channel_id=1, source_target_pairs={{0,16},{1,17},{2,18},{3,19},{4,20},{5,21},{6,22},{7,23},{8,24},{9,... | collective-permute-start | bytes 835592 | tf_op jit(solution)/shard_map/ppermute | solution.py:39
  514.2 18.2 %collective-permute-start.119 = (bf16[272,512]{1,0:T(8,128)(2,1)S(1)}, bf16[272,512]{1,0:T(8,128)(2,1)S(1)}, u32[]{:S(2)}, u32[]{:S(2)}) collective-permute-start(bf16[272,512]{1,0:T(8,128)(2,1)S(1)} %copy-done.121), channel_id=1, source_target_pairs={{0,24},{1,25},{2,26},{3,27},{4,28},{5,29},{6,30},{7,31},{8,16},{9,... | collective-permute-start | bytes 835592 | tf_op jit(solution)/shard_map/ppermute | solution.py:39
  515.1 17.2 %collective-permute-start.120 = (bf16[144,1024]{1,0:T(8,128)(2,1)S(1)}, bf16[144,1024]{1,0:T(8,128)(2,1)S(1)}, u32[]{:S(2)}, u32[]{:S(2)}) collective-permute-start(bf16[144,1024]{1,0:T(8,128)(2,1)S(1)} %add_convert_fusion), channel_id=1, source_target_pairs={{0,0},{16,1},{10,2},{26,3},{4,4},{20,5},{14,6},{30,7},{1,8},{17,9}... | collective-permute-start | bytes 884744 | tf_op jit(solution)/shard_map/ppermute | solution.py:49
  546.4 14.5 %collective-permute-start.123 = (bf16[2,32,1920]{2,1,0:T(8,128)(2,1)S(1)}, bf16[2,32,1920]{2,1,0:T(8,128)(2,1)S(1)}, u32[]{:S(2)}, u32[]{:S(2)}) collective-permute-start(bf16[2,32,1920]{2,1,0:T(8,128)(2,1)S(1)} %pad_maximum_fusion.6), channel_id=1, source_target_pairs={{0,4},{1,5},{2,6},{3,7},{4,0},{5,1},{6,2},{7,3},{8,12},{9,13},{10,... | collective-permute-start | bytes 737288 | tf_op jit(solution)/shard_map/ppermute | solution.py:39
  (236 other events, 1636.6 us)
Sparse Core Ops, SparseCore 0:
  38.3 30.4 all-gather.8
  71.0 44.7 all-gather.10
  117.9 26.6 all-gather.12
  146.6 49.9 all-gather.14
  324.2 48.2 reduce-scatter.3
  382.8 31.1 reduce-scatter.5
  435.0 46.8 reduce-scatter.7
